TPU v7x, 128 devices: a whole 4x4x4 slice. The times are simulated.
128 devices in a mesh: grp: 2 (over core), row: 16 (over y, x), col: 4 (over z).
Axes of the slice: x: 4, y: 4, z: 4, core: 2. Of those that a mesh axis runs over, the one named last changes fastest.
Arguments:
- channels: bfloat16 [6, 4096, 8192], P('grp', 'row', 'col'), may hold values from -0.06629126 to 0.06629126, as said below
- inverse: float32 [6, 4096, 4096], P('grp', 'row', 'col'), may hold values from -1 to 1, as said below
- arrivals: bfloat16 [6, 3, 192, 8192], P(None, None, ('grp', 'row'), 'col'), may hold values from -0.06629126 to 0.06629126
- arrival_cell: int32 [6, 3, 128, 1], replicated, may hold values from 0 to 31; in each aligned block of 128 rows (0 to 127, 128 to 255, ..., all dimensions but the last counted through in order) at most 6 rows name the same one
- cell_owner: int32 [32], replicated, may hold values from 0 to 31, each once
- slots: int32 [6, 3, 128], replicated, may hold values from 0 to 4095, as said below
- symbols: bfloat16 [6, 4096, 256], P('grp', 'col'), may hold values from -45 to 45
Outputs:
- updated_inverse: float32 [6, 4096, 4096], P('grp', 'row', 'col')
- transmit: float32 [256, 6, 8192], P('row', 'grp', 'col')
Inputs may be any that keep to these rules, and one draw needn't show every extreme that they name: In each group the 3 x 128 slots are distinct. `inverse`: Symmetric; in each group the rows and columns at that group's slots are those of the identity. `channels`: rows at a group's slots are zero. `arrival_cell`: in each group and epoch at most 6 arriving users share a cell.
All inputs are finite; a program needn't handle non-finite values.
Results may differ from a plain program's by a relative error of at most 0.0031.
Values may be sent and summed in bfloat16 or wider, within the bound.
No kernel may reach another device: no remote copies, remote signals or barrier semaphores. Data moves between devices by JAX's collectives and lax.ppermute only.
A program may use at most 128 MiB of HBM per device.

v0:
```python
import jax
import jax.numpy as jnp
from jax import lax
from jax.experimental import pallas as pl
from jax.experimental.pallas import tpu as pltpu
from jax.sharding import PartitionSpec as P

ANTENNAS = 8192
ARRIVE = 128
EPOCHS = 3
STREAMS = 256
TOTAL = ARRIVE * EPOCHS
BLOCK = 128
PANEL = 8
WINDOW = 48
SHARE = TOTAL // 16

loading = 1.0
epsilon = 1e-06
highest = lax.Precision.HIGHEST
f32 = jnp.float32
bf16 = jnp.bfloat16
VMEM = pl.BlockSpec(memory_space=pltpu.VMEM)
SMEM = pl.BlockSpec(memory_space=pltpu.SMEM)
HBM = pl.BlockSpec(memory_space=pltpu.HBM)


def params(mib=40):
    return pltpu.CompilerParams(vmem_limit_bytes=mib * 1024 * 1024)


def cost(flops, nbytes):
    return pl.CostEstimate(flops=flops, bytes_accessed=nbytes, transcendentals=0)


def dot(a, b):
    return jnp.dot(a, b, preferred_element_type=f32)


def dot_t(a, b):
    return lax.dot_general(a, b, (((1,), (1,)), ((), ())), preferred_element_type=f32)


def t_dot(a, b):
    return lax.dot_general(a, b, (((0,), (0,)), ((), ())), preferred_element_type=f32)


def halves(a):
    high = a.astype(bf16)
    return high, (a - high.astype(f32)).astype(bf16)


def split(product, a, b):
    a_high, a_low = halves(a)
    b_high, b_low = halves(b)
    return product(a_high, b_low) + product(a_low, b_high) + product(a_high, b_high)


def placing(slots_ref, first, rows):
    ids = first + lax.broadcasted_iota(jnp.int32, (rows, TOTAL), 0)
    return (ids == slots_ref[...].reshape(1, TOTAL)).astype(f32)


def choosing(place_ref, g):
    ids = lax.broadcasted_iota(jnp.int32, (16 * WINDOW, TOTAL), 0)
    return (ids == place_ref[g]).astype(f32).astype(bf16)


def start_inputs(gathered_ref, channel_ref, window_ref, held_ref, sems, row=None):
    groups, user_rows = channel_ref.shape[:2]
    copies = []
    for g in range(groups):
        start = g * 2 * EPOCHS * 6 // 16 * 16
        source = gathered_ref.at[:, pl.ds(start, WINDOW), :]
        parts = [
            pltpu.make_async_copy(channel_ref.at[g], held_ref.at[g, :user_rows], sems.at[0, g]),
            pltpu.make_async_copy(source, window_ref.at[g], sems.at[1, g]),
        ]
        if row is not None:
            source = gathered_ref.at[row, pl.ds(start, WINDOW), :]
            parts.append(
                pltpu.make_async_copy(source, held_ref.at[g, user_rows:], sems.at[2, g])
            )
        for part in parts:
            part.start()
        copies.append(parts)
    return copies


def input_scratch(groups, rows, antennas):
    return [
        pltpu.VMEM((groups, 16, WINDOW, antennas), bf16),
        pltpu.VMEM((groups, rows, antennas), bf16),
        pltpu.SemaphoreType.DMA((3, groups)),
    ]


def columns_kernel(
    row_ref, gathered_ref, channel_ref, place_ref, out_ref, window_ref, held_ref, sems
):
    groups, _, antennas = channel_ref.shape
    copies = start_inputs(gathered_ref, channel_ref, window_ref, held_ref, sems, row_ref[0])
    out_ref[groups] = jnp.zeros(out_ref.shape[1:], bf16)
    for g in range(groups):
        choose = choosing(place_ref, g)
        for copy in copies[g]:
            copy.wait()
        window = window_ref[g].reshape(16 * WINDOW, antennas)
        wide = dot_t(held_ref[g], window).astype(bf16)
        out_ref[g] = dot(wide, choose).astype(bf16)


def make_columns(row, gathered, channels, place):
    groups, user_rows, antennas = channels.shape
    return pl.pallas_call(
        columns_kernel,
        out_shape=jax.ShapeDtypeStruct((groups + 1, user_rows + WINDOW, TOTAL), bf16),
        in_specs=[SMEM, HBM, HBM, VMEM],
        out_specs=VMEM,
        scratch_shapes=input_scratch(groups, user_rows + WINDOW, antennas),
        compiler_params=params(60),
        cost_estimate=cost(4_000_000_000, 12_000_000),
        name="columns",
    )(row, gathered, channels, place)


def channel_kernel(
    first_ref, gathered_ref, channel_ref, place_ref, slots_ref, out_ref, window_ref, held_ref, sems
):
    groups, user_rows, antennas = channel_ref.shape
    copies = start_inputs(gathered_ref, channel_ref, window_ref, held_ref, sems)
    for g in range(groups):
        here = placing(slots_ref.at[g], first_ref[0], user_rows).astype(bf16)
        route = dot_t(here, choosing(place_ref, g)).astype(bf16)
        for copy in copies[g]:
            copy.wait()
        window = window_ref[g].reshape(16 * WINDOW, antennas)
        out_ref[g] = held_ref[g] + dot(route, window).astype(bf16)


def make_channel(first, gathered, channels, place, slots_mine):
    groups, user_rows, antennas = channels.shape
    return pl.pallas_call(
        channel_kernel,
        out_shape=jax.ShapeDtypeStruct(channels.shape, bf16),
        in_specs=[SMEM, HBM, HBM, VMEM, VMEM],
        out_specs=VMEM,
        scratch_shapes=input_scratch(groups, user_rows, antennas),
        compiler_params=params(60),
        cost_estimate=cost(4_000_000_000, 14_000_000),
        name="channel",
    )(first, gathered, channels, place, slots_mine)


def pieces_kernel(x_ref, inverse_ref, out0, out1, out2, out3):
    size = out0.shape[-1]
    for d, out in enumerate([out0, out1, out2, out3]):
        start = pl.multiple_of((x_ref[0] + d) % 4 * size, size)
        out[...] = inverse_ref[:, :, pl.ds(start, size)].astype(bf16)


def make_pieces(x, inverse):
    groups, user_rows = inverse.shape[:2]
    shape = jax.ShapeDtypeStruct((groups, user_rows, user_rows), bf16)
    return pl.pallas_call(
        pieces_kernel,
        out_shape=(shape,) * 4,
        in_specs=[SMEM, VMEM],
        out_specs=(VMEM,) * 4,
        compiler_params=params(16),
        cost_estimate=cost(100_000_000, 5_000_000),
        name="pieces",
    )(x, inverse)


def target_kernel(where_ref, summed_ref, precoded_ref, slots_ref, place_ref, base_out):
    row, first = where_ref[1], where_ref[2]
    user_rows = precoded_ref.shape[0]
    ids = row * WINDOW + lax.broadcasted_iota(jnp.int32, (WINDOW, TOTAL), 0)
    choose = (ids == place_ref[...]).astype(f32).astype(bf16)
    base_out[:, :TOTAL] = -t_dot(choose, summed_ref[user_rows:].astype(bf16))
    border = summed_ref[:user_rows] - placing(slots_ref, first, user_rows)
    base_out[:, TOTAL:] = split(t_dot, border, precoded_ref[...])


def make_target(where, summed, precoded, slot_plane, place_plane):
    return pl.pallas_call(
        target_kernel,
        out_shape=jax.ShapeDtypeStruct((TOTAL, TOTAL + STREAMS), f32),
        in_specs=[SMEM] + [VMEM] * 4,
        out_specs=VMEM,
        compiler_params=params(16),
        cost_estimate=cost(1_000_000_000, 2_000_000),
        name="target",
    )(where, summed, precoded, slot_plane, place_plane)


def middle_kernel(
    where_ref, square_ref, own_ref, row1_ref, row2_ref, row3_ref, col1_ref, col2_ref, col3_ref,
    base_ref, first_out, block1_out, block2_out, block3_out, packed_out,
):
    y = where_ref[0]
    by_row = [own_ref, row1_ref, row2_ref, row3_ref]
    by_col = [own_ref, col1_ref, col2_ref, col3_ref]
    outs = [first_out, block1_out, block2_out, block3_out]
    schur = base_ref[:, :TOTAL]
    for d in range(4):
        block = dot(square_ref[y, d], own_ref[...])
        for e in range(1, 4):
            block += dot(square_ref[(y + e) % 4, d], by_col[e][...])
        low = block.astype(bf16)
        outs[d][...] = block if d == 0 else low
        schur += t_dot(by_row[d][...], low)
    packed_out[:, :TOTAL] = schur.astype(bf16)
    packed_out[:, TOTAL:] = base_ref[:, TOTAL:].astype(bf16)


def make_middle(where, square, by_row, by_col, base):
    shape = by_row[0].shape
    return pl.pallas_call(
        middle_kernel,
        out_shape=(
            jax.ShapeDtypeStruct(shape, f32),
            jax.ShapeDtypeStruct(shape, bf16),
            jax.ShapeDtypeStruct(shape, bf16),
            jax.ShapeDtypeStruct(shape, bf16),
            jax.ShapeDtypeStruct((TOTAL, TOTAL + STREAMS), bf16),
        ),
        in_specs=[SMEM] + [VMEM] * 9,
        out_specs=(VMEM,) * 5,
        compiler_params=params(),
        cost_estimate=cost(2_000_000_000, 8_000_000),
        name="middle",
    )(where, square, *by_row, *by_col[1:], base)


def invert_block(a):
    lane = lax.broadcasted_iota(jnp.int32, (1, BLOCK), 1)
    sub = lax.broadcasted_iota(jnp.int32, (PANEL, 1), 0)
    for k in range(0, BLOCK, PANEL):
        inside = (lane >= k) & (lane < k + PANEL)
        rows = a[k:k + PANEL, :]
        cols = [
            jnp.broadcast_to(rows[:, k + j:k + j + 1], (PANEL, BLOCK)) for j in range(PANEL)
        ]
        rows = jnp.where(inside, (lane - k == sub).astype(f32), rows)
        for i in range(PANEL):
            scale = 1.0 / cols[i][i:i + 1, :]
            factor = cols[i] - (sub == i).astype(f32)
            for j in range(i + 1, PANEL):
                cols[j] = cols[j] - factor * (cols[j][i:i + 1, :] * scale)
            rows = rows - factor * (rows[i:i + 1, :] * scale)
        rest = jnp.where(inside, 0.0, a)
        for i in range(PANEL):
            rest = rest - a[:, k + i:k + i + 1] * rows[i:i + 1, :]
        pieces = [rest[:k]] if k else []
        pieces.append(rows)
        if k + PANEL < BLOCK:
            pieces.append(rest[k + PANEL:])
        a = jnp.concatenate(pieces, axis=0)
    return a


def solve_kernel(
    first_ref, whole_ref, weighted_ref, precoded_ref, slots_ref, pivots_ref, users_ref, work_ref
):
    work_ref[...] = whole_ref[...]

    @pl.loop(0, EPOCHS)
    def _(b):
        start = pl.ds(pl.multiple_of(b * BLOCK, BLOCK), BLOCK)
        pivots_ref[b] = invert_block(work_ref[start, start])
        for k in range(EPOCHS):
            here = slice(k * BLOCK, (k + 1) * BLOCK)

            @pl.when(b == k)
            def _():
                scaled = split(dot, pivots_ref[k], work_ref[here, here.stop:])
                work_ref[here, here.stop:] = scaled
                if k + 1 < EPOCHS:
                    below = work_ref[here.stop:, here]
                    work_ref[here.stop:, here.stop:] -= split(dot, below, scaled)

    effect = work_ref[TOTAL - BLOCK:, TOTAL:]
    for b in range(EPOCHS - 2, -1, -1):
        here = slice(b * BLOCK, (b + 1) * BLOCK)
        part = work_ref[here, TOTAL:] - split(dot, work_ref[here, here.stop:TOTAL], effect)
        effect = jnp.concatenate([part, effect], axis=0)
    place = placing(slots_ref, first_ref[0], weighted_ref.shape[0])
    kept = 1.0 - jnp.sum(place, axis=1, keepdims=True)
    users = precoded_ref[...] * kept + split(dot, weighted_ref[...] - place, effect)
    for z in range(4):
        users_ref[z] = users.astype(bf16)


def make_solve(first, whole, weighted, precoded, slot_plane):
    return pl.pallas_call(
        solve_kernel,
        out_shape=(
            jax.ShapeDtypeStruct((EPOCHS, BLOCK, BLOCK), f32),
            jax.ShapeDtypeStruct((4, weighted.shape[0], STREAMS), bf16),
        ),
        in_specs=[SMEM] + [VMEM] * 4,
        out_specs=(VMEM,) * 2,
        scratch_shapes=[pltpu.VMEM(whole.shape, f32)],
        compiler_params=params(),
        cost_estimate=cost(14_000_000_000, 4_000_000),
        name="solve",
    )(first, whole, weighted, precoded, slot_plane)


def inverse_of(whole_ref, pivots_ref, inv_ref):
    inv_ref[...] = whole_ref[:, :TOTAL]
    row_id = lax.broadcasted_iota(jnp.int32, (TOTAL, BLOCK), 0)
    lane_id = lax.broadcasted_iota(jnp.int32, (TOTAL, BLOCK), 1)
    for b in range(EPOCHS):
        here = slice(b * BLOCK, (b + 1) * BLOCK)
        inside = (row_id >= here.start) & (row_id < here.stop)
        rest = jnp.where(inside, 0.0, inv_ref[:, here])
        inv_ref[:, here] = (row_id == lane_id + here.start).astype(f32)
        scaled = split(dot, pivots_ref[b], inv_ref[here, :])
        inv_ref[here, :] = jnp.zeros((BLOCK, TOTAL), f32)
        inv_ref[...] = inv_ref[...] - split(dot, rest, scaled)
        inv_ref[here, :] = scaled


def signal_kernel(users_ref, channel_ref, out_ref, held_ref, sems):
    groups, _, antennas = channel_ref.shape
    tile = antennas // 2
    copies = []
    for g in range(groups):
        for m in range(0, antennas, tile):
            part = t_dot(users_ref[g], channel_ref[g, :, m:m + tile]).astype(bf16)
            held_ref[g, :, :, m:m + tile] = part.reshape(16, STREAMS // 16, tile)
        copy = pltpu.make_async_copy(held_ref.at[g], out_ref.at[:, g], sems.at[g])
        copy.start()
        copies.append(copy)
    for copy in copies:
        copy.wait()


def make_signal(users_side, channel):
    groups, _, antennas = channel.shape
    each = STREAMS // 16
    return pl.pallas_call(
        signal_kernel,
        out_shape=jax.ShapeDtypeStruct((16, groups, each, antennas), bf16),
        in_specs=[VMEM, VMEM],
        out_specs=HBM,
        scratch_shapes=[
            pltpu.VMEM((groups, 16, each, antennas), bf16),
            pltpu.SemaphoreType.DMA((groups,)),
        ],
        compiler_params=params(),
        cost_estimate=cost(800_000_000, 7_000_000),
        name="signal",
    )(users_side, channel)


def total_kernel(received_ref, signal_ref, power_ref, sums_ref):
    g = pl.program_id(0)
    signal = jnp.sum(received_ref[:, 0].astype(f32), axis=0)
    signal_ref[0] = signal
    power = jnp.sum(signal * signal)
    lane = lax.broadcasted_iota(jnp.int32, sums_ref.shape, 1)

    @pl.when(g == 0)
    def _():
        sums_ref[...] = jnp.zeros(sums_ref.shape, f32)

    sums_ref[...] = jnp.where(lane == g, power, sums_ref[...])

    @pl.when(g == pl.num_programs(0) - 1)
    def _():
        power_ref[...] = jnp.broadcast_to(sums_ref[...][None], power_ref.shape)


def make_total(received):
    sources, groups, each, antennas = received.shape
    return pl.pallas_call(
        total_kernel,
        out_shape=(
            jax.ShapeDtypeStruct((groups, each, antennas), f32),
            jax.ShapeDtypeStruct((64, 1, 128), f32),
        ),
        grid=(groups,),
        in_specs=[pl.BlockSpec((sources, 1, each, antennas), lambda g: (0, g, 0, 0))],
        out_specs=(
            pl.BlockSpec((1, each, antennas), lambda g: (g, 0, 0)),
            pl.BlockSpec((64, 1, 128), lambda g: (0, 0, 0)),
        ),
        scratch_shapes=[pltpu.VMEM((1, 128), f32)],
        compiler_params=params(),
        cost_estimate=cost(2_000_000_000, 4_000_000),
        name="total",
    )(received)


def update_kernel(
    where_ref, weighted_ref, whole_ref, pivots_ref, all_ref, slots_ref,
    out0, out1, out2, out3, inv_ref, held_ref, sems,
):
    first, plane = where_ref[0], where_ref[1]
    user_rows = weighted_ref.shape[0]
    inverse_of(whole_ref, pivots_ref, inv_ref)
    border = weighted_ref[...] - placing(slots_ref, first, user_rows)
    half = split(dot, border, inv_ref[...]).astype(bf16)
    copies = []
    for d, out in enumerate([out0, out1, out2, out3]):
        z = (plane + d) % 4
        there = all_ref[pl.ds(4 * z, 4)].reshape(4 * user_rows, TOTAL).astype(f32)
        there = there - placing(slots_ref, 4 * user_rows * z, 4 * user_rows)
        held_ref[d] = dot_t(half, there.astype(bf16)).astype(bf16)
        copy = pltpu.make_async_copy(held_ref.at[d], out, sems.at[d])
        copy.start()
        copies.append(copy)
    for copy in copies:
        copy.wait()


def make_update(where, weighted, whole, pivots, weighted_all, slot_plane):
    user_rows = weighted.shape[0]
    return pl.pallas_call(
        update_kernel,
        out_shape=(jax.ShapeDtypeStruct((user_rows, 4 * user_rows), bf16),) * 4,
        in_specs=[SMEM] + [VMEM] * 5,
        out_specs=(HBM,) * 4,
        scratch_shapes=[
            pltpu.VMEM((TOTAL, TOTAL), f32),
            pltpu.VMEM((4, user_rows, 4 * user_rows), bf16),
            pltpu.SemaphoreType.DMA((4,)),
        ],
        compiler_params=params(),
        cost_estimate=cost(1_500_000_000, 8_000_000),
        name="update",
    )(where, weighted, whole, pivots, weighted_all, slot_plane)


def local(channels, inverse, arrivals, arrival_cell, cell_owner, slots, symbols):
    group_count, user_rows, antennas = channels.shape
    user_cols = inverse.shape[2]
    capacity = arrivals.shape[2]
    cell_count = cell_owner.shape[0]
    grp_index = lax.axis_index("grp")
    row_index = lax.axis_index("row")
    col_index = lax.axis_index("col")
    y_index, x_index = row_index // 4, row_index % 4

    def along_x(value, step):
        pairs = [(4 * y + x, 4 * y + (x + step) % 4) for y in range(4) for x in range(4)]
        return lax.ppermute(value, "row", pairs)

    def along_y(value, step):
        pairs = [(4 * y + x, 4 * ((y + step) % 4) + x) for y in range(4) for x in range(4)]
        return lax.ppermute(value, "row", pairs)

    def along_z(value, step):
        return lax.ppermute(value, "col", [(z, (z + step) % 4) for z in range(4)])

    def to_planes(value):
        padded = jnp.concatenate([value, jnp.zeros_like(value[:1])], axis=0)
        return lax.all_to_all(padded, "col", 0, 0, tiled=True)

    first_group = grp_index * group_count
    other_first = (1 - grp_index) * group_count
    first_row = row_index * user_rows
    first_arg = first_row.reshape(1)

    with jax.named_scope("newcomers"):
        mine = lax.dynamic_slice_in_dim(arrivals, first_group, group_count, 0)
        theirs = lax.dynamic_slice_in_dim(arrivals, other_first, group_count, 0)
        swapped = lax.ppermute(theirs, "grp", [(0, 1), (1, 0)])
        from_0 = jnp.where(grp_index == 0, mine, swapped)
        from_1 = jnp.where(grp_index == 0, swapped, mine)
        chunk = jnp.stack([from_0, from_1], axis=2)
        per_group = EPOCHS * 2 * capacity
        chunk = chunk.reshape(group_count * per_group, antennas)
        chunk = jnp.pad(chunk, ((0, 112 - group_count * per_group), (0, 0)))
        gathered = lax.all_gather(chunk, "row")

    with jax.named_scope("planes"):
        pieces = list(make_pieces(x_index.reshape(1), inverse))
        for d in (1, 2, 3):
            pieces[d] = along_x(pieces[d], d)
        square = to_planes(jnp.stack(pieces, axis=1))
        symbol_part = jnp.einsum(
            "grc,gcs->grs", inverse, symbols.astype(f32), precision=highest
        )
        precoded = jnp.sum(to_planes(symbol_part), axis=0)

    plane_group = first_group + jnp.minimum(col_index, group_count - 1)
    slot_plane = lax.dynamic_slice_in_dim(slots, plane_group, 1, 0).reshape(1, TOTAL)
    row_ids = first_row + jnp.arange(user_rows, dtype=jnp.int32)

    cells_mine = lax.dynamic_slice_in_dim(arrival_cell, first_group, group_count, 0)[..., 0]
    slots_mine = lax.dynamic_slice_in_dim(slots, first_group, group_count, 0)
    slots_mine = slots_mine.reshape(group_count, 1, TOTAL)
    cell_table = (cells_mine[..., None] == jnp.arange(cell_count, dtype=jnp.int32)).astype(
        jnp.int32
    )
    owners = jnp.sum(cell_table * cell_owner, axis=-1)
    arrival_order = jnp.arange(ARRIVE, dtype=jnp.int32)
    earlier = (cells_mine[..., :, None] == cells_mine[..., None, :]) & (
        arrival_order[:, None] < arrival_order[None, :]
    )
    ranking = jnp.sum(earlier.astype(jnp.int32), axis=-2)
    with jax.named_scope("places"):
        offset = jnp.arange(group_count, dtype=jnp.int32) * per_group % 16
        epoch = jnp.arange(EPOCHS, dtype=jnp.int32)
        inside = offset[:, None] + epoch[None, :] * 2 * capacity
        inside = inside[:, :, None] + owners // 16 * capacity + ranking
        place = (owners % 16 * WINDOW + inside).reshape(group_count, 1, TOTAL)
        plane_place = lax.dynamic_slice_in_dim(
            place, jnp.minimum(col_index, group_count - 1), 1, 0
        ).reshape(1, TOTAL)

    with jax.named_scope("columns"):
        gathered, square, precoded = lax.optimization_barrier((gathered, square, precoded))
        both = make_columns(row_index.reshape(1), gathered, channels, place)
        both = lax.all_to_all(both, "col", 0, 0, tiled=True)
        summed = jnp.sum(both.astype(f32), axis=0)
        own = summed[:user_rows].astype(bf16)
        by_row = [own] + [along_x(own, d) for d in (1, 2, 3)]
        by_col = [own] + [along_y(own, -d) for d in (1, 2, 3)]

    with jax.named_scope("schur"):
        where = jnp.stack([y_index, row_index, first_row])
        base = make_target(where, summed, precoded, slot_plane, plane_place)
        block0, block1, block2, block3, packed = make_middle(where, square, by_row, by_col, base)
        weighted = block0
        for d, block in ((1, block1), (2, block2), (3, block3)):
            weighted = weighted + along_x(block, -d).astype(f32)
        weighted_all = lax.all_gather(weighted.astype(bf16), "row")
        packed = packed.reshape(16, SHARE, TOTAL + STREAMS)
        shared = lax.all_to_all(packed, "row", 0, 0, tiled=True)
        shared = jnp.sum(shared.astype(f32), axis=0)
        share_ids = row_index * SHARE + jnp.arange(SHARE, dtype=jnp.int32)
        identity = loading * (
            share_ids[:, None] == jnp.arange(TOTAL, dtype=jnp.int32)[None, :]
        ).astype(f32)
        schur_rows = identity - shared[:, :TOTAL]
        ready = jnp.concatenate([schur_rows, shared[:, TOTAL:]], axis=1)
        ready = jnp.broadcast_to(ready[None], (16, SHARE, TOTAL + STREAMS))
        whole = lax.all_to_all(ready, "row", 0, 0, tiled=True).reshape(TOTAL, TOTAL + STREAMS)

    with jax.named_scope("users"):
        channel = make_channel(first_arg, gathered, channels, place, slots_mine)
        whole, channel = lax.optimization_barrier((whole, channel))
        pivots, users = make_solve(first_arg, whole, weighted, precoded, slot_plane)
        users_side = lax.all_to_all(users, "col", 0, 0, tiled=True)

    with jax.named_scope("update"):
        changes = make_update(
            jnp.stack([first_row, col_index]), weighted, whole, pivots, weighted_all, slot_plane
        )
        changes = [changes[0]] + [along_z(changes[d], d) for d in (1, 2, 3)]

    with jax.named_scope("signal"):
        signal_part = make_signal(users_side, channel)
        received = lax.all_to_all(signal_part, "row", 0, 0, tiled=True)
        received, changes = lax.optimization_barrier((received, changes))
        signal, power = make_total(received)
        power = lax.all_to_all(power, ("row", "col"), 0, 0, tiled=True)
        total_power = jnp.sum(power, axis=(0, 1))[:group_count] / (STREAMS * ANTENNAS)
        transmit = signal * lax.rsqrt(total_power + epsilon)[:, None, None]
        transmit = jnp.swapaxes(transmit, 0, 1)

    with jax.named_scope("final"):
        col_ids = col_index * user_cols + jnp.arange(user_cols, dtype=jnp.int32)
        diagonal = row_ids[:, None] == col_ids[None, :]
        full = jnp.any(slots_mine == row_ids[None, :, None], axis=2)
        gone = jnp.where(diagonal[None] & full[:, :, None], 1.0 / loading, 0.0)
        updated = []
        for g in range(group_count):
            step = (col_index - g) % 4
            add = changes[0]
            for d in (1, 2, 3):
                add = jnp.where(step == d, changes[d], add)
            updated.append(inverse[g] - gone[g] + add.astype(f32))
        updated = jnp.stack(updated, axis=0)
    return (updated, transmit)


def solution(mesh):
    placed = (
        P("grp", "row", "col"),
        P("grp", "row", "col"),
        P(None, None, ("grp", "row"), "col"),
        P(),
        P(),
        P(),
        P("grp", "col", None),
    )
    return jax.shard_map(
        local,
        mesh=mesh,
        in_specs=placed,
        out_specs=(P("grp", "row", "col"), P("row", "grp", "col")),
        check_vma=False,
    )
```

profile of v0, /device:TPU:0, one launch (start us, length us, event | category | flops | bytes accessed | tf_op | source)
XLA Modules:
  0.0 273.9 jit_solution(14186641988844466966)
XLA Ops:
  7.2 1.1 constant_dynamic-slice_fusion.1
  8.4 1.6 collective-permute-done
  10.0 1.0 select_bitcast_fusion.1
  11.3 0.8 pad.6
  12.2 1.9 copy-done.2
  14.3 3.2 %collective-permute-start.2 = (bf16[3,256,256]{2,1,0:T(8,128)(2,1)S(1)}, bf16[3,256,256]{2,1,0:T(8,128)(2,1)S(1)}, u32[]{:S(2)}, u32[]{:S(2)}) collective-permute-start(bf16[3,256,256]{2,1,0:T(8,128)(2,1)S(1)} %get-tuple-element.31), channel_id=1, source_target_pairs={{0,8},{4,12},{8,0},{12,4},{16,24},{20,28},{24,16},{28,20},{32,40},... | collective-permute-start | bytes 1179656 | tf_op jit(solution)/shard_map/planes/ppermute | solution.py:451
  17.5 1.1 collective-permute-start.3
  18.7 0.9 collective-permute-start.1
  19.6 1.6 fusion.20
  21.2 1.1 concatenate.10
  22.3 5.3 %all-to-all-start.1 = ((f32[4,256,256]{2,1,0:T(8,128)}), f32[4,256,256]{2,1,0:T(8,128)S(1)}, u32[]{:S(2)}, u32[]{:S(2)}) async-start(f32[4,256,256]{2,1,0:T(8,128)} %concatenate.10), calls=%async_computation.1 | async-start | bytes 2097152 | tf_op jit(solution)/shard_map/planes/all_to_all | solution.py:462
  27.6 1.0 collective-permute-done.2
  28.6 14.6 %collective-permute-done.3 = bf16[3,256,256]{2,1,0:T(8,128)(2,1)} collective-permute-done((bf16[3,256,256]{2,1,0:T(8,128)(2,1)S(1)}, bf16[3,256,256]{2,1,0:T(8,128)(2,1)}, u32[]{:S(2)}, u32[]{:S(2)}) %collective-permute-start.3) | collective-permute-done | bytes 393248 | tf_op jit(solution)/shard_map/planes/ppermute | solution.py:451
  43.2 2.5 fusion.6
  45.7 1.0 copy-done.15
  46.7 5.3 %all-to-all-start = ((bf16[4,4,256,256]{3,2,1,0:T(8,128)(2,1)}), bf16[4,4,256,256]{3,2,1,0:T(8,128)(2,1)S(1)}, u32[]{:S(2)}, u32[]{:S(2)}) async-start(bf16[4,4,256,256]{3,2,1,0:T(8,128)(2,1)} %fusion.6), calls=%async_computation | async-start | bytes 4194304 | tf_op jit(solution)/shard_map/planes/all_to_all | solution.py:462
  53.3 1.4 reduce_sum.58.precoded_ref
  54.7 23.7 %all-to-all-done.square_ref = bf16[4,4,256,256]{3,2,1,0:T(8,128)(2,1)S(1)} async-done(((bf16[4,4,256,256]{3,2,1,0:T(8,128)(2,1)}), bf16[4,4,256,256]{3,2,1,0:T(8,128)(2,1)S(1)}, u32[]{:S(2)}, u32[]{:S(2)}) %all-to-all-start) | async-done | bytes 2097184 | tf_op jit(solution)/shard_map/planes/all_to_all | solution.py:462
  78.4 7.7 %all-gather.5.cloned.1.call-done = bf16[1792,2048]{1,0:T(8,128)(2,1)} async-done(((bf16[112,2048]{1,0:T(8,128)(2,1)}), bf16[1792,2048]{1,0:T(8,128)(2,1)}) %all-gather.5.cloned.1.call-update) | async-done | bytes 7340048 | tf_op jit(solution)/shard_map/newcomers/all_gather | solution.py:479
  86.1 9.7 %columns.1 = bf16[4,304,384]{2,1,0:T(8,128)(2,1)} custom-call(s32[1]{0:T(128)} %bitcast.3.row_ref, bf16[16,112,2048]{2,1,0:T(8,128)(2,1)} %bitcast.71, bf16[3,256,2048]{2,1,0:T(8,128)(2,1)} %channel_ref.3, s32[3,1,384]{2,1,0:T(1,128)} %fusion.17.place_ref), custom_call_target="tpu_custom_call" | custom-call | flops 4000000000 | bytes 12000000 | tf_op jit(solution)/shard_map/columns/columns/pallas_call | solution.py:115
  95.8 4.5 %all-to-all-start.2 = ((bf16[4,304,384]{2,1,0:T(8,128)(2,1)}), bf16[4,304,384]{2,1,0:T(8,128)(2,1)}, u32[]{:S(2)}, u32[]{:S(2)}) async-start(bf16[4,304,384]{2,1,0:T(8,128)(2,1)} %columns.1), calls=%async_computation.2 | async-start | bytes 1867776 | tf_op jit(solution)/shard_map/columns/all_to_all | solution.py:520
  100.3 14.0 %all-to-all-done.2 = bf16[4,304,384]{2,1,0:T(8,128)(2,1)} async-done(((bf16[4,304,384]{2,1,0:T(8,128)(2,1)}), bf16[4,304,384]{2,1,0:T(8,128)(2,1)}, u32[]{:S(2)}, u32[]{:S(2)}) %all-to-all-start.2) | async-done | bytes 933920 | tf_op jit(solution)/shard_map/columns/all_to_all | solution.py:520
  114.3 1.4 convert_reduce_fusion.summed_ref
  115.7 1.6 collective-permute-start.4
  118.0 2.6 collective-permute-start.5
  120.6 1.5 collective-permute-start.6
  122.1 1.1 collective-permute-start.7
  123.2 1.2 collective-permute-start.8
  124.4 3.8 %collective-permute-start.9 = (bf16[256,384]{1,0:T(8,128)(2,1)S(1)}, bf16[256,384]{1,0:T(8,128)(2,1)S(1)}, u32[]{:S(2)}, u32[]{:S(2)}) collective-permute-start(bf16[256,384]{1,0:T(8,128)(2,1)S(1)} %slice.74.own_ref), channel_id=1, source_target_pairs={{0,16},{4,20},{8,24},{12,28},{16,32},{20,36},{24,40},{28,44},{32,4... | collective-permute-start | bytes 589832 | tf_op jit(solution)/shard_map/columns/ppermute | solution.py:455
  128.3 1.0 target.1.base_ref
  129.3 1.9 collective-permute-done.8.col2_ref
  131.2 2.1 collective-permute-done.9.col3_ref
  133.3 3.5 %middle.1 = (f32[256,384]{1,0:T(8,128)S(1)}, bf16[256,384]{1,0:T(8,128)(2,1)}, bf16[256,384]{1,0:T(8,128)(2,1)}, bf16[256,384]{1,0:T(8,128)(2,1)}, bf16[384,640]{1,0:T(8,128)(2,1)}) custom-call(s32[3]{0:T(128)S(1)} %pad_add_fusion.where_ref, bf16[4,4,256,256]{3,2,1,0:T(8,128)(2,1)S(1)} %all-to-all-done.square_ref, bf16[256,384]{1,0:T(8,128)(2,1)S(1)} %slice.74.own_ref, ...), custom_call_target="tpu_custom_call" | custom-call | flops 2000000000 | bytes 8000000 | tf_op jit(solution)/shard_map/schur/middle/pallas_call | solution.py:220
  137.3 2.1 collective-permute-start.11
  139.4 0.9 collective-permute-start.12
  140.3 5.4 %all-to-all-start.3 = ((bf16[16,24,640]{2,1,0:T(8,128)(2,1)}), bf16[16,24,640]{2,1,0:T(8,128)(2,1)S(1)}, u32[]{:S(2)}, u32[]{:S(2)}) async-start(bf16[16,24,640]{2,1,0:T(8,128)(2,1)} %bitcast.13), calls=%async_computation.3 | async-start | bytes 983040 | tf_op jit(solution)/shard_map/schur/all_to_all | solution.py:535
  145.8 4.4 %collective-permute-done.12 = bf16[256,384]{1,0:T(8,128)(2,1)S(1)} collective-permute-done((bf16[256,384]{1,0:T(8,128)(2,1)}, bf16[256,384]{1,0:T(8,128)(2,1)S(1)}, u32[]{:S(2)}, u32[]{:S(2)}) %collective-permute-start.12) | collective-permute-done | bytes 196640 | tf_op jit(solution)/shard_map/schur/ppermute | solution.py:451
  151.0 4.7 %all-to-all-done.3 = bf16[16,24,640]{2,1,0:T(8,128)(2,1)S(1)} async-done(((bf16[16,24,640]{2,1,0:T(8,128)(2,1)}), bf16[16,24,640]{2,1,0:T(8,128)(2,1)S(1)}, u32[]{:S(2)}, u32[]{:S(2)}) %all-to-all-start.3) | async-done | bytes 491552 | tf_op jit(solution)/shard_map/schur/all_to_all | solution.py:535
  155.9 1.0 broadcast_in_dim.10
  156.9 3.6 %all-to-all-start.4 = ((f32[16,24,640]{2,1,0:T(8,128)}), f32[16,24,640]{2,1,0:T(8,128)S(1)}, u32[]{:S(2)}, u32[]{:S(2)}) async-start(f32[16,24,640]{2,1,0:T(8,128)} %broadcast_in_dim.10), calls=%async_computation.4 | async-start | bytes 1966080 | tf_op jit(solution)/shard_map/schur/all_to_all | solution.py:544
  161.1 8.2 %channel.1.channel_ref = bf16[3,256,2048]{2,1,0:T(8,128)(2,1)} custom-call(s32[1]{0:T(128)} %bitcast.1.first_ref, bf16[16,112,2048]{2,1,0:T(8,128)(2,1)} %bitcast.72, bf16[3,256,2048]{2,1,0:T(8,128)(2,1)} %channel_ref.3, s32[3,1,384]{2,1,0:T(1,128)} %fusion.17.place_ref, s32[3,1,384]{2,1,0:T(1,128)} %reshape.274.slots_ref), custom_call_target="tpu_custom_call" | custom-call | flops 4000000000 | bytes 14000000 | tf_op jit(solution)/shard_map/users/channel/pallas_call | solution.py:143
  169.3 7.5 %all-to-all-done.4 = f32[16,24,640]{2,1,0:T(8,128)S(1)} async-done(((f32[16,24,640]{2,1,0:T(8,128)}), f32[16,24,640]{2,1,0:T(8,128)S(1)}, u32[]{:S(2)}, u32[]{:S(2)}) %all-to-all-start.4) | async-done | bytes 983072 | tf_op jit(solution)/shard_map/schur/all_to_all | solution.py:544
  176.9 13.0 %solve.1 = (f32[3,128,128]{2,1,0:T(8,128)S(1)}, bf16[4,256,256]{2,1,0:T(8,128)(2,1)S(1)}) custom-call(s32[1]{0:T(128)} %bitcast.1.first_ref, f32[384,640]{1,0:T(8,128)S(1)} %bitcast.60, f32[256,384]{1,0:T(8,128)S(1)} %get-tuple-element.57.weighted_ref, f32[256,256]{1,0:T(8,128)S(1)} %reduce_sum.58.precoded_ref, s32[1,384]{1,0:T(1,128)S(1)} %bitcast.64), custom_call_target="tpu_custom_call" | custom-call | flops 14000000000 | bytes 4000000 | tf_op jit(solution)/shard_map/users/solve/pallas_call | solution.py:297
  190.5 10.5 %all_to_all.40.users_ref = bf16[4,256,256]{2,1,0:T(8,128)(2,1)S(1)} all-to-all(bf16[4,256,256]{2,1,0:T(8,128)(2,1)S(1)} %get-tuple-element.42), channel_id=1, replica_groups=mesh['grp'=2,'row'=16,'col'=4] {'col'}, dimensions={0} | all-to-all | bytes 1048576 | tf_op jit(solution)/shard_map/users/all_to_all | solution.py:550
  201.0 2.1 signal.1
  203.1 3.8 %all-to-all-start.6 = ((bf16[16,3,16,2048]{3,2,1,0:T(8,128)(2,1)}), bf16[16,3,16,2048]{3,2,1,0:T(8,128)(2,1)S(1)}, u32[]{:S(2)}, u32[]{:S(2)}) async-start(bf16[16,3,16,2048]{3,2,1,0:T(8,128)(2,1)} %signal.1), calls=%async_computation.6 | async-start | bytes 6291456 | tf_op jit(solution)/shard_map/signal/all_to_all | solution.py:560
  207.7 0.8 compare_reduce_fusion
  208.5 1.2 copy-done.9
  209.7 1.9 copy-done.12
  211.6 0.9 copy-done.14
  212.5 5.6 %update.1 = (bf16[256,1024]{1,0:T(8,128)(2,1)S(1)}, bf16[256,1024]{1,0:T(8,128)(2,1)}, bf16[256,1024]{1,0:T(8,128)(2,1)}, bf16[256,1024]{1,0:T(8,128)(2,1)}) custom-call(s32[2]{0:T(128)S(1)} %pad_add_fusion.1.where_ref, f32[256,384]{1,0:T(8,128)S(1)} %get-tuple-element.57.weighted_ref, f32[384,640]{1,0:T(8,128)S(1)} %bitcast.61, ...), custom_call_target="tpu_custom_call" | custom-call | flops 1500000000 | bytes 8000000 | tf_op jit(solution)/shard_map/update/update/pallas_call | solution.py:423
  218.8 2.1 collective-permute-start.14
  220.8 0.8 collective-permute-start.15
  221.9 2.1 and_select_fusion
  224.0 21.1 %all-to-all-done.6.received_ref = bf16[16,3,16,2048]{3,2,1,0:T(8,128)(2,1)S(1)} async-done(((bf16[16,3,16,2048]{3,2,1,0:T(8,128)(2,1)}), bf16[16,3,16,2048]{3,2,1,0:T(8,128)(2,1)S(1)}, u32[]{:S(2)}, u32[]{:S(2)}) %all-to-all-start.6) | async-done | bytes 3145760 | tf_op jit(solution)/shard_map/signal/all_to_all | solution.py:560
  245.1 1.6 copy-done.5
  246.7 1.9 copy-done.6
  248.6 1.3 total.1
  250.5 5.4 %all-to-all-start.7 = ((f32[64,1,128]{2,1,0:T(1,128)}), f32[64,1,128]{2,1,0:T(1,128)}, u32[]{:S(2)}, u32[]{:S(2)}) async-start(f32[64,1,128]{2,1,0:T(1,128)} %copy-done.11), calls=%async_computation.7 | async-start | bytes 65536 | tf_op jit(solution)/shard_map/signal/all_to_all | solution.py:563
  256.0 3.0 %fusion.15 = (f32[1,256,1024]{2,1,0:T(8,128)S(1)}, f32[1,256,1024]{2,1,0:T(8,128)S(1)}, f32[1,256,1024]{2,1,0:T(8,128)S(1)}) fusion(f32[3,256,1024]{2,1,0:T(8,128)} %and_select_fusion, f32[3,256,1024]{2,1,0:T(8,128)S(1)} %copy-done.4, bf16[256,1024]{1,0:T(8,128)(2,1)} %collective-permute-done.15, bf16[256,1024]{1,0:T(8,128)(2,1)} %collective-permute-done.14, ...), kind=kLoop, calls=%fused_computation.23 | loop fusion | flops 4718592 | bytes 11534345 | tf_op jit(solution)/shard_map/final/stack | solution.py:580
  259.0 1.9 pad_maximum_fusion
  260.9 4.4 %all-to-all-done.7 = f32[64,1,128]{2,1,0:T(1,128)} async-done(((f32[64,1,128]{2,1,0:T(1,128)}), f32[64,1,128]{2,1,0:T(1,128)}, u32[]{:S(2)}, u32[]{:S(2)}) %all-to-all-start.7) | async-done | bytes 32800 | tf_op jit(solution)/shard_map/signal/all_to_all | solution.py:563
  265.3 0.8 reduce_sum.65
  266.2 0.8 multiply_bitcast_fusion
  (94 shorter events, 7.7 us)
Async XLA Ops:
  7.2 12.4 %copy-start = (bf16[3,1024,256]{2,1,0:T(8,128)(2,1)S(1)}, bf16[3,1024,256]{2,1,0:T(8,128)(2,1)}, u32[]{:S(2)}) copy-start(bf16[3,1024,256]{2,1,0:T(8,128)(2,1)} %param.13) | copy-start | bytes 4718596
  7.2 78.9 %all-gather.5.cloned.1.call-start = ((), (), s32[]{:S(2)}) async-start(), calls=%async_computation.8 | async-start | bytes 7798784 | tf_op jit(solution)/shard_map/newcomers/all_gather | solution.py:479
  8.3 1.7 collective-permute-start
  12.2 1.9 copy-start.2
  14.1 5.4 %copy-start.3 = (f32[3,256,1024]{2,1,0:T(8,128)S(1)}, f32[3,256,1024]{2,1,0:T(8,128)}, u32[]{:S(2)}) copy-start(f32[3,256,1024]{2,1,0:T(8,128)} %inverse_ref.1) | copy-start | bytes 9437188
  14.3 14.3 %collective-permute-start.2 = (bf16[3,256,256]{2,1,0:T(8,128)(2,1)S(1)}, bf16[3,256,256]{2,1,0:T(8,128)(2,1)S(1)}, u32[]{:S(2)}, u32[]{:S(2)}) collective-permute-start(bf16[3,256,256]{2,1,0:T(8,128)(2,1)S(1)} %get-tuple-element.31), channel_id=1, source_target_pairs={{0,8},{4,12},{8,0},{12,4},{16,24},{20,28},{24,16},{28,20},{32,40},... | collective-permute-start | bytes 1179656 | tf_op jit(solution)/shard_map/planes/ppermute | solution.py:451
  17.5 25.7 %collective-permute-start.3 = (bf16[3,256,256]{2,1,0:T(8,128)(2,1)S(1)}, bf16[3,256,256]{2,1,0:T(8,128)(2,1)}, u32[]{:S(2)}, u32[]{:S(2)}) collective-permute-start(bf16[3,256,256]{2,1,0:T(8,128)(2,1)S(1)} %get-tuple-element.32), channel_id=1, source_target_pairs={{0,12},{4,0},{8,4},{12,8},{16,28},{20,16},{24,20},{28,24},{32,44},... | collective-permute-start | bytes 1179656 | tf_op jit(solution)/shard_map/planes/ppermute | solution.py:451
  18.7 24.5 %collective-permute-start.1 = (bf16[3,256,256]{2,1,0:T(8,128)(2,1)S(1)}, bf16[3,256,256]{2,1,0:T(8,128)(2,1)}, u32[]{:S(2)}, u32[]{:S(2)}) collective-permute-start(bf16[3,256,256]{2,1,0:T(8,128)(2,1)S(1)} %get-tuple-element.30), channel_id=1, source_target_pairs={{0,4},{4,8},{8,12},{12,0},{16,20},{20,24},{24,28},{28,16},{32,36},... | collective-permute-start | bytes 1179656 | tf_op jit(solution)/shard_map/planes/ppermute | solution.py:451
  22.3 23.3 %all-to-all-start.1 = ((f32[4,256,256]{2,1,0:T(8,128)}), f32[4,256,256]{2,1,0:T(8,128)S(1)}, u32[]{:S(2)}, u32[]{:S(2)}) async-start(f32[4,256,256]{2,1,0:T(8,128)} %concatenate.10), calls=%async_computation.1 | async-start | bytes 2097152 | tf_op jit(solution)/shard_map/planes/all_to_all | solution.py:462
  43.2 8.8 %copy-start.21 = (s32[6,3,128,1]{2,3,1,0:T(1,128)S(1)}, s32[6,3,128,1]{2,3,1,0:T(1,128)}, u32[]{:S(2)}) copy-start(s32[6,3,128,1]{2,3,1,0:T(1,128)} %param.10) | copy-start | bytes 27652
  43.2 9.1 %copy-start.22 = (s32[32]{0:T(128)S(1)}, s32[32]{0:T(128)}, u32[]{:S(2)}) copy-start(s32[32]{0:T(128)} %param.11) | copy-start | bytes 388
  45.7 1.0 copy-start.15
  46.7 31.7 %all-to-all-start = ((bf16[4,4,256,256]{3,2,1,0:T(8,128)(2,1)}), bf16[4,4,256,256]{3,2,1,0:T(8,128)(2,1)S(1)}, u32[]{:S(2)}, u32[]{:S(2)}) async-start(bf16[4,4,256,256]{3,2,1,0:T(8,128)(2,1)} %fusion.6), calls=%async_computation | async-start | bytes 4194304 | tf_op jit(solution)/shard_map/planes/all_to_all | solution.py:462
  95.8 21.5 %copy-start.16 = (s32[6,3,128]{2,1,0:T(4,128)S(1)}, s32[6,3,128]{2,1,0:T(4,128)}, u32[]{:S(2)}) copy-start(s32[6,3,128]{2,1,0:T(4,128)} %param.12) | copy-start | bytes 27652
  95.8 18.5 %all-to-all-start.2 = ((bf16[4,304,384]{2,1,0:T(8,128)(2,1)}), bf16[4,304,384]{2,1,0:T(8,128)(2,1)}, u32[]{:S(2)}, u32[]{:S(2)}) async-start(bf16[4,304,384]{2,1,0:T(8,128)(2,1)} %columns.1), calls=%async_computation.2 | async-start | bytes 1867776 | tf_op jit(solution)/shard_map/columns/all_to_all | solution.py:520
  115.7 8.7 %collective-permute-start.4 = (bf16[256,384]{1,0:T(8,128)(2,1)S(1)}, bf16[256,384]{1,0:T(8,128)(2,1)S(1)}, u32[]{:S(2)}, u32[]{:S(2)}) collective-permute-start(bf16[256,384]{1,0:T(8,128)(2,1)S(1)} %slice.74.own_ref), channel_id=1, source_target_pairs={{0,4},{4,8},{8,12},{12,0},{16,20},{20,24},{24,28},{28,16},{32,36},... | collective-permute-start | bytes 589832 | tf_op jit(solution)/shard_map/columns/ppermute | solution.py:451
  118.0 11.3 %collective-permute-start.5 = (bf16[256,384]{1,0:T(8,128)(2,1)S(1)}, bf16[256,384]{1,0:T(8,128)(2,1)S(1)}, u32[]{:S(2)}, u32[]{:S(2)}) collective-permute-start(bf16[256,384]{1,0:T(8,128)(2,1)S(1)} %slice.74.own_ref), channel_id=1, source_target_pairs={{0,8},{4,12},{8,0},{12,4},{16,24},{20,28},{24,16},{28,20},{32,40},... | collective-permute-start | bytes 589832 | tf_op jit(solution)/shard_map/columns/ppermute | solution.py:451
  120.6 8.6 %collective-permute-start.6 = (bf16[256,384]{1,0:T(8,128)(2,1)S(1)}, bf16[256,384]{1,0:T(8,128)(2,1)S(1)}, u32[]{:S(2)}, u32[]{:S(2)}) collective-permute-start(bf16[256,384]{1,0:T(8,128)(2,1)S(1)} %slice.74.own_ref), channel_id=1, source_target_pairs={{0,12},{4,0},{8,4},{12,8},{16,28},{20,16},{24,20},{28,24},{32,44},... | collective-permute-start | bytes 589832 | tf_op jit(solution)/shard_map/columns/ppermute | solution.py:451
  122.1 7.1 %collective-permute-start.7 = (bf16[256,384]{1,0:T(8,128)(2,1)S(1)}, bf16[256,384]{1,0:T(8,128)(2,1)S(1)}, u32[]{:S(2)}, u32[]{:S(2)}) collective-permute-start(bf16[256,384]{1,0:T(8,128)(2,1)S(1)} %slice.74.own_ref), channel_id=1, source_target_pairs={{0,48},{4,52},{8,56},{12,60},{16,0},{20,4},{24,8},{28,12},{32,16},... | collective-permute-start | bytes 589832 | tf_op jit(solution)/shard_map/columns/ppermute | solution.py:455
  123.2 8.0 %collective-permute-start.8 = (bf16[256,384]{1,0:T(8,128)(2,1)S(1)}, bf16[256,384]{1,0:T(8,128)(2,1)S(1)}, u32[]{:S(2)}, u32[]{:S(2)}) collective-permute-start(bf16[256,384]{1,0:T(8,128)(2,1)S(1)} %slice.74.own_ref), channel_id=1, source_target_pairs={{0,32},{4,36},{8,40},{12,44},{16,48},{20,52},{24,56},{28,60},{32,0... | collective-permute-start | bytes 589832 | tf_op jit(solution)/shard_map/columns/ppermute | solution.py:455
  124.4 8.9 %collective-permute-start.9 = (bf16[256,384]{1,0:T(8,128)(2,1)S(1)}, bf16[256,384]{1,0:T(8,128)(2,1)S(1)}, u32[]{:S(2)}, u32[]{:S(2)}) collective-permute-start(bf16[256,384]{1,0:T(8,128)(2,1)S(1)} %slice.74.own_ref), channel_id=1, source_target_pairs={{0,16},{4,20},{8,24},{12,28},{16,32},{20,36},{24,40},{28,44},{32,4... | collective-permute-start | bytes 589832 | tf_op jit(solution)/shard_map/columns/ppermute | solution.py:455
  136.8 9.0 %collective-permute-start.10 = (bf16[256,384]{1,0:T(8,128)(2,1)}, bf16[256,384]{1,0:T(8,128)(2,1)S(1)}, u32[]{:S(2)}, u32[]{:S(2)}) collective-permute-start(bf16[256,384]{1,0:T(8,128)(2,1)} %get-tuple-element.39), channel_id=1, source_target_pairs={{0,12},{4,0},{8,4},{12,8},{16,28},{20,16},{24,20},{28,24},{32,44},... | collective-permute-start | bytes 589832 | tf_op jit(solution)/shard_map/schur/ppermute | solution.py:451
  137.3 8.5 %collective-permute-start.11 = (bf16[256,384]{1,0:T(8,128)(2,1)}, bf16[256,384]{1,0:T(8,128)(2,1)S(1)}, u32[]{:S(2)}, u32[]{:S(2)}) collective-permute-start(bf16[256,384]{1,0:T(8,128)(2,1)} %get-tuple-element.40), channel_id=1, source_target_pairs={{0,8},{4,12},{8,0},{12,4},{16,24},{20,28},{24,16},{28,20},{32,40},... | collective-permute-start | bytes 589832 | tf_op jit(solution)/shard_map/schur/ppermute | solution.py:451
  139.4 10.8 %collective-permute-start.12 = (bf16[256,384]{1,0:T(8,128)(2,1)}, bf16[256,384]{1,0:T(8,128)(2,1)S(1)}, u32[]{:S(2)}, u32[]{:S(2)}) collective-permute-start(bf16[256,384]{1,0:T(8,128)(2,1)} %get-tuple-element.41), channel_id=1, source_target_pairs={{0,4},{4,8},{8,12},{12,0},{16,20},{20,24},{24,28},{28,16},{32,36},... | collective-permute-start | bytes 589832 | tf_op jit(solution)/shard_map/schur/ppermute | solution.py:451
  140.3 15.4 %all-to-all-start.3 = ((bf16[16,24,640]{2,1,0:T(8,128)(2,1)}), bf16[16,24,640]{2,1,0:T(8,128)(2,1)S(1)}, u32[]{:S(2)}, u32[]{:S(2)}) async-start(bf16[16,24,640]{2,1,0:T(8,128)(2,1)} %bitcast.13), calls=%async_computation.3 | async-start | bytes 983040 | tf_op jit(solution)/shard_map/schur/all_to_all | solution.py:535
  145.7 62.8 %all-gather.7.cloned.1.call-start = ((), (), s32[]{:S(2)}) async-start(), calls=%async_computation.9 | async-start | bytes 3342336 | tf_op jit(solution)/shard_map/schur/all_gather | solution.py:533
  156.9 20.0 %all-to-all-start.4 = ((f32[16,24,640]{2,1,0:T(8,128)}), f32[16,24,640]{2,1,0:T(8,128)S(1)}, u32[]{:S(2)}, u32[]{:S(2)}) async-start(f32[16,24,640]{2,1,0:T(8,128)} %broadcast_in_dim.10), calls=%async_computation.4 | async-start | bytes 1966080 | tf_op jit(solution)/shard_map/schur/all_to_all | solution.py:544
  176.8 13.0 %copy-start.8 = (f32[16,24,640]{2,1,0:T(8,128)}, f32[16,24,640]{2,1,0:T(8,128)S(1)}, u32[]{:S(2)}) copy-start(f32[16,24,640]{2,1,0:T(8,128)S(1)} %all-to-all-done.4) | copy-start | bytes 2949124
  176.8 24.2 %copy-start.7 = (bf16[3,256,2048]{2,1,0:T(8,128)(2,1)S(1)}, bf16[3,256,2048]{2,1,0:T(8,128)(2,1)}, u32[]{:S(2)}) copy-start(bf16[3,256,2048]{2,1,0:T(8,128)(2,1)} %channel.1.channel_ref) | copy-start | bytes 9437188
  189.9 0.7 copy-start.13
  203.1 41.9 %all-to-all-start.6 = ((bf16[16,3,16,2048]{3,2,1,0:T(8,128)(2,1)}), bf16[16,3,16,2048]{3,2,1,0:T(8,128)(2,1)S(1)}, u32[]{:S(2)}, u32[]{:S(2)}) async-start(bf16[16,3,16,2048]{3,2,1,0:T(8,128)(2,1)} %signal.1), calls=%async_computation.6 | async-start | bytes 6291456 | tf_op jit(solution)/shard_map/signal/all_to_all | solution.py:560
  207.1 0.6 copy-start.19
  208.5 13.2 %copy-start.20 = (s32[256]{0:T(256)S(1)}, s32[256]{0:T(256)}, u32[]{:S(2)}) copy-start(s32[256]{0:T(256)} %copy-done.19) | copy-start | bytes 3076
  208.5 13.4 %copy-start.18 = (pred[3,256]{1,0:T(4,128)(4,1)S(1)}, pred[3,256]{1,0:T(4,128)(4,1)}, u32[]{:S(2)}) copy-start(pred[3,256]{1,0:T(4,128)(4,1)} %compare_reduce_fusion) | copy-start | bytes 2308
  208.5 1.2 copy-start.9
  209.7 1.9 copy-start.12
  211.6 0.9 copy-start.14
  212.5 9.1 %copy-start.17 = (s32[1024]{0:T(1024)S(1)}, s32[1024]{0:T(1024)}, u32[]{:S(2)}) copy-start(s32[1024]{0:T(1024)} %iota_add_fusion) | copy-start | bytes 12292
  218.1 3.8 %copy-start.10 = (bf16[256,1024]{1,0:T(8,128)(2,1)}, bf16[256,1024]{1,0:T(8,128)(2,1)S(1)}, u32[]{:S(2)}) copy-start(bf16[256,1024]{1,0:T(8,128)(2,1)S(1)} %get-tuple-element.52) | copy-start | bytes 1572868
  218.1 28.6 %collective-permute-start.13 = (bf16[256,1024]{1,0:T(8,128)(2,1)}, bf16[256,1024]{1,0:T(8,128)(2,1)}, u32[]{:S(2)}, u32[]{:S(2)}) collective-permute-start(bf16[256,1024]{1,0:T(8,128)(2,1)} %get-tuple-element.46), channel_id=1, source_target_pairs={{0,1},{1,2},{2,3},{3,0},{4,5},{5,6},{6,7},{7,4},{8,9},{9,10},{10,1... | collective-permute-start | bytes 1572872 | tf_op jit(solution)/shard_map/update/ppermute | solution.py:458
  218.8 27.9 %collective-permute-start.14 = (bf16[256,1024]{1,0:T(8,128)(2,1)}, bf16[256,1024]{1,0:T(8,128)(2,1)}, u32[]{:S(2)}, u32[]{:S(2)}) collective-permute-start(bf16[256,1024]{1,0:T(8,128)(2,1)} %get-tuple-element.47), channel_id=1, source_target_pairs={{0,2},{1,3},{2,0},{3,1},{4,6},{5,7},{6,4},{7,5},{8,10},{9,11},{10,... | collective-permute-start | bytes 1572872 | tf_op jit(solution)/shard_map/update/ppermute | solution.py:458
  220.8 25.9 %collective-permute-start.15 = (bf16[256,1024]{1,0:T(8,128)(2,1)}, bf16[256,1024]{1,0:T(8,128)(2,1)}, u32[]{:S(2)}, u32[]{:S(2)}) collective-permute-start(bf16[256,1024]{1,0:T(8,128)(2,1)} %get-tuple-element.48), channel_id=1, source_target_pairs={{0,3},{1,0},{2,1},{3,2},{4,7},{5,4},{6,5},{7,6},{8,11},{9,8},{10,9... | collective-permute-start | bytes 1572872 | tf_op jit(solution)/shard_map/update/ppermute | solution.py:458
  245.1 1.6 copy-start.5
  246.7 1.9 copy-start.6
  248.6 7.4 %copy-start.4 = (f32[3,256,1024]{2,1,0:T(8,128)S(1)}, f32[3,256,1024]{2,1,0:T(8,128)}, u32[]{:S(2)}) copy-start(f32[3,256,1024]{2,1,0:T(8,128)} %inverse_ref.1) | copy-start | bytes 9437188
  249.9 0.6 copy-start.11
  250.5 14.8 %all-to-all-start.7 = ((f32[64,1,128]{2,1,0:T(1,128)}), f32[64,1,128]{2,1,0:T(1,128)}, u32[]{:S(2)}, u32[]{:S(2)}) async-start(f32[64,1,128]{2,1,0:T(1,128)} %copy-done.11), calls=%async_computation.7 | async-start | bytes 65536 | tf_op jit(solution)/shard_map/signal/all_to_all | solution.py:563
  259.0 8.0 %copy-start.1 = (bf16[3,1024,256]{2,1,0:T(8,128)(2,1)S(1)}, bf16[3,1024,256]{2,1,0:T(8,128)(2,1)}, u32[]{:S(2)}) copy-start(bf16[3,1024,256]{2,1,0:T(8,128)(2,1)} %param.13) | copy-start | bytes 4718596
Sparse Core Ops, SparseCore 0:
  12.3 73.7 all-gather.4
  151.1 50.1 all-gather.6
where the time goes:
time: 275 us; the launch traced here: 274 us
  waiting for transfers between devices  109 us (40%)
  starting transfers between devices  57.5 us (21%)
  Pallas kernels  44.6 us (16%)
  other arithmetic  18.8 us (7%)
  local copies, waits for them, and re-layouts  17.6 us (6%)
  between operations  14.5 us (5%)
  blocking collectives  10.5 us (4%)
    all_to_all x2, waiting for transfers between devices, to_planes(): return lax.all_to_all(padded, 'col', 0, 0, tiled=True)  23.7 us
    all_to_all x1, waiting for transfers between devices, local(): received = lax.all_to_all(signal_part, 'row', 0, 0, tiled=True)  21.1 us
    ppermute x9, waiting for transfers between devices, along_x(): return lax.ppermute(value, 'row', pairs)  20 us
    ppermute x9, starting transfers between devices, along_x(): return lax.ppermute(value, 'row', pairs)  14.5 us
    all_to_all x1, waiting for transfers between devices, local(): both = lax.all_to_all(both, 'col', 0, 0, tiled=True)  14 us
    pallas_call x1, Pallas kernels, make_solve(): pl.pallas_call(solve_kernel, out_shape=(jax.ShapeDtypeStruct((EPOCHS, BLO...  13 us
    unnamed x51, local copies, waits for them, and re-layouts  11.9 us
    all_to_all x2, starting transfers between devices, to_planes(): return lax.all_to_all(padded, 'col', 0, 0, tiled=True)  10.6 us
  transfers between devices with their start and end apart: 25, of which 13 were waited for; matrix products, arithmetic and copies ran while one was open for 7% of the time, Pallas kernels for 11%

commit v1 on v0

--- a/solution.py
+++ b/solution.py
@@ -66,7 +66,7 @@
     return (ids == place_ref[g]).astype(f32).astype(bf16)
 
 
-def start_inputs(gathered_ref, channel_ref, window_ref, held_ref, sems, row=None):
+def start_inputs(gathered_ref, channel_ref, window_ref, held_ref, sems):
     groups, user_rows = channel_ref.shape[:2]
     copies = []
     for g in range(groups):
@@ -76,11 +76,6 @@
             pltpu.make_async_copy(channel_ref.at[g], held_ref.at[g, :user_rows], sems.at[0, g]),
             pltpu.make_async_copy(source, window_ref.at[g], sems.at[1, g]),
         ]
-        if row is not None:
-            source = gathered_ref.at[row, pl.ds(start, WINDOW), :]
-            parts.append(
-                pltpu.make_async_copy(source, held_ref.at[g, user_rows:], sems.at[2, g])
-            )
         for part in parts:
             part.start()
         copies.append(parts)
@@ -91,20 +86,28 @@
     return [
         pltpu.VMEM((groups, 16, WINDOW, antennas), bf16),
         pltpu.VMEM((groups, rows, antennas), bf16),
-        pltpu.SemaphoreType.DMA((3, groups)),
+        pltpu.SemaphoreType.DMA((2, groups)),
     ]
 
 
 def columns_kernel(
     row_ref, gathered_ref, channel_ref, place_ref, out_ref, window_ref, held_ref, sems
 ):
-    groups, _, antennas = channel_ref.shape
-    copies = start_inputs(gathered_ref, channel_ref, window_ref, held_ref, sems, row_ref[0])
+    groups, user_rows, antennas = channel_ref.shape
+    copies = []
+    for g in range(groups):
+        start = g * 2 * EPOCHS * 6 // 16 * 16
+        copy = pltpu.make_async_copy(
+            gathered_ref.at[:, pl.ds(start, WINDOW), :], window_ref.at[g], sems.at[g]
+        )
+        copy.start()
+        copies.append(copy)
     out_ref[groups] = jnp.zeros(out_ref.shape[1:], bf16)
     for g in range(groups):
+        held_ref[g, :user_rows] = channel_ref[g]
         choose = choosing(place_ref, g)
-        for copy in copies[g]:
-            copy.wait()
+        copies[g].wait()
+        held_ref[g, user_rows:] = window_ref[g, row_ref[0]]
         window = window_ref[g].reshape(16 * WINDOW, antennas)
         wide = dot_t(held_ref[g], window).astype(bf16)
         out_ref[g] = dot(wide, choose).astype(bf16)
@@ -115,11 +118,15 @@
     return pl.pallas_call(
         columns_kernel,
         out_shape=jax.ShapeDtypeStruct((groups + 1, user_rows + WINDOW, TOTAL), bf16),
-        in_specs=[SMEM, HBM, HBM, VMEM],
+        in_specs=[SMEM, HBM, VMEM, VMEM],
         out_specs=VMEM,
-        scratch_shapes=input_scratch(groups, user_rows + WINDOW, antennas),
-        compiler_params=params(60),
-        cost_estimate=cost(4_000_000_000, 12_000_000),
+        scratch_shapes=[
+            pltpu.VMEM((groups, 16, WINDOW, antennas), bf16),
+            pltpu.VMEM((groups, user_rows + WINDOW, antennas), bf16),
+            pltpu.SemaphoreType.DMA((groups,)),
+        ],
+        compiler_params=params(54),
+        cost_estimate=cost(8_000_000_000, 12_000_000),
         name="columns",
     )(row, gathered, channels, place)
 
@@ -372,7 +379,7 @@
 
     @pl.when(g == pl.num_programs(0) - 1)
     def _():
-        power_ref[...] = jnp.broadcast_to(sums_ref[...][None], power_ref.shape)
+        power_ref[...] = jnp.broadcast_to(sums_ref[...], power_ref.shape)
 
 
 def make_total(received):
@@ -381,13 +388,13 @@
         total_kernel,
         out_shape=(
             jax.ShapeDtypeStruct((groups, each, antennas), f32),
-            jax.ShapeDtypeStruct((64, 1, 128), f32),
+            jax.ShapeDtypeStruct((64 * 8, 128), f32),
         ),
         grid=(groups,),
         in_specs=[pl.BlockSpec((sources, 1, each, antennas), lambda g: (0, g, 0, 0))],
         out_specs=(
             pl.BlockSpec((1, each, antennas), lambda g: (g, 0, 0)),
-            pl.BlockSpec((64, 1, 128), lambda g: (0, 0, 0)),
+            pl.BlockSpec((64 * 8, 128), lambda g: (0, 0)),
         ),
         scratch_shapes=[pltpu.VMEM((1, 128), f32)],
         compiler_params=params(),
@@ -558,10 +565,10 @@
     with jax.named_scope("signal"):
         signal_part = make_signal(users_side, channel)
         received = lax.all_to_all(signal_part, "row", 0, 0, tiled=True)
-        received, changes = lax.optimization_barrier((received, changes))
         signal, power = make_total(received)
+        power, changes = lax.optimization_barrier((power, changes))
         power = lax.all_to_all(power, ("row", "col"), 0, 0, tiled=True)
-        total_power = jnp.sum(power, axis=(0, 1))[:group_count] / (STREAMS * ANTENNAS)
+        total_power = jnp.sum(power, axis=0)[:group_count] / (8 * STREAMS * ANTENNAS)
         transmit = signal * lax.rsqrt(total_power + epsilon)[:, None, None]
         transmit = jnp.swapaxes(transmit, 0, 1)
 

time: 275 us -> 276 us (level)
  local copies, waits for them, and re-layouts: 17.6 us -> 12.2 us
  waiting for transfers between devices: 109 us -> 113 us
  Pallas kernels: 44.6 us -> 47.4 us
    unnamed x51 -> x31, local copies, waits for them, and re-layouts: 11.9 us -> 6.41 us
  transfers between devices with their start and end apart: 25 -> 25, of which waited for: 13 -> 13; matrix products, arithmetic and copies ran while one was open for 7% -> 7% of each run, Pallas kernels for 11% -> 12%
where the time goes in v1:
time: 276 us; the launch traced here: 275 us
  waiting for transfers between devices  113 us (41%)
  starting transfers between devices  57.8 us (21%)
  Pallas kernels  47.4 us (17%)
  other arithmetic  17.8 us (6%)
  between operations  14.5 us (5%)
  local copies, waits for them, and re-layouts  12.2 us (4%)
  blocking collectives  10.5 us (4%)
    all_to_all x2, waiting for transfers between devices, to_planes(): return lax.all_to_all(padded, 'col', 0, 0, tiled=True)  23.7 us
    all_to_all x1, waiting for transfers between devices, local(): received = lax.all_to_all(signal_part, 'row', 0, 0, tiled=True)  23.7 us
    ppermute x9, waiting for transfers between devices, along_x(): return lax.ppermute(value, 'row', pairs)  19.7 us
    all_to_all x1, waiting for transfers between devices, local(): both = lax.all_to_all(both, 'col', 0, 0, tiled=True)  14.2 us
    ppermute x9, starting transfers between devices, along_x(): return lax.ppermute(value, 'row', pairs)  14.1 us
    pallas_call x1, Pallas kernels, make_solve(): pl.pallas_call(solve_kernel, out_shape=(jax.ShapeDtypeStruct((EPOCHS, BLO...  13 us
    pallas_call x1, Pallas kernels, make_columns(): pl.pallas_call(columns_kernel, out_shape=jax.ShapeDtypeStruct((groups + 1...  10.7 us
    all_to_all x2, starting transfers between devices, to_planes(): return lax.all_to_all(padded, 'col', 0, 0, tiled=True)  10.6 us
  transfers between devices with their start and end apart: 25, of which 13 were waited for; matrix products, arithmetic and copies ran while one was open for 7% of the time, Pallas kernels for 12%

profile of v1, /device:TPU:0, one launch (start us, length us, event | category | flops | bytes accessed | tf_op | source)
XLA Modules:
  0.0 274.7 jit_solution(17763045895338095268)
XLA Ops:
  7.2 1.1 constant_dynamic-slice_fusion.1
  8.4 1.6 collective-permute-done
  10.0 1.0 select_bitcast_fusion.1
  11.3 0.9 pad.6
  12.2 1.9 copy-done.2
  14.4 3.2 %collective-permute-start.2 = (bf16[3,256,256]{2,1,0:T(8,128)(2,1)S(1)}, bf16[3,256,256]{2,1,0:T(8,128)(2,1)S(1)}, u32[]{:S(2)}, u32[]{:S(2)}) collective-permute-start(bf16[3,256,256]{2,1,0:T(8,128)(2,1)S(1)} %get-tuple-element.31), channel_id=1, source_target_pairs={{0,8},{4,12},{8,0},{12,4},{16,24},{20,28},{24,16},{28,20},{32,40},... | collective-permute-start | bytes 1179656 | tf_op jit(solution)/shard_map/planes/ppermute | solution.py:458
  17.5 1.1 collective-permute-start.3
  18.7 0.9 collective-permute-start.1
  19.6 1.6 fusion.20
  21.2 1.2 concatenate.10
  22.4 5.3 %all-to-all-start.1 = ((f32[4,256,256]{2,1,0:T(8,128)}), f32[4,256,256]{2,1,0:T(8,128)S(1)}, u32[]{:S(2)}, u32[]{:S(2)}) async-start(f32[4,256,256]{2,1,0:T(8,128)} %concatenate.10), calls=%async_computation.1 | async-start | bytes 2097152 | tf_op jit(solution)/shard_map/planes/all_to_all | solution.py:469
  27.7 1.0 collective-permute-done.2
  28.6 14.6 %collective-permute-done.3 = bf16[3,256,256]{2,1,0:T(8,128)(2,1)} collective-permute-done((bf16[3,256,256]{2,1,0:T(8,128)(2,1)S(1)}, bf16[3,256,256]{2,1,0:T(8,128)(2,1)}, u32[]{:S(2)}, u32[]{:S(2)}) %collective-permute-start.3) | collective-permute-done | bytes 393248 | tf_op jit(solution)/shard_map/planes/ppermute | solution.py:458
  43.2 2.5 fusion.6
  45.7 1.1 copy-done.9
  46.8 5.3 %all-to-all-start = ((bf16[4,4,256,256]{3,2,1,0:T(8,128)(2,1)}), bf16[4,4,256,256]{3,2,1,0:T(8,128)(2,1)S(1)}, u32[]{:S(2)}, u32[]{:S(2)}) async-start(bf16[4,4,256,256]{3,2,1,0:T(8,128)(2,1)} %fusion.6), calls=%async_computation | async-start | bytes 4194304 | tf_op jit(solution)/shard_map/planes/all_to_all | solution.py:469
  52.7 0.6 fusion.17.place_ref
  53.3 1.4 reduce_sum.58.precoded_ref
  54.7 23.7 %all-to-all-done.square_ref = bf16[4,4,256,256]{3,2,1,0:T(8,128)(2,1)S(1)} async-done(((bf16[4,4,256,256]{3,2,1,0:T(8,128)(2,1)}), bf16[4,4,256,256]{3,2,1,0:T(8,128)(2,1)S(1)}, u32[]{:S(2)}, u32[]{:S(2)}) %all-to-all-start) | async-done | bytes 2097184 | tf_op jit(solution)/shard_map/planes/all_to_all | solution.py:469
  78.4 7.7 %all-gather.5.cloned.1.call-done = bf16[1792,2048]{1,0:T(8,128)(2,1)} async-done(((bf16[112,2048]{1,0:T(8,128)(2,1)}), bf16[1792,2048]{1,0:T(8,128)(2,1)}) %all-gather.5.cloned.1.call-update) | async-done | bytes 7340048 | tf_op jit(solution)/shard_map/newcomers/all_gather | solution.py:486
  86.1 10.7 %columns.1 = bf16[4,304,384]{2,1,0:T(8,128)(2,1)} custom-call(s32[1]{0:T(128)} %bitcast.3.row_ref, bf16[16,112,2048]{2,1,0:T(8,128)(2,1)} %bitcast.73, bf16[3,256,2048]{2,1,0:T(8,128)(2,1)} %channel_ref.3, s32[3,1,384]{2,1,0:T(1,128)} %fusion.17.place_ref), custom_call_target="tpu_custom_call" | custom-call | flops 8000000000 | bytes 12000000 | tf_op jit(solution)/shard_map/columns/columns/pallas_call | solution.py:118
  96.8 4.4 %all-to-all-start.2 = ((bf16[4,304,384]{2,1,0:T(8,128)(2,1)}), bf16[4,304,384]{2,1,0:T(8,128)(2,1)}, u32[]{:S(2)}, u32[]{:S(2)}) async-start(bf16[4,304,384]{2,1,0:T(8,128)(2,1)} %columns.1), calls=%async_computation.2 | async-start | bytes 1867776 | tf_op jit(solution)/shard_map/columns/all_to_all | solution.py:527
  101.2 14.2 %all-to-all-done.2 = bf16[4,304,384]{2,1,0:T(8,128)(2,1)} async-done(((bf16[4,304,384]{2,1,0:T(8,128)(2,1)}), bf16[4,304,384]{2,1,0:T(8,128)(2,1)}, u32[]{:S(2)}, u32[]{:S(2)}) %all-to-all-start.2) | async-done | bytes 933920 | tf_op jit(solution)/shard_map/columns/all_to_all | solution.py:527
  115.4 1.4 convert_reduce_fusion.summed_ref
  116.7 1.4 collective-permute-start.4
  118.2 0.7 dynamic-slice_bitcast_fusion.1.place_ref
  118.9 2.7 collective-permute-start.5
  121.6 1.4 collective-permute-start.6
  123.0 1.2 collective-permute-start.7
  124.2 1.1 collective-permute-start.8
  125.3 3.9 %collective-permute-start.9 = (bf16[256,384]{1,0:T(8,128)(2,1)S(1)}, bf16[256,384]{1,0:T(8,128)(2,1)S(1)}, u32[]{:S(2)}, u32[]{:S(2)}) collective-permute-start(bf16[256,384]{1,0:T(8,128)(2,1)S(1)} %slice.74.own_ref), channel_id=1, source_target_pairs={{0,16},{4,20},{8,24},{12,28},{16,32},{20,36},{24,40},{28,44},{32,4... | collective-permute-start | bytes 589832 | tf_op jit(solution)/shard_map/columns/ppermute | solution.py:462
  129.3 1.0 target.1.base_ref
  130.3 2.2 collective-permute-done.8.col2_ref
  132.6 2.1 collective-permute-done.9.col3_ref
  134.6 3.5 %middle.1 = (f32[256,384]{1,0:T(8,128)S(1)}, bf16[256,384]{1,0:T(8,128)(2,1)}, bf16[256,384]{1,0:T(8,128)(2,1)}, bf16[256,384]{1,0:T(8,128)(2,1)S(1)}, bf16[384,640]{1,0:T(8,128)(2,1)}) custom-call(s32[3]{0:T(128)S(1)} %pad_add_fusion.where_ref, bf16[4,4,256,256]{3,2,1,0:T(8,128)(2,1)S(1)} %all-to-all-done.square_ref, bf16[256,384]{1,0:T(8,128)(2,1)S(1)} %slice.74.own_ref, ...), custom_call_target="tpu_custom_call" | custom-call | flops 2000000000 | bytes 8000000 | tf_op jit(solution)/shard_map/schur/middle/pallas_call | solution.py:227
  138.3 2.0 collective-permute-start.11
  140.3 1.2 collective-permute-start.12
  141.4 5.4 %all-to-all-start.3 = ((bf16[16,24,640]{2,1,0:T(8,128)(2,1)}), bf16[16,24,640]{2,1,0:T(8,128)(2,1)S(1)}, u32[]{:S(2)}, u32[]{:S(2)}) async-start(bf16[16,24,640]{2,1,0:T(8,128)(2,1)} %bitcast.13), calls=%async_computation.3 | async-start | bytes 983040 | tf_op jit(solution)/shard_map/schur/all_to_all | solution.py:542
  146.9 4.1 %collective-permute-done.12 = bf16[256,384]{1,0:T(8,128)(2,1)S(1)} collective-permute-done((bf16[256,384]{1,0:T(8,128)(2,1)S(1)}, bf16[256,384]{1,0:T(8,128)(2,1)S(1)}, u32[]{:S(2)}, u32[]{:S(2)}) %collective-permute-start.12) | collective-permute-done | bytes 196640 | tf_op jit(solution)/shard_map/schur/ppermute | solution.py:458
  151.1 0.8 fusion.19
  151.9 4.9 %all-to-all-done.3 = bf16[16,24,640]{2,1,0:T(8,128)(2,1)S(1)} async-done(((bf16[16,24,640]{2,1,0:T(8,128)(2,1)}), bf16[16,24,640]{2,1,0:T(8,128)(2,1)S(1)}, u32[]{:S(2)}, u32[]{:S(2)}) %all-to-all-start.3) | async-done | bytes 491552 | tf_op jit(solution)/shard_map/schur/all_to_all | solution.py:542
  157.0 1.0 broadcast_in_dim.10
  158.0 3.6 %all-to-all-start.4 = ((f32[16,24,640]{2,1,0:T(8,128)}), f32[16,24,640]{2,1,0:T(8,128)S(1)}, u32[]{:S(2)}, u32[]{:S(2)}) async-start(f32[16,24,640]{2,1,0:T(8,128)} %broadcast_in_dim.10), calls=%async_computation.4 | async-start | bytes 1966080 | tf_op jit(solution)/shard_map/schur/all_to_all | solution.py:551
  162.3 8.2 %channel.1.channel_ref = bf16[3,256,2048]{2,1,0:T(8,128)(2,1)} custom-call(s32[1]{0:T(128)} %bitcast.1.first_ref, bf16[16,112,2048]{2,1,0:T(8,128)(2,1)} %bitcast.74, bf16[3,256,2048]{2,1,0:T(8,128)(2,1)} %channel_ref.3, s32[3,1,384]{2,1,0:T(1,128)} %fusion.17.place_ref, s32[3,1,384]{2,1,0:T(1,128)} %reshape.276.slots_ref), custom_call_target="tpu_custom_call" | custom-call | flops 4000000000 | bytes 14000000 | tf_op jit(solution)/shard_map/users/channel/pallas_call | solution.py:150
  170.4 7.4 %all-to-all-done.4 = f32[16,24,640]{2,1,0:T(8,128)S(1)} async-done(((f32[16,24,640]{2,1,0:T(8,128)}), f32[16,24,640]{2,1,0:T(8,128)S(1)}, u32[]{:S(2)}, u32[]{:S(2)}) %all-to-all-start.4) | async-done | bytes 983072 | tf_op jit(solution)/shard_map/schur/all_to_all | solution.py:551
  177.8 13.0 %solve.1 = (f32[3,128,128]{2,1,0:T(8,128)S(1)}, bf16[4,256,256]{2,1,0:T(8,128)(2,1)S(1)}) custom-call(s32[1]{0:T(128)} %bitcast.1.first_ref, f32[384,640]{1,0:T(8,128)S(1)} %bitcast.61, f32[256,384]{1,0:T(8,128)S(1)} %get-tuple-element.57.weighted_ref, f32[256,256]{1,0:T(8,128)S(1)} %reduce_sum.58.precoded_ref, s32[1,384]{1,0:T(1,128)S(1)} %bitcast.66), custom_call_target="tpu_custom_call" | custom-call | flops 14000000000 | bytes 4000000 | tf_op jit(solution)/shard_map/users/solve/pallas_call | solution.py:304
  190.8 10.5 %all_to_all.44.users_ref = bf16[4,256,256]{2,1,0:T(8,128)(2,1)S(1)} all-to-all(bf16[4,256,256]{2,1,0:T(8,128)(2,1)S(1)} %get-tuple-element.42), channel_id=1, replica_groups=mesh['grp'=2,'row'=16,'col'=4] {'col'}, dimensions={0} | all-to-all | bytes 1048576 | tf_op jit(solution)/shard_map/users/all_to_all | solution.py:557
  201.3 2.2 signal.1
  203.5 4.5 %all-to-all-start.6 = ((bf16[16,3,16,2048]{3,2,1,0:T(8,128)(2,1)}), bf16[16,3,16,2048]{3,2,1,0:T(8,128)(2,1)}, u32[]{:S(2)}, u32[]{:S(2)}) async-start(bf16[16,3,16,2048]{3,2,1,0:T(8,128)(2,1)} %signal.1), calls=%async_computation.6 | async-start | bytes 6291456 | tf_op jit(solution)/shard_map/signal/all_to_all | solution.py:567
  208.3 1.9 copy-done.8
  210.2 5.6 %update.1 = (bf16[256,1024]{1,0:T(8,128)(2,1)S(1)}, bf16[256,1024]{1,0:T(8,128)(2,1)}, bf16[256,1024]{1,0:T(8,128)(2,1)}, bf16[256,1024]{1,0:T(8,128)(2,1)}) custom-call(s32[2]{0:T(128)S(1)} %pad_add_fusion.1.where_ref, f32[256,384]{1,0:T(8,128)S(1)} %get-tuple-element.57.weighted_ref, f32[384,640]{1,0:T(8,128)S(1)} %bitcast.62, ...), custom_call_target="tpu_custom_call" | custom-call | flops 1500000000 | bytes 8000000 | tf_op jit(solution)/shard_map/update/update/pallas_call | solution.py:430
  215.8 0.8 copy-done.6
  217.2 2.1 collective-permute-start.14
  219.3 0.8 collective-permute-start.15
  220.4 2.1 and_select_fusion
  222.5 23.7 %all-to-all-done.6.received_ref = bf16[16,3,16,2048]{3,2,1,0:T(8,128)(2,1)} async-done(((bf16[16,3,16,2048]{3,2,1,0:T(8,128)(2,1)}), bf16[16,3,16,2048]{3,2,1,0:T(8,128)(2,1)}, u32[]{:S(2)}, u32[]{:S(2)}) %all-to-all-start.6) | async-done | bytes 3145760 | tf_op jit(solution)/shard_map/signal/all_to_all | solution.py:567
  246.2 3.2 %total.1 = (f32[3,16,2048]{2,1,0:T(8,128)S(1)}, f32[512,128]{1,0:T(8,128)S(1)}) custom-call(bf16[16,3,16,2048]{3,2,1,0:T(8,128)(2,1)} %all-to-all-done.6.received_ref), custom_call_target="tpu_custom_call" | custom-call | flops 2000000000 | bytes 4000000 | tf_op jit(solution)/shard_map/signal/total/pallas_call | solution.py:387
  249.4 0.7 copy-done.7
  250.1 5.5 %all-to-all-start.7 = ((f32[64,8,128]{2,1,0:T(8,128)}), f32[64,8,128]{2,1,0:T(8,128)}, u32[]{:S(2)}, u32[]{:S(2)}) async-start(f32[64,8,128]{2,1,0:T(8,128)} %bitcast.64), calls=%async_computation.7 | async-start | bytes 524288 | tf_op jit(solution)/shard_map/signal/all_to_all | solution.py:570
  255.6 3.0 %fusion.15 = (f32[1,256,1024]{2,1,0:T(8,128)S(1)}, f32[1,256,1024]{2,1,0:T(8,128)S(1)}, f32[1,256,1024]{2,1,0:T(8,128)S(1)}) fusion(f32[3,256,1024]{2,1,0:T(8,128)} %and_select_fusion, f32[3,256,1024]{2,1,0:T(8,128)S(1)} %copy-done.4, bf16[256,1024]{1,0:T(8,128)(2,1)} %collective-permute-done.15, bf16[256,1024]{1,0:T(8,128)(2,1)} %collective-permute-done.14, ...), kind=kLoop, calls=%fused_computation.23 | loop fusion | flops 4718592 | bytes 11534345 | tf_op jit(solution)/shard_map/final/stack | solution.py:587
  258.6 1.9 pad_maximum_fusion
  260.4 5.5 %all-to-all-done.7 = f32[64,8,128]{2,1,0:T(8,128)} async-done(((f32[64,8,128]{2,1,0:T(8,128)}), f32[64,8,128]{2,1,0:T(8,128)}, u32[]{:S(2)}, u32[]{:S(2)}) %all-to-all-start.7) | async-done | bytes 262176 | tf_op jit(solution)/shard_map/signal/all_to_all | solution.py:570
  265.9 1.0 reduce_sum.65
  267.0 0.8 multiply_bitcast_fusion
  (74 shorter events, 3.7 us)
Async XLA Ops:
  7.2 12.4 %copy-start = (bf16[3,1024,256]{2,1,0:T(8,128)(2,1)S(1)}, bf16[3,1024,256]{2,1,0:T(8,128)(2,1)}, u32[]{:S(2)}) copy-start(bf16[3,1024,256]{2,1,0:T(8,128)(2,1)} %param.13) | copy-start | bytes 4718596
  7.2 78.9 %all-gather.5.cloned.1.call-start = ((), (), s32[]{:S(2)}) async-start(), calls=%async_computation.8 | async-start | bytes 7798784 | tf_op jit(solution)/shard_map/newcomers/all_gather | solution.py:486
  8.3 1.7 collective-permute-start
  12.2 1.9 copy-start.2
  14.1 5.4 %copy-start.3 = (f32[3,256,1024]{2,1,0:T(8,128)S(1)}, f32[3,256,1024]{2,1,0:T(8,128)}, u32[]{:S(2)}) copy-start(f32[3,256,1024]{2,1,0:T(8,128)} %inverse_ref.1) | copy-start | bytes 9437188
  14.4 14.3 %collective-permute-start.2 = (bf16[3,256,256]{2,1,0:T(8,128)(2,1)S(1)}, bf16[3,256,256]{2,1,0:T(8,128)(2,1)S(1)}, u32[]{:S(2)}, u32[]{:S(2)}) collective-permute-start(bf16[3,256,256]{2,1,0:T(8,128)(2,1)S(1)} %get-tuple-element.31), channel_id=1, source_target_pairs={{0,8},{4,12},{8,0},{12,4},{16,24},{20,28},{24,16},{28,20},{32,40},... | collective-permute-start | bytes 1179656 | tf_op jit(solution)/shard_map/planes/ppermute | solution.py:458
  17.5 25.7 %collective-permute-start.3 = (bf16[3,256,256]{2,1,0:T(8,128)(2,1)S(1)}, bf16[3,256,256]{2,1,0:T(8,128)(2,1)}, u32[]{:S(2)}, u32[]{:S(2)}) collective-permute-start(bf16[3,256,256]{2,1,0:T(8,128)(2,1)S(1)} %get-tuple-element.32), channel_id=1, source_target_pairs={{0,12},{4,0},{8,4},{12,8},{16,28},{20,16},{24,20},{28,24},{32,44},... | collective-permute-start | bytes 1179656 | tf_op jit(solution)/shard_map/planes/ppermute | solution.py:458
  18.7 24.5 %collective-permute-start.1 = (bf16[3,256,256]{2,1,0:T(8,128)(2,1)S(1)}, bf16[3,256,256]{2,1,0:T(8,128)(2,1)}, u32[]{:S(2)}, u32[]{:S(2)}) collective-permute-start(bf16[3,256,256]{2,1,0:T(8,128)(2,1)S(1)} %get-tuple-element.30), channel_id=1, source_target_pairs={{0,4},{4,8},{8,12},{12,0},{16,20},{20,24},{24,28},{28,16},{32,36},... | collective-permute-start | bytes 1179656 | tf_op jit(solution)/shard_map/planes/ppermute | solution.py:458
  22.4 23.3 %all-to-all-start.1 = ((f32[4,256,256]{2,1,0:T(8,128)}), f32[4,256,256]{2,1,0:T(8,128)S(1)}, u32[]{:S(2)}, u32[]{:S(2)}) async-start(f32[4,256,256]{2,1,0:T(8,128)} %concatenate.10), calls=%async_computation.1 | async-start | bytes 2097152 | tf_op jit(solution)/shard_map/planes/all_to_all | solution.py:469
  43.2 8.8 %copy-start.11 = (s32[6,3,128,1]{2,3,1,0:T(1,128)S(1)}, s32[6,3,128,1]{2,3,1,0:T(1,128)}, u32[]{:S(2)}) copy-start(s32[6,3,128,1]{2,3,1,0:T(1,128)} %param.10) | copy-start | bytes 27652
  43.2 9.1 %copy-start.12 = (s32[32]{0:T(128)S(1)}, s32[32]{0:T(128)}, u32[]{:S(2)}) copy-start(s32[32]{0:T(128)} %param.11) | copy-start | bytes 388
  45.7 1.1 copy-start.9
  46.8 31.7 %all-to-all-start = ((bf16[4,4,256,256]{3,2,1,0:T(8,128)(2,1)}), bf16[4,4,256,256]{3,2,1,0:T(8,128)(2,1)S(1)}, u32[]{:S(2)}, u32[]{:S(2)}) async-start(bf16[4,4,256,256]{3,2,1,0:T(8,128)(2,1)} %fusion.6), calls=%async_computation | async-start | bytes 4194304 | tf_op jit(solution)/shard_map/planes/all_to_all | solution.py:469
  96.8 21.4 %copy-start.10 = (s32[6,3,128]{2,1,0:T(4,128)S(1)}, s32[6,3,128]{2,1,0:T(4,128)}, u32[]{:S(2)}) copy-start(s32[6,3,128]{2,1,0:T(4,128)} %param.12) | copy-start | bytes 27652
  96.8 18.5 %all-to-all-start.2 = ((bf16[4,304,384]{2,1,0:T(8,128)(2,1)}), bf16[4,304,384]{2,1,0:T(8,128)(2,1)}, u32[]{:S(2)}, u32[]{:S(2)}) async-start(bf16[4,304,384]{2,1,0:T(8,128)(2,1)} %columns.1), calls=%async_computation.2 | async-start | bytes 1867776 | tf_op jit(solution)/shard_map/columns/all_to_all | solution.py:527
  116.7 8.6 %collective-permute-start.4 = (bf16[256,384]{1,0:T(8,128)(2,1)S(1)}, bf16[256,384]{1,0:T(8,128)(2,1)S(1)}, u32[]{:S(2)}, u32[]{:S(2)}) collective-permute-start(bf16[256,384]{1,0:T(8,128)(2,1)S(1)} %slice.74.own_ref), channel_id=1, source_target_pairs={{0,4},{4,8},{8,12},{12,0},{16,20},{20,24},{24,28},{28,16},{32,36},... | collective-permute-start | bytes 589832 | tf_op jit(solution)/shard_map/columns/ppermute | solution.py:458
  118.9 11.4 %collective-permute-start.5 = (bf16[256,384]{1,0:T(8,128)(2,1)S(1)}, bf16[256,384]{1,0:T(8,128)(2,1)S(1)}, u32[]{:S(2)}, u32[]{:S(2)}) collective-permute-start(bf16[256,384]{1,0:T(8,128)(2,1)S(1)} %slice.74.own_ref), channel_id=1, source_target_pairs={{0,8},{4,12},{8,0},{12,4},{16,24},{20,28},{24,16},{28,20},{32,40},... | collective-permute-start | bytes 589832 | tf_op jit(solution)/shard_map/columns/ppermute | solution.py:458
  121.6 8.7 %collective-permute-start.6 = (bf16[256,384]{1,0:T(8,128)(2,1)S(1)}, bf16[256,384]{1,0:T(8,128)(2,1)S(1)}, u32[]{:S(2)}, u32[]{:S(2)}) collective-permute-start(bf16[256,384]{1,0:T(8,128)(2,1)S(1)} %slice.74.own_ref), channel_id=1, source_target_pairs={{0,12},{4,0},{8,4},{12,8},{16,28},{20,16},{24,20},{28,24},{32,44},... | collective-permute-start | bytes 589832 | tf_op jit(solution)/shard_map/columns/ppermute | solution.py:458
  123.0 7.3 %collective-permute-start.7 = (bf16[256,384]{1,0:T(8,128)(2,1)S(1)}, bf16[256,384]{1,0:T(8,128)(2,1)S(1)}, u32[]{:S(2)}, u32[]{:S(2)}) collective-permute-start(bf16[256,384]{1,0:T(8,128)(2,1)S(1)} %slice.74.own_ref), channel_id=1, source_target_pairs={{0,48},{4,52},{8,56},{12,60},{16,0},{20,4},{24,8},{28,12},{32,16},... | collective-permute-start | bytes 589832 | tf_op jit(solution)/shard_map/columns/ppermute | solution.py:462
  124.2 8.3 %collective-permute-start.8 = (bf16[256,384]{1,0:T(8,128)(2,1)S(1)}, bf16[256,384]{1,0:T(8,128)(2,1)S(1)}, u32[]{:S(2)}, u32[]{:S(2)}) collective-permute-start(bf16[256,384]{1,0:T(8,128)(2,1)S(1)} %slice.74.own_ref), channel_id=1, source_target_pairs={{0,32},{4,36},{8,40},{12,44},{16,48},{20,52},{24,56},{28,60},{32,0... | collective-permute-start | bytes 589832 | tf_op jit(solution)/shard_map/columns/ppermute | solution.py:462
  125.3 9.3 %collective-permute-start.9 = (bf16[256,384]{1,0:T(8,128)(2,1)S(1)}, bf16[256,384]{1,0:T(8,128)(2,1)S(1)}, u32[]{:S(2)}, u32[]{:S(2)}) collective-permute-start(bf16[256,384]{1,0:T(8,128)(2,1)S(1)} %slice.74.own_ref), channel_id=1, source_target_pairs={{0,16},{4,20},{8,24},{12,28},{16,32},{20,36},{24,40},{28,44},{32,4... | collective-permute-start | bytes 589832 | tf_op jit(solution)/shard_map/columns/ppermute | solution.py:462
  138.1 8.8 %collective-permute-start.10 = (bf16[256,384]{1,0:T(8,128)(2,1)}, bf16[256,384]{1,0:T(8,128)(2,1)S(1)}, u32[]{:S(2)}, u32[]{:S(2)}) collective-permute-start(bf16[256,384]{1,0:T(8,128)(2,1)} %get-tuple-element.39), channel_id=1, source_target_pairs={{0,12},{4,0},{8,4},{12,8},{16,28},{20,16},{24,20},{28,24},{32,44},... | collective-permute-start | bytes 589832 | tf_op jit(solution)/shard_map/schur/ppermute | solution.py:458
  138.3 8.6 %collective-permute-start.11 = (bf16[256,384]{1,0:T(8,128)(2,1)}, bf16[256,384]{1,0:T(8,128)(2,1)S(1)}, u32[]{:S(2)}, u32[]{:S(2)}) collective-permute-start(bf16[256,384]{1,0:T(8,128)(2,1)} %get-tuple-element.40), channel_id=1, source_target_pairs={{0,8},{4,12},{8,0},{12,4},{16,24},{20,28},{24,16},{28,20},{32,40},... | collective-permute-start | bytes 589832 | tf_op jit(solution)/shard_map/schur/ppermute | solution.py:458
  140.3 10.8 %collective-permute-start.12 = (bf16[256,384]{1,0:T(8,128)(2,1)S(1)}, bf16[256,384]{1,0:T(8,128)(2,1)S(1)}, u32[]{:S(2)}, u32[]{:S(2)}) collective-permute-start(bf16[256,384]{1,0:T(8,128)(2,1)S(1)} %get-tuple-element.41), channel_id=1, source_target_pairs={{0,4},{4,8},{8,12},{12,0},{16,20},{20,24},{24,28},{28,16},{32,36},... | collective-permute-start | bytes 589832 | tf_op jit(solution)/shard_map/schur/ppermute | solution.py:458
  141.4 15.4 %all-to-all-start.3 = ((bf16[16,24,640]{2,1,0:T(8,128)(2,1)}), bf16[16,24,640]{2,1,0:T(8,128)(2,1)S(1)}, u32[]{:S(2)}, u32[]{:S(2)}) async-start(bf16[16,24,640]{2,1,0:T(8,128)(2,1)} %bitcast.13), calls=%async_computation.3 | async-start | bytes 983040 | tf_op jit(solution)/shard_map/schur/all_to_all | solution.py:542
  146.8 61.5 %all-gather.7.cloned.1.call-start = ((), (), s32[]{:S(2)}) async-start(), calls=%async_computation.9 | async-start | bytes 3342336 | tf_op jit(solution)/shard_map/schur/all_gather | solution.py:540
  158.0 19.8 %all-to-all-start.4 = ((f32[16,24,640]{2,1,0:T(8,128)}), f32[16,24,640]{2,1,0:T(8,128)S(1)}, u32[]{:S(2)}, u32[]{:S(2)}) async-start(f32[16,24,640]{2,1,0:T(8,128)} %broadcast_in_dim.10), calls=%async_computation.4 | async-start | bytes 1966080 | tf_op jit(solution)/shard_map/schur/all_to_all | solution.py:551
  177.8 23.5 %copy-start.5 = (bf16[3,256,2048]{2,1,0:T(8,128)(2,1)S(1)}, bf16[3,256,2048]{2,1,0:T(8,128)(2,1)}, u32[]{:S(2)}) copy-start(bf16[3,256,2048]{2,1,0:T(8,128)(2,1)} %channel.1.channel_ref) | copy-start | bytes 9437188
  203.5 42.7 %all-to-all-start.6 = ((bf16[16,3,16,2048]{3,2,1,0:T(8,128)(2,1)}), bf16[16,3,16,2048]{3,2,1,0:T(8,128)(2,1)}, u32[]{:S(2)}, u32[]{:S(2)}) async-start(bf16[16,3,16,2048]{3,2,1,0:T(8,128)(2,1)} %signal.1), calls=%async_computation.6 | async-start | bytes 6291456 | tf_op jit(solution)/shard_map/signal/all_to_all | solution.py:567
  208.3 1.9 copy-start.8
  215.8 0.8 copy-start.6
  216.7 32.7 %collective-permute-start.13 = (bf16[256,1024]{1,0:T(8,128)(2,1)}, bf16[256,1024]{1,0:T(8,128)(2,1)}, u32[]{:S(2)}, u32[]{:S(2)}) collective-permute-start(bf16[256,1024]{1,0:T(8,128)(2,1)} %get-tuple-element.47), channel_id=1, source_target_pairs={{0,1},{1,2},{2,3},{3,0},{4,5},{5,6},{6,7},{7,4},{8,9},{9,10},{10,1... | collective-permute-start | bytes 1572872 | tf_op jit(solution)/shard_map/update/ppermute | solution.py:465
  217.2 32.2 %collective-permute-start.14 = (bf16[256,1024]{1,0:T(8,128)(2,1)}, bf16[256,1024]{1,0:T(8,128)(2,1)}, u32[]{:S(2)}, u32[]{:S(2)}) collective-permute-start(bf16[256,1024]{1,0:T(8,128)(2,1)} %get-tuple-element.48), channel_id=1, source_target_pairs={{0,2},{1,3},{2,0},{3,1},{4,6},{5,7},{6,4},{7,5},{8,10},{9,11},{10,... | collective-permute-start | bytes 1572872 | tf_op jit(solution)/shard_map/update/ppermute | solution.py:465
  219.3 30.1 %collective-permute-start.15 = (bf16[256,1024]{1,0:T(8,128)(2,1)}, bf16[256,1024]{1,0:T(8,128)(2,1)}, u32[]{:S(2)}, u32[]{:S(2)}) collective-permute-start(bf16[256,1024]{1,0:T(8,128)(2,1)} %get-tuple-element.49), channel_id=1, source_target_pairs={{0,3},{1,0},{2,1},{3,2},{4,7},{5,4},{6,5},{7,6},{8,11},{9,8},{10,9... | collective-permute-start | bytes 1572872 | tf_op jit(solution)/shard_map/update/ppermute | solution.py:465
  222.5 33.0 %copy-start.4 = (f32[3,256,1024]{2,1,0:T(8,128)S(1)}, f32[3,256,1024]{2,1,0:T(8,128)}, u32[]{:S(2)}) copy-start(f32[3,256,1024]{2,1,0:T(8,128)} %inverse_ref.1) | copy-start | bytes 9437188
  249.4 0.7 copy-start.7
  250.1 15.9 %all-to-all-start.7 = ((f32[64,8,128]{2,1,0:T(8,128)}), f32[64,8,128]{2,1,0:T(8,128)}, u32[]{:S(2)}, u32[]{:S(2)}) async-start(f32[64,8,128]{2,1,0:T(8,128)} %bitcast.64), calls=%async_computation.7 | async-start | bytes 524288 | tf_op jit(solution)/shard_map/signal/all_to_all | solution.py:570
  258.5 9.3 %copy-start.1 = (bf16[3,1024,256]{2,1,0:T(8,128)(2,1)S(1)}, bf16[3,1024,256]{2,1,0:T(8,128)(2,1)}, u32[]{:S(2)}) copy-start(bf16[3,1024,256]{2,1,0:T(8,128)(2,1)} %param.13) | copy-start | bytes 4718596
Sparse Core Ops, SparseCore 0:
  12.3 73.7 all-gather.4
  152.0 50.4 all-gather.6

commit v2 on v0

--- a/solution.py
+++ b/solution.py
@@ -357,45 +357,6 @@
     )(users_side, channel)
 
 
-def total_kernel(received_ref, signal_ref, power_ref, sums_ref):
-    g = pl.program_id(0)
-    signal = jnp.sum(received_ref[:, 0].astype(f32), axis=0)
-    signal_ref[0] = signal
-    power = jnp.sum(signal * signal)
-    lane = lax.broadcasted_iota(jnp.int32, sums_ref.shape, 1)
-
-    @pl.when(g == 0)
-    def _():
-        sums_ref[...] = jnp.zeros(sums_ref.shape, f32)
-
-    sums_ref[...] = jnp.where(lane == g, power, sums_ref[...])
-
-    @pl.when(g == pl.num_programs(0) - 1)
-    def _():
-        power_ref[...] = jnp.broadcast_to(sums_ref[...][None], power_ref.shape)
-
-
-def make_total(received):
-    sources, groups, each, antennas = received.shape
-    return pl.pallas_call(
-        total_kernel,
-        out_shape=(
-            jax.ShapeDtypeStruct((groups, each, antennas), f32),
-            jax.ShapeDtypeStruct((64, 1, 128), f32),
-        ),
-        grid=(groups,),
-        in_specs=[pl.BlockSpec((sources, 1, each, antennas), lambda g: (0, g, 0, 0))],
-        out_specs=(
-            pl.BlockSpec((1, each, antennas), lambda g: (g, 0, 0)),
-            pl.BlockSpec((64, 1, 128), lambda g: (0, 0, 0)),
-        ),
-        scratch_shapes=[pltpu.VMEM((1, 128), f32)],
-        compiler_params=params(),
-        cost_estimate=cost(2_000_000_000, 4_000_000),
-        name="total",
-    )(received)
-
-
 def update_kernel(
     where_ref, weighted_ref, whole_ref, pivots_ref, all_ref, slots_ref,
     out0, out1, out2, out3, inv_ref, held_ref, sems,
@@ -558,10 +519,12 @@
     with jax.named_scope("signal"):
         signal_part = make_signal(users_side, channel)
         received = lax.all_to_all(signal_part, "row", 0, 0, tiled=True)
-        received, changes = lax.optimization_barrier((received, changes))
-        signal, power = make_total(received)
+        signal = jnp.sum(received.astype(f32), axis=0)
+        power = jnp.sum(signal * signal, axis=(1, 2))
+        power, changes = lax.optimization_barrier((power, changes))
+        power = jnp.broadcast_to(power[None, None, :], (64, 1, group_count))
         power = lax.all_to_all(power, ("row", "col"), 0, 0, tiled=True)
-        total_power = jnp.sum(power, axis=(0, 1))[:group_count] / (STREAMS * ANTENNAS)
+        total_power = jnp.sum(power, axis=(0, 1)) / (STREAMS * ANTENNAS)
         transmit = signal * lax.rsqrt(total_power + epsilon)[:, None, None]
         transmit = jnp.swapaxes(transmit, 0, 1)
 

time: 275 us -> 273 us (level)
  local copies, waits for them, and re-layouts: 17.6 us -> 10.2 us
  waiting for transfers between devices: 109 us -> 113 us
    unnamed x51 -> x27, local copies, waits for them, and re-layouts: 11.9 us -> 3.84 us
    all_to_all x1, waiting for transfers between devices: 21.1 us -> 24.5 us  [local(): received = lax.all_to_all(signal_part, 'row', 0, 0, tiled=True)]
  transfers between devices with their start and end apart: 25 -> 25, of which waited for: 13 -> 13; matrix products, arithmetic and copies ran while one was open for 7% -> 8% of each run, Pallas kernels for 11% -> 11%
where the time goes in v2:
time: 273 us; the launch traced here: 272 us
  waiting for transfers between devices  113 us (41%)
  starting transfers between devices  58 us (21%)
  Pallas kernels  43.3 us (16%)
  other arithmetic  20.5 us (8%)
  between operations  14.4 us (5%)
  blocking collectives  10.5 us (4%)
  local copies, waits for them, and re-layouts  10.2 us (4%)
    all_to_all x1, waiting for transfers between devices, local(): received = lax.all_to_all(signal_part, 'row', 0, 0, tiled=True)  24.5 us
    all_to_all x2, waiting for transfers between devices, to_planes(): return lax.all_to_all(padded, 'col', 0, 0, tiled=True)  23.5 us
    ppermute x9, waiting for transfers between devices, along_x(): return lax.ppermute(value, 'row', pairs)  19.6 us
    ppermute x9, starting transfers between devices, along_x(): return lax.ppermute(value, 'row', pairs)  14.1 us
    all_to_all x1, waiting for transfers between devices, local(): both = lax.all_to_all(both, 'col', 0, 0, tiled=True)  14 us
    pallas_call x1, Pallas kernels, make_solve(): pl.pallas_call(solve_kernel, out_shape=(jax.ShapeDtypeStruct((EPOCHS, BLO...  13 us
    all_to_all x2, starting transfers between devices, to_planes(): return lax.all_to_all(padded, 'col', 0, 0, tiled=True)  10.6 us
    all_to_all x1, blocking collectives, local(): users_side = lax.all_to_all(users, 'col', 0, 0, tiled=True)  10.5 us
  transfers between devices with their start and end apart: 25, of which 13 were waited for; matrix products, arithmetic and copies ran while one was open for 8% of the time, Pallas kernels for 11%

profile of v2, /device:TPU:0, one launch (start us, length us, event | category | flops | bytes accessed | tf_op | source)
XLA Modules:
  0.0 271.5 jit_solution(14033760548761163460)
XLA Ops:
  7.2 1.1 constant_dynamic-slice_fusion.1
  8.4 1.6 collective-permute-done
  10.0 1.0 select_bitcast_fusion.1
  11.3 0.8 pad.6
  12.2 1.9 copy-done.2
  14.3 3.2 %collective-permute-start.2 = (bf16[3,256,256]{2,1,0:T(8,128)(2,1)S(1)}, bf16[3,256,256]{2,1,0:T(8,128)(2,1)S(1)}, u32[]{:S(2)}, u32[]{:S(2)}) collective-permute-start(bf16[3,256,256]{2,1,0:T(8,128)(2,1)S(1)} %get-tuple-element.29), channel_id=1, source_target_pairs={{0,8},{4,12},{8,0},{12,4},{16,24},{20,28},{24,16},{28,20},{32,40},... | collective-permute-start | bytes 1179656 | tf_op jit(solution)/shard_map/planes/ppermute | solution.py:412
  17.5 1.1 collective-permute-start.3
  18.6 0.9 collective-permute-start.1
  19.5 1.6 fusion.20
  21.2 1.1 concatenate.10
  22.3 5.3 %all-to-all-start.1 = ((f32[4,256,256]{2,1,0:T(8,128)}), f32[4,256,256]{2,1,0:T(8,128)}, u32[]{:S(2)}, u32[]{:S(2)}) async-start(f32[4,256,256]{2,1,0:T(8,128)} %concatenate.10), calls=%async_computation.1 | async-start | bytes 2097152 | tf_op jit(solution)/shard_map/planes/all_to_all | solution.py:423
  27.6 1.0 collective-permute-done.2
  28.6 14.6 %collective-permute-done.3 = bf16[3,256,256]{2,1,0:T(8,128)(2,1)} collective-permute-done((bf16[3,256,256]{2,1,0:T(8,128)(2,1)S(1)}, bf16[3,256,256]{2,1,0:T(8,128)(2,1)}, u32[]{:S(2)}, u32[]{:S(2)}) %collective-permute-start.3) | collective-permute-done | bytes 393248 | tf_op jit(solution)/shard_map/planes/ppermute | solution.py:412
  43.2 2.5 fusion.6
  45.6 5.3 %all-to-all-start = ((bf16[4,4,256,256]{3,2,1,0:T(8,128)(2,1)}), bf16[4,4,256,256]{3,2,1,0:T(8,128)(2,1)S(1)}, u32[]{:S(2)}, u32[]{:S(2)}) async-start(bf16[4,4,256,256]{3,2,1,0:T(8,128)(2,1)} %fusion.6), calls=%async_computation | async-start | bytes 4194304 | tf_op jit(solution)/shard_map/planes/all_to_all | solution.py:423
  51.6 0.6 fusion.17.place_ref
  52.2 1.6 reduce_sum.76.precoded_ref
  53.8 23.5 %all-to-all-done.square_ref = bf16[4,4,256,256]{3,2,1,0:T(8,128)(2,1)S(1)} async-done(((bf16[4,4,256,256]{3,2,1,0:T(8,128)(2,1)}), bf16[4,4,256,256]{3,2,1,0:T(8,128)(2,1)S(1)}, u32[]{:S(2)}, u32[]{:S(2)}) %all-to-all-start) | async-done | bytes 2097184 | tf_op jit(solution)/shard_map/planes/all_to_all | solution.py:423
  77.3 8.7 %all-gather.5.cloned.1.call-done = bf16[1792,2048]{1,0:T(8,128)(2,1)} async-done(((bf16[112,2048]{1,0:T(8,128)(2,1)}), bf16[1792,2048]{1,0:T(8,128)(2,1)}) %all-gather.5.cloned.1.call-update) | async-done | bytes 7340048 | tf_op jit(solution)/shard_map/newcomers/all_gather | solution.py:440
  86.0 9.7 %columns.1 = bf16[4,304,384]{2,1,0:T(8,128)(2,1)} custom-call(s32[1]{0:T(128)} %bitcast.3.row_ref, bf16[16,112,2048]{2,1,0:T(8,128)(2,1)} %bitcast.71, bf16[3,256,2048]{2,1,0:T(8,128)(2,1)} %channel_ref.3, s32[3,1,384]{2,1,0:T(1,128)} %fusion.17.place_ref), custom_call_target="tpu_custom_call" | custom-call | flops 4000000000 | bytes 12000000 | tf_op jit(solution)/shard_map/columns/columns/pallas_call | solution.py:115
  95.7 4.4 %all-to-all-start.2 = ((bf16[4,304,384]{2,1,0:T(8,128)(2,1)}), bf16[4,304,384]{2,1,0:T(8,128)(2,1)}, u32[]{:S(2)}, u32[]{:S(2)}) async-start(bf16[4,304,384]{2,1,0:T(8,128)(2,1)} %columns.1), calls=%async_computation.2 | async-start | bytes 1867776 | tf_op jit(solution)/shard_map/columns/all_to_all | solution.py:481
  100.2 14.0 %all-to-all-done.2 = bf16[4,304,384]{2,1,0:T(8,128)(2,1)} async-done(((bf16[4,304,384]{2,1,0:T(8,128)(2,1)}), bf16[4,304,384]{2,1,0:T(8,128)(2,1)}, u32[]{:S(2)}, u32[]{:S(2)}) %all-to-all-start.2) | async-done | bytes 933920 | tf_op jit(solution)/shard_map/columns/all_to_all | solution.py:481
  114.2 1.4 convert_reduce_fusion.1.summed_ref
  115.6 1.6 collective-permute-start.4
  117.2 0.7 dynamic-slice_bitcast_fusion.1.place_ref
  117.8 2.7 collective-permute-start.5
  120.5 1.4 collective-permute-start.6
  121.9 1.2 collective-permute-start.7
  123.2 1.1 collective-permute-start.8
  124.3 3.8 %collective-permute-start.9 = (bf16[256,384]{1,0:T(8,128)(2,1)S(1)}, bf16[256,384]{1,0:T(8,128)(2,1)S(1)}, u32[]{:S(2)}, u32[]{:S(2)}) collective-permute-start(bf16[256,384]{1,0:T(8,128)(2,1)S(1)} %slice.69.own_ref), channel_id=1, source_target_pairs={{0,16},{4,20},{8,24},{12,28},{16,32},{20,36},{24,40},{28,44},{32,4... | collective-permute-start | bytes 589832 | tf_op jit(solution)/shard_map/columns/ppermute | solution.py:416
  128.1 1.0 target.1.base_ref
  129.1 2.3 collective-permute-done.8.col2_ref
  131.5 2.1 collective-permute-done.9.col3_ref
  133.5 3.5 %middle.1 = (f32[256,384]{1,0:T(8,128)S(1)}, bf16[256,384]{1,0:T(8,128)(2,1)}, bf16[256,384]{1,0:T(8,128)(2,1)}, bf16[256,384]{1,0:T(8,128)(2,1)S(1)}, bf16[384,640]{1,0:T(8,128)(2,1)}) custom-call(s32[3]{0:T(128)S(1)} %pad_add_fusion.where_ref, bf16[4,4,256,256]{3,2,1,0:T(8,128)(2,1)S(1)} %all-to-all-done.square_ref, bf16[256,384]{1,0:T(8,128)(2,1)S(1)} %slice.69.own_ref, ...), custom_call_target="tpu_custom_call" | custom-call | flops 2000000000 | bytes 8000000 | tf_op jit(solution)/shard_map/schur/middle/pallas_call | solution.py:220
  137.1 2.0 collective-permute-start.11
  139.1 1.1 collective-permute-start.12
  140.3 5.4 %all-to-all-start.3 = ((bf16[16,24,640]{2,1,0:T(8,128)(2,1)}), bf16[16,24,640]{2,1,0:T(8,128)(2,1)S(1)}, u32[]{:S(2)}, u32[]{:S(2)}) async-start(bf16[16,24,640]{2,1,0:T(8,128)(2,1)} %bitcast.13), calls=%async_computation.3 | async-start | bytes 983040 | tf_op jit(solution)/shard_map/schur/all_to_all | solution.py:496
  145.8 4.0 %collective-permute-done.12 = bf16[256,384]{1,0:T(8,128)(2,1)S(1)} collective-permute-done((bf16[256,384]{1,0:T(8,128)(2,1)S(1)}, bf16[256,384]{1,0:T(8,128)(2,1)S(1)}, u32[]{:S(2)}, u32[]{:S(2)}) %collective-permute-start.12) | collective-permute-done | bytes 196640 | tf_op jit(solution)/shard_map/schur/ppermute | solution.py:412
  149.9 0.8 fusion.19
  150.7 5.0 %all-to-all-done.3 = bf16[16,24,640]{2,1,0:T(8,128)(2,1)S(1)} async-done(((bf16[16,24,640]{2,1,0:T(8,128)(2,1)}), bf16[16,24,640]{2,1,0:T(8,128)(2,1)S(1)}, u32[]{:S(2)}, u32[]{:S(2)}) %all-to-all-start.3) | async-done | bytes 491552 | tf_op jit(solution)/shard_map/schur/all_to_all | solution.py:496
  155.9 1.0 broadcast_in_dim.12
  156.9 3.6 %all-to-all-start.4 = ((f32[16,24,640]{2,1,0:T(8,128)}), f32[16,24,640]{2,1,0:T(8,128)S(1)}, u32[]{:S(2)}, u32[]{:S(2)}) async-start(f32[16,24,640]{2,1,0:T(8,128)} %broadcast_in_dim.12), calls=%async_computation.4 | async-start | bytes 1966080 | tf_op jit(solution)/shard_map/schur/all_to_all | solution.py:505
  160.6 0.6 reshape.281.slots_ref
  161.2 8.2 %channel.1.channel_ref = bf16[3,256,2048]{2,1,0:T(8,128)(2,1)} custom-call(s32[1]{0:T(128)} %bitcast.1.first_ref, bf16[16,112,2048]{2,1,0:T(8,128)(2,1)} %bitcast.72, bf16[3,256,2048]{2,1,0:T(8,128)(2,1)} %channel_ref.3, s32[3,1,384]{2,1,0:T(1,128)} %fusion.17.place_ref, s32[3,1,384]{2,1,0:T(1,128)} %reshape.281.slots_ref), custom_call_target="tpu_custom_call" | custom-call | flops 4000000000 | bytes 14000000 | tf_op jit(solution)/shard_map/users/channel/pallas_call | solution.py:143
  169.4 7.2 %all-to-all-done.4 = f32[16,24,640]{2,1,0:T(8,128)S(1)} async-done(((f32[16,24,640]{2,1,0:T(8,128)}), f32[16,24,640]{2,1,0:T(8,128)S(1)}, u32[]{:S(2)}, u32[]{:S(2)}) %all-to-all-start.4) | async-done | bytes 983072 | tf_op jit(solution)/shard_map/schur/all_to_all | solution.py:505
  176.5 13.0 %solve.1 = (f32[3,128,128]{2,1,0:T(8,128)S(1)}, bf16[4,256,256]{2,1,0:T(8,128)(2,1)S(1)}) custom-call(s32[1]{0:T(128)} %bitcast.1.first_ref, f32[384,640]{1,0:T(8,128)S(1)} %bitcast.60, f32[256,384]{1,0:T(8,128)S(1)} %get-tuple-element.53.weighted_ref, f32[256,256]{1,0:T(8,128)S(1)} %reduce_sum.76.precoded_ref, s32[1,384]{1,0:T(1,128)S(1)} %bitcast.64), custom_call_target="tpu_custom_call" | custom-call | flops 14000000000 | bytes 4000000 | tf_op jit(solution)/shard_map/users/solve/pallas_call | solution.py:297
  189.5 10.5 %all_to_all.40.users_ref = bf16[4,256,256]{2,1,0:T(8,128)(2,1)S(1)} all-to-all(bf16[4,256,256]{2,1,0:T(8,128)(2,1)S(1)} %get-tuple-element.40), channel_id=1, replica_groups=mesh['grp'=2,'row'=16,'col'=4] {'col'}, dimensions={0} | all-to-all | bytes 1048576 | tf_op jit(solution)/shard_map/users/all_to_all | solution.py:511
  200.0 2.1 signal.1
  202.2 4.5 %all-to-all-start.6 = ((bf16[16,3,16,2048]{3,2,1,0:T(8,128)(2,1)}), bf16[16,3,16,2048]{3,2,1,0:T(8,128)(2,1)}, u32[]{:S(2)}, u32[]{:S(2)}) async-start(bf16[16,3,16,2048]{3,2,1,0:T(8,128)(2,1)} %signal.1), calls=%async_computation.6 | async-start | bytes 6291456 | tf_op jit(solution)/shard_map/signal/all_to_all | solution.py:521
  207.3 1.9 copy-done.7
  209.2 5.6 %update.1 = (bf16[256,1024]{1,0:T(8,128)(2,1)S(1)}, bf16[256,1024]{1,0:T(8,128)(2,1)}, bf16[256,1024]{1,0:T(8,128)(2,1)}, bf16[256,1024]{1,0:T(8,128)(2,1)}) custom-call(s32[2]{0:T(128)S(1)} %pad_add_fusion.1.where_ref, f32[256,384]{1,0:T(8,128)S(1)} %get-tuple-element.53.weighted_ref, f32[384,640]{1,0:T(8,128)S(1)} %bitcast.61, ...), custom_call_target="tpu_custom_call" | custom-call | flops 1500000000 | bytes 8000000 | tf_op jit(solution)/shard_map/update/update/pallas_call | solution.py:384
  214.8 0.6 collective-permute-start.13
  215.5 2.1 collective-permute-start.14
  217.5 0.8 collective-permute-start.15
  218.4 2.1 and_select_fusion
  220.4 24.5 %all-to-all-done.6 = bf16[16,3,16,2048]{3,2,1,0:T(8,128)(2,1)} async-done(((bf16[16,3,16,2048]{3,2,1,0:T(8,128)(2,1)}), bf16[16,3,16,2048]{3,2,1,0:T(8,128)(2,1)}, u32[]{:S(2)}, u32[]{:S(2)}) %all-to-all-start.6) | async-done | bytes 3145760 | tf_op jit(solution)/shard_map/signal/all_to_all | solution.py:521
  244.9 2.5 convert_reduce_fusion
  247.6 0.6 broadcast_in_dim.13
  248.2 5.4 %all-to-all-start.7 = ((f32[64,1,3]{2,1,0:T(1,128)}), f32[64,1,3]{2,1,0:T(1,128)}, u32[]{:S(2)}, u32[]{:S(2)}) async-start(f32[64,1,3]{2,1,0:T(1,128)} %broadcast_in_dim.13), calls=%async_computation.7 | async-start | bytes 65536 | tf_op jit(solution)/shard_map/signal/all_to_all | solution.py:526
  253.7 3.0 %fusion.15 = (f32[1,256,1024]{2,1,0:T(8,128)S(1)}, f32[1,256,1024]{2,1,0:T(8,128)S(1)}, f32[1,256,1024]{2,1,0:T(8,128)S(1)}) fusion(f32[3,256,1024]{2,1,0:T(8,128)} %and_select_fusion, f32[3,256,1024]{2,1,0:T(8,128)S(1)} %copy-done.4, bf16[256,1024]{1,0:T(8,128)(2,1)} %collective-permute-done.15, bf16[256,1024]{1,0:T(8,128)(2,1)} %collective-permute-done.14, ...), kind=kLoop, calls=%fused_computation.24 | loop fusion | flops 4718592 | bytes 11534345 | tf_op jit(solution)/shard_map/final/stack | solution.py:543
  256.7 1.9 pad_maximum_fusion
  258.6 4.4 %all-to-all-done.7 = f32[64,1,3]{2,1,0:T(1,128)} async-done(((f32[64,1,3]{2,1,0:T(1,128)}), f32[64,1,3]{2,1,0:T(1,128)}, u32[]{:S(2)}, u32[]{:S(2)}) %all-to-all-start.7) | async-done | bytes 800 | tf_op jit(solution)/shard_map/signal/all_to_all | solution.py:526
  263.0 0.8 reduce_sum.85
  263.9 0.8 multiply_bitcast_fusion
  (72 shorter events, 2.6 us)
Async XLA Ops:
  7.2 12.4 %copy-start = (bf16[3,1024,256]{2,1,0:T(8,128)(2,1)S(1)}, bf16[3,1024,256]{2,1,0:T(8,128)(2,1)}, u32[]{:S(2)}) copy-start(bf16[3,1024,256]{2,1,0:T(8,128)(2,1)} %param.13) | copy-start | bytes 4718596
  7.2 78.8 %all-gather.5.cloned.1.call-start = ((), (), s32[]{:S(2)}) async-start(), calls=%async_computation.8 | async-start | bytes 7798784 | tf_op jit(solution)/shard_map/newcomers/all_gather | solution.py:440
  8.3 1.7 collective-permute-start
  12.2 1.9 copy-start.2
  14.1 5.4 %copy-start.3 = (f32[3,256,1024]{2,1,0:T(8,128)S(1)}, f32[3,256,1024]{2,1,0:T(8,128)}, u32[]{:S(2)}) copy-start(f32[3,256,1024]{2,1,0:T(8,128)} %inverse_ref.1) | copy-start | bytes 9437188
  14.3 14.3 %collective-permute-start.2 = (bf16[3,256,256]{2,1,0:T(8,128)(2,1)S(1)}, bf16[3,256,256]{2,1,0:T(8,128)(2,1)S(1)}, u32[]{:S(2)}, u32[]{:S(2)}) collective-permute-start(bf16[3,256,256]{2,1,0:T(8,128)(2,1)S(1)} %get-tuple-element.29), channel_id=1, source_target_pairs={{0,8},{4,12},{8,0},{12,4},{16,24},{20,28},{24,16},{28,20},{32,40},... | collective-permute-start | bytes 1179656 | tf_op jit(solution)/shard_map/planes/ppermute | solution.py:412
  17.5 25.7 %collective-permute-start.3 = (bf16[3,256,256]{2,1,0:T(8,128)(2,1)S(1)}, bf16[3,256,256]{2,1,0:T(8,128)(2,1)}, u32[]{:S(2)}, u32[]{:S(2)}) collective-permute-start(bf16[3,256,256]{2,1,0:T(8,128)(2,1)S(1)} %get-tuple-element.30), channel_id=1, source_target_pairs={{0,12},{4,0},{8,4},{12,8},{16,28},{20,16},{24,20},{28,24},{32,44},... | collective-permute-start | bytes 1179656 | tf_op jit(solution)/shard_map/planes/ppermute | solution.py:412
  18.6 24.5 %collective-permute-start.1 = (bf16[3,256,256]{2,1,0:T(8,128)(2,1)S(1)}, bf16[3,256,256]{2,1,0:T(8,128)(2,1)}, u32[]{:S(2)}, u32[]{:S(2)}) collective-permute-start(bf16[3,256,256]{2,1,0:T(8,128)(2,1)S(1)} %get-tuple-element.28), channel_id=1, source_target_pairs={{0,4},{4,8},{8,12},{12,0},{16,20},{20,24},{24,28},{28,16},{32,36},... | collective-permute-start | bytes 1179656 | tf_op jit(solution)/shard_map/planes/ppermute | solution.py:412
  22.3 23.3 %all-to-all-start.1 = ((f32[4,256,256]{2,1,0:T(8,128)}), f32[4,256,256]{2,1,0:T(8,128)}, u32[]{:S(2)}, u32[]{:S(2)}) async-start(f32[4,256,256]{2,1,0:T(8,128)} %concatenate.10), calls=%async_computation.1 | async-start | bytes 2097152 | tf_op jit(solution)/shard_map/planes/all_to_all | solution.py:423
  43.2 7.8 %copy-start.9 = (s32[6,3,128,1]{2,3,1,0:T(1,128)S(1)}, s32[6,3,128,1]{2,3,1,0:T(1,128)}, u32[]{:S(2)}) copy-start(s32[6,3,128,1]{2,3,1,0:T(1,128)} %param.10) | copy-start | bytes 27652
  43.2 8.1 %copy-start.10 = (s32[32]{0:T(128)S(1)}, s32[32]{0:T(128)}, u32[]{:S(2)}) copy-start(s32[32]{0:T(128)} %param.11) | copy-start | bytes 388
  45.6 31.7 %all-to-all-start = ((bf16[4,4,256,256]{3,2,1,0:T(8,128)(2,1)}), bf16[4,4,256,256]{3,2,1,0:T(8,128)(2,1)S(1)}, u32[]{:S(2)}, u32[]{:S(2)}) async-start(bf16[4,4,256,256]{3,2,1,0:T(8,128)(2,1)} %fusion.6), calls=%async_computation | async-start | bytes 4194304 | tf_op jit(solution)/shard_map/planes/all_to_all | solution.py:423
  95.7 21.4 %copy-start.8 = (s32[6,3,128]{2,1,0:T(4,128)S(1)}, s32[6,3,128]{2,1,0:T(4,128)}, u32[]{:S(2)}) copy-start(s32[6,3,128]{2,1,0:T(4,128)} %param.12) | copy-start | bytes 27652
  95.7 18.5 %all-to-all-start.2 = ((bf16[4,304,384]{2,1,0:T(8,128)(2,1)}), bf16[4,304,384]{2,1,0:T(8,128)(2,1)}, u32[]{:S(2)}, u32[]{:S(2)}) async-start(bf16[4,304,384]{2,1,0:T(8,128)(2,1)} %columns.1), calls=%async_computation.2 | async-start | bytes 1867776 | tf_op jit(solution)/shard_map/columns/all_to_all | solution.py:481
  115.6 8.7 %collective-permute-start.4 = (bf16[256,384]{1,0:T(8,128)(2,1)S(1)}, bf16[256,384]{1,0:T(8,128)(2,1)S(1)}, u32[]{:S(2)}, u32[]{:S(2)}) collective-permute-start(bf16[256,384]{1,0:T(8,128)(2,1)S(1)} %slice.69.own_ref), channel_id=1, source_target_pairs={{0,4},{4,8},{8,12},{12,0},{16,20},{20,24},{24,28},{28,16},{32,36},... | collective-permute-start | bytes 589832 | tf_op jit(solution)/shard_map/columns/ppermute | solution.py:412
  117.8 11.3 %collective-permute-start.5 = (bf16[256,384]{1,0:T(8,128)(2,1)S(1)}, bf16[256,384]{1,0:T(8,128)(2,1)S(1)}, u32[]{:S(2)}, u32[]{:S(2)}) collective-permute-start(bf16[256,384]{1,0:T(8,128)(2,1)S(1)} %slice.69.own_ref), channel_id=1, source_target_pairs={{0,8},{4,12},{8,0},{12,4},{16,24},{20,28},{24,16},{28,20},{32,40},... | collective-permute-start | bytes 589832 | tf_op jit(solution)/shard_map/columns/ppermute | solution.py:412
  120.5 8.6 %collective-permute-start.6 = (bf16[256,384]{1,0:T(8,128)(2,1)S(1)}, bf16[256,384]{1,0:T(8,128)(2,1)S(1)}, u32[]{:S(2)}, u32[]{:S(2)}) collective-permute-start(bf16[256,384]{1,0:T(8,128)(2,1)S(1)} %slice.69.own_ref), channel_id=1, source_target_pairs={{0,12},{4,0},{8,4},{12,8},{16,28},{20,16},{24,20},{28,24},{32,44},... | collective-permute-start | bytes 589832 | tf_op jit(solution)/shard_map/columns/ppermute | solution.py:412
  121.9 7.2 %collective-permute-start.7 = (bf16[256,384]{1,0:T(8,128)(2,1)S(1)}, bf16[256,384]{1,0:T(8,128)(2,1)S(1)}, u32[]{:S(2)}, u32[]{:S(2)}) collective-permute-start(bf16[256,384]{1,0:T(8,128)(2,1)S(1)} %slice.69.own_ref), channel_id=1, source_target_pairs={{0,48},{4,52},{8,56},{12,60},{16,0},{20,4},{24,8},{28,12},{32,16},... | collective-permute-start | bytes 589832 | tf_op jit(solution)/shard_map/columns/ppermute | solution.py:416
  123.2 8.3 %collective-permute-start.8 = (bf16[256,384]{1,0:T(8,128)(2,1)S(1)}, bf16[256,384]{1,0:T(8,128)(2,1)S(1)}, u32[]{:S(2)}, u32[]{:S(2)}) collective-permute-start(bf16[256,384]{1,0:T(8,128)(2,1)S(1)} %slice.69.own_ref), channel_id=1, source_target_pairs={{0,32},{4,36},{8,40},{12,44},{16,48},{20,52},{24,56},{28,60},{32,0... | collective-permute-start | bytes 589832 | tf_op jit(solution)/shard_map/columns/ppermute | solution.py:416
  124.3 9.2 %collective-permute-start.9 = (bf16[256,384]{1,0:T(8,128)(2,1)S(1)}, bf16[256,384]{1,0:T(8,128)(2,1)S(1)}, u32[]{:S(2)}, u32[]{:S(2)}) collective-permute-start(bf16[256,384]{1,0:T(8,128)(2,1)S(1)} %slice.69.own_ref), channel_id=1, source_target_pairs={{0,16},{4,20},{8,24},{12,28},{16,32},{20,36},{24,40},{28,44},{32,4... | collective-permute-start | bytes 589832 | tf_op jit(solution)/shard_map/columns/ppermute | solution.py:416
  137.0 8.8 %collective-permute-start.10 = (bf16[256,384]{1,0:T(8,128)(2,1)}, bf16[256,384]{1,0:T(8,128)(2,1)S(1)}, u32[]{:S(2)}, u32[]{:S(2)}) collective-permute-start(bf16[256,384]{1,0:T(8,128)(2,1)} %get-tuple-element.37), channel_id=1, source_target_pairs={{0,12},{4,0},{8,4},{12,8},{16,28},{20,16},{24,20},{28,24},{32,44},... | collective-permute-start | bytes 589832 | tf_op jit(solution)/shard_map/schur/ppermute | solution.py:412
  137.1 8.7 %collective-permute-start.11 = (bf16[256,384]{1,0:T(8,128)(2,1)}, bf16[256,384]{1,0:T(8,128)(2,1)S(1)}, u32[]{:S(2)}, u32[]{:S(2)}) collective-permute-start(bf16[256,384]{1,0:T(8,128)(2,1)} %get-tuple-element.38), channel_id=1, source_target_pairs={{0,8},{4,12},{8,0},{12,4},{16,24},{20,28},{24,16},{28,20},{32,40},... | collective-permute-start | bytes 589832 | tf_op jit(solution)/shard_map/schur/ppermute | solution.py:412
  139.1 10.7 %collective-permute-start.12 = (bf16[256,384]{1,0:T(8,128)(2,1)S(1)}, bf16[256,384]{1,0:T(8,128)(2,1)S(1)}, u32[]{:S(2)}, u32[]{:S(2)}) collective-permute-start(bf16[256,384]{1,0:T(8,128)(2,1)S(1)} %get-tuple-element.39), channel_id=1, source_target_pairs={{0,4},{4,8},{8,12},{12,0},{16,20},{20,24},{24,28},{28,16},{32,36},... | collective-permute-start | bytes 589832 | tf_op jit(solution)/shard_map/schur/ppermute | solution.py:412
  140.3 15.4 %all-to-all-start.3 = ((bf16[16,24,640]{2,1,0:T(8,128)(2,1)}), bf16[16,24,640]{2,1,0:T(8,128)(2,1)S(1)}, u32[]{:S(2)}, u32[]{:S(2)}) async-start(bf16[16,24,640]{2,1,0:T(8,128)(2,1)} %bitcast.13), calls=%async_computation.3 | async-start | bytes 983040 | tf_op jit(solution)/shard_map/schur/all_to_all | solution.py:496
  145.7 61.6 %all-gather.7.cloned.1.call-start = ((), (), s32[]{:S(2)}) async-start(), calls=%async_computation.9 | async-start | bytes 3342336 | tf_op jit(solution)/shard_map/schur/all_gather | solution.py:494
  156.9 19.6 %all-to-all-start.4 = ((f32[16,24,640]{2,1,0:T(8,128)}), f32[16,24,640]{2,1,0:T(8,128)S(1)}, u32[]{:S(2)}, u32[]{:S(2)}) async-start(f32[16,24,640]{2,1,0:T(8,128)} %broadcast_in_dim.12), calls=%async_computation.4 | async-start | bytes 1966080 | tf_op jit(solution)/shard_map/schur/all_to_all | solution.py:505
  176.5 23.5 %copy-start.5 = (bf16[3,256,2048]{2,1,0:T(8,128)(2,1)S(1)}, bf16[3,256,2048]{2,1,0:T(8,128)(2,1)}, u32[]{:S(2)}) copy-start(bf16[3,256,2048]{2,1,0:T(8,128)(2,1)} %channel.1.channel_ref) | copy-start | bytes 9437188
  202.2 42.7 %all-to-all-start.6 = ((bf16[16,3,16,2048]{3,2,1,0:T(8,128)(2,1)}), bf16[16,3,16,2048]{3,2,1,0:T(8,128)(2,1)}, u32[]{:S(2)}, u32[]{:S(2)}) async-start(bf16[16,3,16,2048]{3,2,1,0:T(8,128)(2,1)} %signal.1), calls=%async_computation.6 | async-start | bytes 6291456 | tf_op jit(solution)/shard_map/signal/all_to_all | solution.py:521
  207.3 1.9 copy-start.7
  214.8 2.7 copy-start.6
  214.8 32.7 %collective-permute-start.13 = (bf16[256,1024]{1,0:T(8,128)(2,1)}, bf16[256,1024]{1,0:T(8,128)(2,1)}, u32[]{:S(2)}, u32[]{:S(2)}) collective-permute-start(bf16[256,1024]{1,0:T(8,128)(2,1)} %get-tuple-element.44), channel_id=1, source_target_pairs={{0,1},{1,2},{2,3},{3,0},{4,5},{5,6},{6,7},{7,4},{8,9},{9,10},{10,1... | collective-permute-start | bytes 1572872 | tf_op jit(solution)/shard_map/update/ppermute | solution.py:419
  215.5 32.1 %collective-permute-start.14 = (bf16[256,1024]{1,0:T(8,128)(2,1)}, bf16[256,1024]{1,0:T(8,128)(2,1)}, u32[]{:S(2)}, u32[]{:S(2)}) collective-permute-start(bf16[256,1024]{1,0:T(8,128)(2,1)} %get-tuple-element.45), channel_id=1, source_target_pairs={{0,2},{1,3},{2,0},{3,1},{4,6},{5,7},{6,4},{7,5},{8,10},{9,11},{10,... | collective-permute-start | bytes 1572872 | tf_op jit(solution)/shard_map/update/ppermute | solution.py:419
  217.5 36.1 %copy-start.4 = (f32[3,256,1024]{2,1,0:T(8,128)S(1)}, f32[3,256,1024]{2,1,0:T(8,128)}, u32[]{:S(2)}) copy-start(f32[3,256,1024]{2,1,0:T(8,128)} %inverse_ref.1) | copy-start | bytes 9437188
  217.5 30.0 %collective-permute-start.15 = (bf16[256,1024]{1,0:T(8,128)(2,1)}, bf16[256,1024]{1,0:T(8,128)(2,1)}, u32[]{:S(2)}, u32[]{:S(2)}) collective-permute-start(bf16[256,1024]{1,0:T(8,128)(2,1)} %get-tuple-element.46), channel_id=1, source_target_pairs={{0,3},{1,0},{2,1},{3,2},{4,7},{5,4},{6,5},{7,6},{8,11},{9,8},{10,9... | collective-permute-start | bytes 1572872 | tf_op jit(solution)/shard_map/update/ppermute | solution.py:419
  248.2 14.8 %all-to-all-start.7 = ((f32[64,1,3]{2,1,0:T(1,128)}), f32[64,1,3]{2,1,0:T(1,128)}, u32[]{:S(2)}, u32[]{:S(2)}) async-start(f32[64,1,3]{2,1,0:T(1,128)} %broadcast_in_dim.13), calls=%async_computation.7 | async-start | bytes 65536 | tf_op jit(solution)/shard_map/signal/all_to_all | solution.py:526
  256.7 8.0 %copy-start.1 = (bf16[3,1024,256]{2,1,0:T(8,128)(2,1)S(1)}, bf16[3,1024,256]{2,1,0:T(8,128)(2,1)}, u32[]{:S(2)}) copy-start(bf16[3,1024,256]{2,1,0:T(8,128)(2,1)} %param.13) | copy-start | bytes 4718596
Sparse Core Ops, SparseCore 0:
  12.3 73.6 all-gather.4
  150.8 50.4 all-gather.6

commit v3 on v2

--- a/solution.py
+++ b/solution.py
@@ -99,15 +99,16 @@
     row_ref, gathered_ref, channel_ref, place_ref, out_ref, window_ref, held_ref, sems
 ):
     groups, _, antennas = channel_ref.shape
-    copies = start_inputs(gathered_ref, channel_ref, window_ref, held_ref, sems, row_ref[0])
-    out_ref[groups] = jnp.zeros(out_ref.shape[1:], bf16)
+    row, plane = row_ref[0], row_ref[1]
+    copies = start_inputs(gathered_ref, channel_ref, window_ref, held_ref, sems, row)
+    out_ref[(groups - plane) % 4] = jnp.zeros(out_ref.shape[1:], bf16)
     for g in range(groups):
         choose = choosing(place_ref, g)
         for copy in copies[g]:
             copy.wait()
         window = window_ref[g].reshape(16 * WINDOW, antennas)
         wide = dot_t(held_ref[g], window).astype(bf16)
-        out_ref[g] = dot(wide, choose).astype(bf16)
+        out_ref[(g - plane) % 4] = dot(wide, choose).astype(bf16)
 
 
 def make_columns(row, gathered, channels, place):
@@ -477,9 +478,10 @@
 
     with jax.named_scope("columns"):
         gathered, square, precoded = lax.optimization_barrier((gathered, square, precoded))
-        both = make_columns(row_index.reshape(1), gathered, channels, place)
-        both = lax.all_to_all(both, "col", 0, 0, tiled=True)
-        summed = jnp.sum(both.astype(f32), axis=0)
+        both = make_columns(jnp.stack([row_index, col_index]), gathered, channels, place)
+        summed = both[0].astype(f32)
+        for d in (1, 2, 3):
+            summed = summed + along_z(both[d], d).astype(f32)
         own = summed[:user_rows].astype(bf16)
         by_row = [own] + [along_x(own, d) for d in (1, 2, 3)]
         by_col = [own] + [along_y(own, -d) for d in (1, 2, 3)]

time: 273 us -> 279 us (1.022)
  blocking collectives: 10.5 us -> 14.9 us
    all_to_all x1 -> x0, waiting for transfers between devices: 14 us -> none  [local(): both = lax.all_to_all(both, 'col', 0, 0, tiled=True)]
    ppermute x3 -> x6, waiting for transfers between devices: 0.01 us -> 9.26 us  [along_z(): return lax.ppermute(value, 'col', [(z, (z + step) % 4) for z in range(4)])]
    ppermute x3 -> x6, starting transfers between devices: 3.52 us -> 9.29 us  [along_z(): return lax.ppermute(value, 'col', [(z, (z + step) % 4) for z in range(4)])]
    all_to_all x1, blocking collectives: 10.5 us -> 14.9 us  [local(): users_side = lax.all_to_all(users, 'col', 0, 0, tiled=True)]
    all_to_all x1 -> x0, starting transfers between devices: 4.44 us -> none  [local(): both = lax.all_to_all(both, 'col', 0, 0, tiled=True)]
  transfers between devices with their start and end apart: 25 -> 27, of which waited for: 13 -> 17; matrix products, arithmetic and copies ran while one was open for 8% -> 8% of each run, Pallas kernels for 11% -> 11%
where the time goes in v3:
time: 279 us; the launch traced here: 278 us
  waiting for transfers between devices  114 us (41%)
  starting transfers between devices  56.7 us (20%)
  Pallas kernels  43.3 us (16%)
  other arithmetic  20.8 us (7%)
  blocking collectives  14.9 us (5%)
  between operations  14.4 us (5%)
  local copies, waits for them, and re-layouts  12.1 us (4%)
    all_to_all x1, waiting for transfers between devices, local(): received = lax.all_to_all(signal_part, 'row', 0, 0, tiled=True)  27.2 us
    all_to_all x2, waiting for transfers between devices, to_planes(): return lax.all_to_all(padded, 'col', 0, 0, tiled=True)  22.9 us
    ppermute x9, waiting for transfers between devices, along_x(): return lax.ppermute(value, 'row', pairs)  19.8 us
    all_to_all x1, blocking collectives, local(): users_side = lax.all_to_all(users, 'col', 0, 0, tiled=True)  14.9 us
    pallas_call x1, Pallas kernels, make_solve(): pl.pallas_call(solve_kernel, out_shape=(jax.ShapeDtypeStruct((EPOCHS, BLO...  13 us
    ppermute x9, starting transfers between devices, along_x(): return lax.ppermute(value, 'row', pairs)  11.7 us
    all_to_all x2, starting transfers between devices, to_planes(): return lax.all_to_all(padded, 'col', 0, 0, tiled=True)  10.6 us
    pallas_call x1, Pallas kernels, make_columns(): pl.pallas_call(columns_kernel, out_shape=jax.ShapeDtypeStruct((groups + 1...  9.72 us
  transfers between devices with their start and end apart: 27, of which 17 were waited for; matrix products, arithmetic and copies ran while one was open for 8% of the time, Pallas kernels for 11%

profile of v3, /device:TPU:0, one launch (start us, length us, event | category | flops | bytes accessed | tf_op | source)
XLA Modules:
  0.0 277.9 jit_solution(9979993188278301697)
XLA Ops:
  7.2 1.1 constant_dynamic-slice_fusion.1
  8.4 1.6 collective-permute-done
  10.0 1.0 select_bitcast_fusion.1
  11.3 0.8 pad.6
  12.2 1.9 copy-done.2
  14.3 3.2 %collective-permute-start.2 = (bf16[3,256,256]{2,1,0:T(8,128)(2,1)S(1)}, bf16[3,256,256]{2,1,0:T(8,128)(2,1)S(1)}, u32[]{:S(2)}, u32[]{:S(2)}) collective-permute-start(bf16[3,256,256]{2,1,0:T(8,128)(2,1)S(1)} %get-tuple-element.29), channel_id=1, source_target_pairs={{0,8},{4,12},{8,0},{12,4},{16,24},{20,28},{24,16},{28,20},{32,40},... | collective-permute-start | bytes 1179656 | tf_op jit(solution)/shard_map/planes/ppermute | solution.py:413
  17.5 1.1 collective-permute-start.3
  18.6 0.9 collective-permute-start.1
  19.5 1.6 fusion.22
  21.2 1.1 concatenate.10
  22.3 5.3 %all-to-all-start.1 = ((f32[4,256,256]{2,1,0:T(8,128)}), f32[4,256,256]{2,1,0:T(8,128)}, u32[]{:S(2)}, u32[]{:S(2)}) async-start(f32[4,256,256]{2,1,0:T(8,128)} %concatenate.10), calls=%async_computation.1 | async-start | bytes 2097152 | tf_op jit(solution)/shard_map/planes/all_to_all | solution.py:424
  27.6 1.0 collective-permute-done.2
  28.6 14.6 %collective-permute-done.3 = bf16[3,256,256]{2,1,0:T(8,128)(2,1)} collective-permute-done((bf16[3,256,256]{2,1,0:T(8,128)(2,1)S(1)}, bf16[3,256,256]{2,1,0:T(8,128)(2,1)}, u32[]{:S(2)}, u32[]{:S(2)}) %collective-permute-start.3) | collective-permute-done | bytes 393248 | tf_op jit(solution)/shard_map/planes/ppermute | solution.py:413
  43.2 2.5 fusion.6
  45.6 5.3 %all-to-all-start = ((bf16[4,4,256,256]{3,2,1,0:T(8,128)(2,1)}), bf16[4,4,256,256]{3,2,1,0:T(8,128)(2,1)S(1)}, u32[]{:S(2)}, u32[]{:S(2)}) async-start(bf16[4,4,256,256]{3,2,1,0:T(8,128)(2,1)} %fusion.6), calls=%async_computation | async-start | bytes 4194304 | tf_op jit(solution)/shard_map/planes/all_to_all | solution.py:424
  52.1 0.6 fusion.19.place_ref
  52.8 1.6 reduce_sum.67.precoded_ref
  54.4 22.9 %all-to-all-done.square_ref = bf16[4,4,256,256]{3,2,1,0:T(8,128)(2,1)S(1)} async-done(((bf16[4,4,256,256]{3,2,1,0:T(8,128)(2,1)}), bf16[4,4,256,256]{3,2,1,0:T(8,128)(2,1)S(1)}, u32[]{:S(2)}, u32[]{:S(2)}) %all-to-all-start) | async-done | bytes 2097184 | tf_op jit(solution)/shard_map/planes/all_to_all | solution.py:424
  77.3 8.7 %all-gather.5.cloned.1.call-done = bf16[1792,2048]{1,0:T(8,128)(2,1)} async-done(((bf16[112,2048]{1,0:T(8,128)(2,1)}), bf16[1792,2048]{1,0:T(8,128)(2,1)}) %all-gather.5.cloned.1.call-update) | async-done | bytes 7340048 | tf_op jit(solution)/shard_map/newcomers/all_gather | solution.py:441
  86.0 9.7 %columns.1 = bf16[4,304,384]{2,1,0:T(8,128)(2,1)} custom-call(s32[2]{0:T(128)} %pad_add_fusion.1.row_ref, bf16[16,112,2048]{2,1,0:T(8,128)(2,1)} %bitcast.82, bf16[3,256,2048]{2,1,0:T(8,128)(2,1)} %channel_ref.3, s32[3,1,384]{2,1,0:T(1,128)} %fusion.19.place_ref), custom_call_target="tpu_custom_call" | custom-call | flops 4000000000 | bytes 12000000 | tf_op jit(solution)/shard_map/columns/columns/pallas_call | solution.py:116
  95.8 1.9 slice_bitcast_fusion.2
  97.7 1.6 collective-permute-start.4
  99.2 2.8 %collective-permute-start.5 = (bf16[304,384]{1,0:T(8,128)(2,1)S(1)}, bf16[304,384]{1,0:T(8,128)(2,1)S(1)}, u32[]{:S(2)}, u32[]{:S(2)}) collective-permute-start(bf16[304,384]{1,0:T(8,128)(2,1)S(1)} %get-tuple-element.59), channel_id=1, source_target_pairs={{0,2},{1,3},{2,0},{3,1},{4,6},{5,7},{6,4},{7,5},{8,10},{9,11},{10,... | collective-permute-start | bytes 700424 | tf_op jit(solution)/shard_map/columns/ppermute | solution.py:420
  102.1 1.4 collective-permute-start.6
  103.4 3.1 %collective-permute-done.4 = bf16[304,384]{1,0:T(8,128)(2,1)S(1)} collective-permute-done((bf16[304,384]{1,0:T(8,128)(2,1)}, bf16[304,384]{1,0:T(8,128)(2,1)S(1)}, u32[]{:S(2)}, u32[]{:S(2)}) %collective-permute-start.4) | collective-permute-done | bytes 233504 | tf_op jit(solution)/shard_map/columns/ppermute | solution.py:420
  106.5 6.2 %collective-permute-done.5 = bf16[304,384]{1,0:T(8,128)(2,1)S(1)} collective-permute-done((bf16[304,384]{1,0:T(8,128)(2,1)S(1)}, bf16[304,384]{1,0:T(8,128)(2,1)S(1)}, u32[]{:S(2)}, u32[]{:S(2)}) %collective-permute-start.5) | collective-permute-done | bytes 233504 | tf_op jit(solution)/shard_map/columns/ppermute | solution.py:420
  112.7 1.1 fusion.17.summed_ref
  113.8 2.7 collective-permute-start.10
  116.5 0.7 dynamic-slice_bitcast_fusion.1.place_ref
  117.2 0.8 collective-permute-start.11
  118.0 0.9 collective-permute-start.12
  119.1 2.5 collective-permute-start.8
  121.6 2.5 collective-permute-done.10.col1_ref
  124.5 1.0 target.1.base_ref
  125.5 0.9 collective-permute-done.11.col2_ref
  126.4 2.0 collective-permute-done.12.col3_ref
  128.4 0.9 collective-permute-done.7.row1_ref
  129.9 3.5 %middle.1 = (f32[256,384]{1,0:T(8,128)S(1)}, bf16[256,384]{1,0:T(8,128)(2,1)}, bf16[256,384]{1,0:T(8,128)(2,1)}, bf16[256,384]{1,0:T(8,128)(2,1)S(1)}, bf16[384,640]{1,0:T(8,128)(2,1)}) custom-call(s32[3]{0:T(128)S(1)} %pad_add_fusion.where_ref, bf16[4,4,256,256]{3,2,1,0:T(8,128)(2,1)S(1)} %all-to-all-done.square_ref, bf16[256,384]{1,0:T(8,128)(2,1)S(1)} %slice.95.own_ref, ...), custom_call_target="tpu_custom_call" | custom-call | flops 2000000000 | bytes 8000000 | tf_op jit(solution)/shard_map/schur/middle/pallas_call | solution.py:221
  133.4 2.6 collective-permute-start.13
  136.9 6.9 %all-to-all-start.2 = ((bf16[16,24,640]{2,1,0:T(8,128)(2,1)}), bf16[16,24,640]{2,1,0:T(8,128)(2,1)S(1)}, u32[]{:S(2)}, u32[]{:S(2)}) async-start(bf16[16,24,640]{2,1,0:T(8,128)(2,1)} %bitcast.18), calls=%async_computation.2 | async-start | bytes 983040 | tf_op jit(solution)/shard_map/schur/all_to_all | solution.py:498
  143.9 2.8 collective-permute-done.15
  146.7 0.8 fusion.21
  147.5 6.3 %all-to-all-done.2 = bf16[16,24,640]{2,1,0:T(8,128)(2,1)S(1)} async-done(((bf16[16,24,640]{2,1,0:T(8,128)(2,1)}), bf16[16,24,640]{2,1,0:T(8,128)(2,1)S(1)}, u32[]{:S(2)}, u32[]{:S(2)}) %all-to-all-start.2) | async-done | bytes 491552 | tf_op jit(solution)/shard_map/schur/all_to_all | solution.py:498
  154.0 1.0 broadcast_in_dim.12
  155.0 3.6 %all-to-all-start.3 = ((f32[16,24,640]{2,1,0:T(8,128)}), f32[16,24,640]{2,1,0:T(8,128)S(1)}, u32[]{:S(2)}, u32[]{:S(2)}) async-start(f32[16,24,640]{2,1,0:T(8,128)} %broadcast_in_dim.12), calls=%async_computation.3 | async-start | bytes 1966080 | tf_op jit(solution)/shard_map/schur/all_to_all | solution.py:507
  159.3 8.2 %channel.1.channel_ref = bf16[3,256,2048]{2,1,0:T(8,128)(2,1)} custom-call(s32[1]{0:T(128)} %bitcast.1.first_ref, bf16[16,112,2048]{2,1,0:T(8,128)(2,1)} %bitcast.83, bf16[3,256,2048]{2,1,0:T(8,128)(2,1)} %channel_ref.3, s32[3,1,384]{2,1,0:T(1,128)} %fusion.19.place_ref, s32[3,1,384]{2,1,0:T(1,128)} %reshape.282.slots_ref), custom_call_target="tpu_custom_call" | custom-call | flops 4000000000 | bytes 14000000 | tf_op jit(solution)/shard_map/users/channel/pallas_call | solution.py:144
  167.5 8.1 %all-to-all-done.3 = f32[16,24,640]{2,1,0:T(8,128)S(1)} async-done(((f32[16,24,640]{2,1,0:T(8,128)}), f32[16,24,640]{2,1,0:T(8,128)S(1)}, u32[]{:S(2)}, u32[]{:S(2)}) %all-to-all-start.3) | async-done | bytes 983072 | tf_op jit(solution)/shard_map/schur/all_to_all | solution.py:507
  175.6 13.0 %solve.1 = (f32[3,128,128]{2,1,0:T(8,128)S(1)}, bf16[4,256,256]{2,1,0:T(8,128)(2,1)S(1)}) custom-call(s32[1]{0:T(128)} %bitcast.1.first_ref, f32[384,640]{1,0:T(8,128)S(1)} %bitcast.71, f32[256,384]{1,0:T(8,128)S(1)} %get-tuple-element.53.weighted_ref, f32[256,256]{1,0:T(8,128)S(1)} %reduce_sum.67.precoded_ref, s32[1,384]{1,0:T(1,128)S(1)} %bitcast.75), custom_call_target="tpu_custom_call" | custom-call | flops 14000000000 | bytes 4000000 | tf_op jit(solution)/shard_map/users/solve/pallas_call | solution.py:298
  188.6 14.9 %all_to_all.35.users_ref = bf16[4,256,256]{2,1,0:T(8,128)(2,1)S(1)} all-to-all(bf16[4,256,256]{2,1,0:T(8,128)(2,1)S(1)} %get-tuple-element.40), channel_id=1, replica_groups=mesh['grp'=2,'row'=16,'col'=4] {'col'}, dimensions={0} | all-to-all | bytes 1048576 | tf_op jit(solution)/shard_map/users/all_to_all | solution.py:513
  203.5 2.2 signal.1
  205.7 4.5 %all-to-all-start.5 = ((bf16[16,3,16,2048]{3,2,1,0:T(8,128)(2,1)}), bf16[16,3,16,2048]{3,2,1,0:T(8,128)(2,1)}, u32[]{:S(2)}, u32[]{:S(2)}) async-start(bf16[16,3,16,2048]{3,2,1,0:T(8,128)(2,1)} %signal.1), calls=%async_computation.5 | async-start | bytes 6291456 | tf_op jit(solution)/shard_map/signal/all_to_all | solution.py:523
  210.8 1.9 copy-done.7
  212.7 5.6 %update.1 = (bf16[256,1024]{1,0:T(8,128)(2,1)S(1)}, bf16[256,1024]{1,0:T(8,128)(2,1)}, bf16[256,1024]{1,0:T(8,128)(2,1)}, bf16[256,1024]{1,0:T(8,128)(2,1)}) custom-call(s32[2]{0:T(128)S(1)} %pad_add_fusion.2.where_ref, f32[256,384]{1,0:T(8,128)S(1)} %get-tuple-element.53.weighted_ref, f32[384,640]{1,0:T(8,128)S(1)} %bitcast.72, ...), custom_call_target="tpu_custom_call" | custom-call | flops 1500000000 | bytes 8000000 | tf_op jit(solution)/shard_map/update/update/pallas_call | solution.py:385
  218.9 2.1 collective-permute-start.17
  221.0 0.8 collective-permute-start.18
  221.8 2.1 and_select_fusion
  223.9 27.2 %all-to-all-done.5 = bf16[16,3,16,2048]{3,2,1,0:T(8,128)(2,1)} async-done(((bf16[16,3,16,2048]{3,2,1,0:T(8,128)(2,1)}), bf16[16,3,16,2048]{3,2,1,0:T(8,128)(2,1)}, u32[]{:S(2)}, u32[]{:S(2)}) %all-to-all-start.5) | async-done | bytes 3145760 | tf_op jit(solution)/shard_map/signal/all_to_all | solution.py:523
  251.1 2.5 convert_reduce_fusion
  254.4 5.4 %all-to-all-start.6 = ((f32[64,1,3]{2,1,0:T(1,128)}), f32[64,1,3]{2,1,0:T(1,128)}, u32[]{:S(2)}, u32[]{:S(2)}) async-start(f32[64,1,3]{2,1,0:T(1,128)} %broadcast_in_dim.13), calls=%async_computation.6 | async-start | bytes 65536 | tf_op jit(solution)/shard_map/signal/all_to_all | solution.py:528
  259.8 3.0 %fusion.15 = (f32[1,256,1024]{2,1,0:T(8,128)S(1)}, f32[1,256,1024]{2,1,0:T(8,128)S(1)}, f32[1,256,1024]{2,1,0:T(8,128)S(1)}) fusion(f32[3,256,1024]{2,1,0:T(8,128)} %and_select_fusion, f32[3,256,1024]{2,1,0:T(8,128)S(1)} %copy-done.4, bf16[256,1024]{1,0:T(8,128)(2,1)} %collective-permute-done.18, bf16[256,1024]{1,0:T(8,128)(2,1)} %collective-permute-done.17, ...), kind=kLoop, calls=%fused_computation.23 | loop fusion | flops 4718592 | bytes 11534345 | tf_op jit(solution)/shard_map/final/stack | solution.py:545
  262.8 1.9 pad_maximum_fusion
  264.7 4.6 %all-to-all-done.6 = f32[64,1,3]{2,1,0:T(1,128)} async-done(((f32[64,1,3]{2,1,0:T(1,128)}), f32[64,1,3]{2,1,0:T(1,128)}, u32[]{:S(2)}, u32[]{:S(2)}) %all-to-all-start.6) | async-done | bytes 800 | tf_op jit(solution)/shard_map/signal/all_to_all | solution.py:528
  269.3 0.8 reduce_sum.75
  270.2 0.8 multiply_bitcast_fusion
  (78 shorter events, 6.8 us)
Async XLA Ops:
  7.2 12.4 %copy-start = (bf16[3,1024,256]{2,1,0:T(8,128)(2,1)S(1)}, bf16[3,1024,256]{2,1,0:T(8,128)(2,1)}, u32[]{:S(2)}) copy-start(bf16[3,1024,256]{2,1,0:T(8,128)(2,1)} %param.13) | copy-start | bytes 4718596
  7.2 78.8 %all-gather.5.cloned.1.call-start = ((), (), s32[]{:S(2)}) async-start(), calls=%async_computation.7 | async-start | bytes 7798784 | tf_op jit(solution)/shard_map/newcomers/all_gather | solution.py:441
  8.3 1.7 collective-permute-start
  12.2 1.9 copy-start.2
  14.1 5.4 %copy-start.3 = (f32[3,256,1024]{2,1,0:T(8,128)S(1)}, f32[3,256,1024]{2,1,0:T(8,128)}, u32[]{:S(2)}) copy-start(f32[3,256,1024]{2,1,0:T(8,128)} %inverse_ref.1) | copy-start | bytes 9437188
  14.3 14.3 %collective-permute-start.2 = (bf16[3,256,256]{2,1,0:T(8,128)(2,1)S(1)}, bf16[3,256,256]{2,1,0:T(8,128)(2,1)S(1)}, u32[]{:S(2)}, u32[]{:S(2)}) collective-permute-start(bf16[3,256,256]{2,1,0:T(8,128)(2,1)S(1)} %get-tuple-element.29), channel_id=1, source_target_pairs={{0,8},{4,12},{8,0},{12,4},{16,24},{20,28},{24,16},{28,20},{32,40},... | collective-permute-start | bytes 1179656 | tf_op jit(solution)/shard_map/planes/ppermute | solution.py:413
  17.5 25.7 %collective-permute-start.3 = (bf16[3,256,256]{2,1,0:T(8,128)(2,1)S(1)}, bf16[3,256,256]{2,1,0:T(8,128)(2,1)}, u32[]{:S(2)}, u32[]{:S(2)}) collective-permute-start(bf16[3,256,256]{2,1,0:T(8,128)(2,1)S(1)} %get-tuple-element.30), channel_id=1, source_target_pairs={{0,12},{4,0},{8,4},{12,8},{16,28},{20,16},{24,20},{28,24},{32,44},... | collective-permute-start | bytes 1179656 | tf_op jit(solution)/shard_map/planes/ppermute | solution.py:413
  18.6 24.5 %collective-permute-start.1 = (bf16[3,256,256]{2,1,0:T(8,128)(2,1)S(1)}, bf16[3,256,256]{2,1,0:T(8,128)(2,1)}, u32[]{:S(2)}, u32[]{:S(2)}) collective-permute-start(bf16[3,256,256]{2,1,0:T(8,128)(2,1)S(1)} %get-tuple-element.28), channel_id=1, source_target_pairs={{0,4},{4,8},{8,12},{12,0},{16,20},{20,24},{24,28},{28,16},{32,36},... | collective-permute-start | bytes 1179656 | tf_op jit(solution)/shard_map/planes/ppermute | solution.py:413
  22.3 23.4 %all-to-all-start.1 = ((f32[4,256,256]{2,1,0:T(8,128)}), f32[4,256,256]{2,1,0:T(8,128)}, u32[]{:S(2)}, u32[]{:S(2)}) async-start(f32[4,256,256]{2,1,0:T(8,128)} %concatenate.10), calls=%async_computation.1 | async-start | bytes 2097152 | tf_op jit(solution)/shard_map/planes/all_to_all | solution.py:424
  43.2 7.8 %copy-start.9 = (s32[6,3,128,1]{2,3,1,0:T(1,128)S(1)}, s32[6,3,128,1]{2,3,1,0:T(1,128)}, u32[]{:S(2)}) copy-start(s32[6,3,128,1]{2,3,1,0:T(1,128)} %param.10) | copy-start | bytes 27652
  43.2 8.1 %copy-start.10 = (s32[32]{0:T(128)S(1)}, s32[32]{0:T(128)}, u32[]{:S(2)}) copy-start(s32[32]{0:T(128)} %param.11) | copy-start | bytes 388
  45.6 31.7 %all-to-all-start = ((bf16[4,4,256,256]{3,2,1,0:T(8,128)(2,1)}), bf16[4,4,256,256]{3,2,1,0:T(8,128)(2,1)S(1)}, u32[]{:S(2)}, u32[]{:S(2)}) async-start(bf16[4,4,256,256]{3,2,1,0:T(8,128)(2,1)} %fusion.6), calls=%async_computation | async-start | bytes 4194304 | tf_op jit(solution)/shard_map/planes/all_to_all | solution.py:424
  95.7 20.8 %copy-start.8 = (s32[6,3,128]{2,1,0:T(4,128)S(1)}, s32[6,3,128]{2,1,0:T(4,128)}, u32[]{:S(2)}) copy-start(s32[6,3,128]{2,1,0:T(4,128)} %param.12) | copy-start | bytes 27652
  97.7 8.8 %collective-permute-start.4 = (bf16[304,384]{1,0:T(8,128)(2,1)}, bf16[304,384]{1,0:T(8,128)(2,1)S(1)}, u32[]{:S(2)}, u32[]{:S(2)}) collective-permute-start(bf16[304,384]{1,0:T(8,128)(2,1)} %get-tuple-element.57), channel_id=1, source_target_pairs={{0,1},{1,2},{2,3},{3,0},{4,5},{5,6},{6,7},{7,4},{8,9},{9,10},{10,1... | collective-permute-start | bytes 700424 | tf_op jit(solution)/shard_map/columns/ppermute | solution.py:420
  99.2 13.5 %collective-permute-start.5 = (bf16[304,384]{1,0:T(8,128)(2,1)S(1)}, bf16[304,384]{1,0:T(8,128)(2,1)S(1)}, u32[]{:S(2)}, u32[]{:S(2)}) collective-permute-start(bf16[304,384]{1,0:T(8,128)(2,1)S(1)} %get-tuple-element.59), channel_id=1, source_target_pairs={{0,2},{1,3},{2,0},{3,1},{4,6},{5,7},{6,4},{7,5},{8,10},{9,11},{10,... | collective-permute-start | bytes 700424 | tf_op jit(solution)/shard_map/columns/ppermute | solution.py:420
  102.1 10.6 %collective-permute-start.6 = (bf16[304,384]{1,0:T(8,128)(2,1)S(1)}, bf16[304,384]{1,0:T(8,128)(2,1)S(1)}, u32[]{:S(2)}, u32[]{:S(2)}) collective-permute-start(bf16[304,384]{1,0:T(8,128)(2,1)S(1)} %get-tuple-element.58), channel_id=1, source_target_pairs={{0,3},{1,0},{2,1},{3,2},{4,7},{5,4},{6,5},{7,6},{8,11},{9,8},{10,9... | collective-permute-start | bytes 700424 | tf_op jit(solution)/shard_map/columns/ppermute | solution.py:420
  113.8 10.3 %collective-permute-start.10 = (bf16[256,384]{1,0:T(8,128)(2,1)S(1)}, bf16[256,384]{1,0:T(8,128)(2,1)S(1)}, u32[]{:S(2)}, u32[]{:S(2)}) collective-permute-start(bf16[256,384]{1,0:T(8,128)(2,1)S(1)} %slice.95.own_ref), channel_id=1, source_target_pairs={{0,48},{4,52},{8,56},{12,60},{16,0},{20,4},{24,8},{28,12},{32,16},... | collective-permute-start | bytes 589832 | tf_op jit(solution)/shard_map/columns/ppermute | solution.py:417
  117.2 9.2 %collective-permute-start.11 = (bf16[256,384]{1,0:T(8,128)(2,1)S(1)}, bf16[256,384]{1,0:T(8,128)(2,1)S(1)}, u32[]{:S(2)}, u32[]{:S(2)}) collective-permute-start(bf16[256,384]{1,0:T(8,128)(2,1)S(1)} %slice.95.own_ref), channel_id=1, source_target_pairs={{0,32},{4,36},{8,40},{12,44},{16,48},{20,52},{24,56},{28,60},{32,0... | collective-permute-start | bytes 589832 | tf_op jit(solution)/shard_map/columns/ppermute | solution.py:417
  118.0 10.4 %collective-permute-start.12 = (bf16[256,384]{1,0:T(8,128)(2,1)S(1)}, bf16[256,384]{1,0:T(8,128)(2,1)S(1)}, u32[]{:S(2)}, u32[]{:S(2)}) collective-permute-start(bf16[256,384]{1,0:T(8,128)(2,1)S(1)} %slice.95.own_ref), channel_id=1, source_target_pairs={{0,16},{4,20},{8,24},{12,28},{16,32},{20,36},{24,40},{28,44},{32,4... | collective-permute-start | bytes 589832 | tf_op jit(solution)/shard_map/columns/ppermute | solution.py:417
  118.9 10.4 %collective-permute-start.7 = (bf16[256,384]{1,0:T(8,128)(2,1)S(1)}, bf16[256,384]{1,0:T(8,128)(2,1)S(1)}, u32[]{:S(2)}, u32[]{:S(2)}) collective-permute-start(bf16[256,384]{1,0:T(8,128)(2,1)S(1)} %slice.95.own_ref), channel_id=1, source_target_pairs={{0,4},{4,8},{8,12},{12,0},{16,20},{20,24},{24,28},{28,16},{32,36},... | collective-permute-start | bytes 589832 | tf_op jit(solution)/shard_map/columns/ppermute | solution.py:413
  119.1 10.2 %collective-permute-start.8 = (bf16[256,384]{1,0:T(8,128)(2,1)S(1)}, bf16[256,384]{1,0:T(8,128)(2,1)S(1)}, u32[]{:S(2)}, u32[]{:S(2)}) collective-permute-start(bf16[256,384]{1,0:T(8,128)(2,1)S(1)} %slice.95.own_ref), channel_id=1, source_target_pairs={{0,8},{4,12},{8,0},{12,4},{16,24},{20,28},{24,16},{28,20},{32,40},... | collective-permute-start | bytes 589832 | tf_op jit(solution)/shard_map/columns/ppermute | solution.py:413
  124.1 5.8 %collective-permute-start.9 = (bf16[256,384]{1,0:T(8,128)(2,1)S(1)}, bf16[256,384]{1,0:T(8,128)(2,1)S(1)}, u32[]{:S(2)}, u32[]{:S(2)}) collective-permute-start(bf16[256,384]{1,0:T(8,128)(2,1)S(1)} %slice.95.own_ref), channel_id=1, source_target_pairs={{0,12},{4,0},{8,4},{12,8},{16,28},{20,16},{24,20},{28,24},{32,44},... | collective-permute-start | bytes 589832 | tf_op jit(solution)/shard_map/columns/ppermute | solution.py:413
  133.4 10.5 %collective-permute-start.13 = (bf16[256,384]{1,0:T(8,128)(2,1)}, bf16[256,384]{1,0:T(8,128)(2,1)S(1)}, u32[]{:S(2)}, u32[]{:S(2)}) collective-permute-start(bf16[256,384]{1,0:T(8,128)(2,1)} %get-tuple-element.37), channel_id=1, source_target_pairs={{0,12},{4,0},{8,4},{12,8},{16,28},{20,16},{24,20},{28,24},{32,44},... | collective-permute-start | bytes 589832 | tf_op jit(solution)/shard_map/schur/ppermute | solution.py:413
  136.1 7.9 %collective-permute-start.14 = (bf16[256,384]{1,0:T(8,128)(2,1)}, bf16[256,384]{1,0:T(8,128)(2,1)S(1)}, u32[]{:S(2)}, u32[]{:S(2)}) collective-permute-start(bf16[256,384]{1,0:T(8,128)(2,1)} %get-tuple-element.38), channel_id=1, source_target_pairs={{0,8},{4,12},{8,0},{12,4},{16,24},{20,28},{24,16},{28,20},{32,40},... | collective-permute-start | bytes 589832 | tf_op jit(solution)/shard_map/schur/ppermute | solution.py:413
  136.3 10.4 %collective-permute-start.15 = (bf16[256,384]{1,0:T(8,128)(2,1)S(1)}, bf16[256,384]{1,0:T(8,128)(2,1)S(1)}, u32[]{:S(2)}, u32[]{:S(2)}) collective-permute-start(bf16[256,384]{1,0:T(8,128)(2,1)S(1)} %get-tuple-element.39), channel_id=1, source_target_pairs={{0,4},{4,8},{8,12},{12,0},{16,20},{20,24},{24,28},{28,16},{32,36},... | collective-permute-start | bytes 589832 | tf_op jit(solution)/shard_map/schur/ppermute | solution.py:413
  136.9 16.9 %all-to-all-start.2 = ((bf16[16,24,640]{2,1,0:T(8,128)(2,1)}), bf16[16,24,640]{2,1,0:T(8,128)(2,1)S(1)}, u32[]{:S(2)}, u32[]{:S(2)}) async-start(bf16[16,24,640]{2,1,0:T(8,128)(2,1)} %bitcast.18), calls=%async_computation.2 | async-start | bytes 983040 | tf_op jit(solution)/shard_map/schur/all_to_all | solution.py:498
  143.9 66.9 %all-gather.7.cloned.1.call-start = ((), (), s32[]{:S(2)}) async-start(), calls=%async_computation.8 | async-start | bytes 3342336 | tf_op jit(solution)/shard_map/schur/all_gather | solution.py:496
  155.0 20.6 %all-to-all-start.3 = ((f32[16,24,640]{2,1,0:T(8,128)}), f32[16,24,640]{2,1,0:T(8,128)S(1)}, u32[]{:S(2)}, u32[]{:S(2)}) async-start(f32[16,24,640]{2,1,0:T(8,128)} %broadcast_in_dim.12), calls=%async_computation.3 | async-start | bytes 1966080 | tf_op jit(solution)/shard_map/schur/all_to_all | solution.py:507
  175.6 27.9 %copy-start.5 = (bf16[3,256,2048]{2,1,0:T(8,128)(2,1)S(1)}, bf16[3,256,2048]{2,1,0:T(8,128)(2,1)}, u32[]{:S(2)}) copy-start(bf16[3,256,2048]{2,1,0:T(8,128)(2,1)} %channel.1.channel_ref) | copy-start | bytes 9437188
  205.7 45.4 %all-to-all-start.5 = ((bf16[16,3,16,2048]{3,2,1,0:T(8,128)(2,1)}), bf16[16,3,16,2048]{3,2,1,0:T(8,128)(2,1)}, u32[]{:S(2)}, u32[]{:S(2)}) async-start(bf16[16,3,16,2048]{3,2,1,0:T(8,128)(2,1)} %signal.1), calls=%async_computation.5 | async-start | bytes 6291456 | tf_op jit(solution)/shard_map/signal/all_to_all | solution.py:523
  210.8 1.9 copy-start.7
  218.3 2.7 copy-start.6
  218.3 35.4 %collective-permute-start.16 = (bf16[256,1024]{1,0:T(8,128)(2,1)}, bf16[256,1024]{1,0:T(8,128)(2,1)}, u32[]{:S(2)}, u32[]{:S(2)}) collective-permute-start(bf16[256,1024]{1,0:T(8,128)(2,1)} %get-tuple-element.44), channel_id=1, source_target_pairs={{0,1},{1,2},{2,3},{3,0},{4,5},{5,6},{6,7},{7,4},{8,9},{9,10},{10,1... | collective-permute-start | bytes 1572872 | tf_op jit(solution)/shard_map/update/ppermute | solution.py:420
  218.9 34.8 %collective-permute-start.17 = (bf16[256,1024]{1,0:T(8,128)(2,1)}, bf16[256,1024]{1,0:T(8,128)(2,1)}, u32[]{:S(2)}, u32[]{:S(2)}) collective-permute-start(bf16[256,1024]{1,0:T(8,128)(2,1)} %get-tuple-element.45), channel_id=1, source_target_pairs={{0,2},{1,3},{2,0},{3,1},{4,6},{5,7},{6,4},{7,5},{8,10},{9,11},{10,... | collective-permute-start | bytes 1572872 | tf_op jit(solution)/shard_map/update/ppermute | solution.py:420
  221.0 38.8 %copy-start.4 = (f32[3,256,1024]{2,1,0:T(8,128)S(1)}, f32[3,256,1024]{2,1,0:T(8,128)}, u32[]{:S(2)}) copy-start(f32[3,256,1024]{2,1,0:T(8,128)} %inverse_ref.1) | copy-start | bytes 9437188
  221.0 32.7 %collective-permute-start.18 = (bf16[256,1024]{1,0:T(8,128)(2,1)}, bf16[256,1024]{1,0:T(8,128)(2,1)}, u32[]{:S(2)}, u32[]{:S(2)}) collective-permute-start(bf16[256,1024]{1,0:T(8,128)(2,1)} %get-tuple-element.46), channel_id=1, source_target_pairs={{0,3},{1,0},{2,1},{3,2},{4,7},{5,4},{6,5},{7,6},{8,11},{9,8},{10,9... | collective-permute-start | bytes 1572872 | tf_op jit(solution)/shard_map/update/ppermute | solution.py:420
  254.4 14.9 %all-to-all-start.6 = ((f32[64,1,3]{2,1,0:T(1,128)}), f32[64,1,3]{2,1,0:T(1,128)}, u32[]{:S(2)}, u32[]{:S(2)}) async-start(f32[64,1,3]{2,1,0:T(1,128)} %broadcast_in_dim.13), calls=%async_computation.6 | async-start | bytes 65536 | tf_op jit(solution)/shard_map/signal/all_to_all | solution.py:528
  262.8 8.2 %copy-start.1 = (bf16[3,1024,256]{2,1,0:T(8,128)(2,1)S(1)}, bf16[3,1024,256]{2,1,0:T(8,128)(2,1)}, u32[]{:S(2)}) copy-start(bf16[3,1024,256]{2,1,0:T(8,128)(2,1)} %param.13) | copy-start | bytes 4718596
Sparse Core Ops, SparseCore 0:
  12.3 73.6 all-gather.4
  147.6 56.3 all-gather.6

commit v4 on v2

--- a/solution.py
+++ b/solution.py
@@ -11,7 +11,7 @@
 STREAMS = 256
 TOTAL = ARRIVE * EPOCHS
 BLOCK = 128
-PANEL = 8
+PANEL = 16
 WINDOW = 48
 SHARE = TOTAL // 16
 
@@ -232,6 +232,28 @@
         cost_estimate=cost(2_000_000_000, 8_000_000),
         name="middle",
     )(where, square, *by_row, *by_col[1:], base)
+
+
+def ready_kernel(row_ref, shared_ref, out_ref):
+    total = jnp.sum(shared_ref[...].astype(f32), axis=0)
+    ids = row_ref[0] * SHARE + lax.broadcasted_iota(jnp.int32, (SHARE, TOTAL), 0)
+    lanes = lax.broadcasted_iota(jnp.int32, (SHARE, TOTAL), 1)
+    schur = loading * (ids == lanes).astype(f32) - total[:, :TOTAL]
+    for n in range(out_ref.shape[0]):
+        out_ref[n, :, :TOTAL] = schur
+        out_ref[n, :, TOTAL:] = total[:, TOTAL:]
+
+
+def make_ready(row, shared):
+    return pl.pallas_call(
+        ready_kernel,
+        out_shape=jax.ShapeDtypeStruct(shared.shape, f32),
+        in_specs=[SMEM, VMEM],
+        out_specs=VMEM,
+        compiler_params=params(16),
+        cost_estimate=cost(500_000_000, 2_000_000),
+        name="ready",
+    )(row, shared)
 
 
 def invert_block(a):
@@ -494,14 +516,7 @@
         weighted_all = lax.all_gather(weighted.astype(bf16), "row")
         packed = packed.reshape(16, SHARE, TOTAL + STREAMS)
         shared = lax.all_to_all(packed, "row", 0, 0, tiled=True)
-        shared = jnp.sum(shared.astype(f32), axis=0)
-        share_ids = row_index * SHARE + jnp.arange(SHARE, dtype=jnp.int32)
-        identity = loading * (
-            share_ids[:, None] == jnp.arange(TOTAL, dtype=jnp.int32)[None, :]
-        ).astype(f32)
-        schur_rows = identity - shared[:, :TOTAL]
-        ready = jnp.concatenate([schur_rows, shared[:, TOTAL:]], axis=1)
-        ready = jnp.broadcast_to(ready[None], (16, SHARE, TOTAL + STREAMS))
+        ready = make_ready(row_index.reshape(1), shared)
         whole = lax.all_to_all(ready, "row", 0, 0, tiled=True).reshape(TOTAL, TOTAL + STREAMS)
 
     with jax.named_scope("users"):

time: 273 us -> 276 us (1.011)
  blocking collectives: 10.5 us -> 25.4 us
  starting transfers between devices: 58 us -> 52.7 us
  waiting for transfers between devices: 113 us -> 109 us
    all_to_all x0 -> x1, blocking collectives: none -> 14.9 us  [local(): shared = lax.all_to_all(packed, 'row', 0, 0, tiled=True)]
    all_to_all x1 -> x0, starting transfers between devices: 5.45 us -> none  [local(): shared = lax.all_to_all(packed, 'row', 0, 0, tiled=True)]
    all_to_all x1 -> x0, waiting for transfers between devices: 5.03 us -> none  [local(): shared = lax.all_to_all(packed, 'row', 0, 0, tiled=True)]
    ppermute x9, waiting for transfers between devices: 19.6 us -> 22.5 us  [along_x(): return lax.ppermute(value, 'row', pairs)]
  transfers between devices with their start and end apart: 25 -> 24, of which waited for: 13 -> 14; matrix products, arithmetic and copies ran while one was open for 8% -> 7% of each run, Pallas kernels for 11% -> 11%
where the time goes in v4:
time: 276 us; the launch traced here: 275 us
  waiting for transfers between devices  109 us (39%)
  starting transfers between devices  52.7 us (19%)
  Pallas kernels  42.7 us (15%)
  blocking collectives  25.4 us (9%)
  other arithmetic  20.4 us (7%)
  between operations  14.4 us (5%)
  local copies, waits for them, and re-layouts  9.15 us (3%)
    all_to_all x1, waiting for transfers between devices, local(): received = lax.all_to_all(signal_part, 'row', 0, 0, tiled=True)  24.6 us
    all_to_all x2, waiting for transfers between devices, to_planes(): return lax.all_to_all(padded, 'col', 0, 0, tiled=True)  23.5 us
    ppermute x9, waiting for transfers between devices, along_x(): return lax.ppermute(value, 'row', pairs)  22.5 us
    all_to_all x1, blocking collectives, local(): shared = lax.all_to_all(packed, 'row', 0, 0, tiled=True)  14.9 us
    ppermute x9, starting transfers between devices, along_x(): return lax.ppermute(value, 'row', pairs)  14.3 us
    all_to_all x1, waiting for transfers between devices, local(): both = lax.all_to_all(both, 'col', 0, 0, tiled=True)  14 us
    pallas_call x1, Pallas kernels, make_solve(): pl.pallas_call(solve_kernel, out_shape=(jax.ShapeDtypeStruct((EPOCHS, BLO...  12.1 us
    all_to_all x2, starting transfers between devices, to_planes(): return lax.all_to_all(padded, 'col', 0, 0, tiled=True)  10.6 us
  transfers between devices with their start and end apart: 24, of which 14 were waited for; matrix products, arithmetic and copies ran while one was open for 7% of the time, Pallas kernels for 11%

profile of v4, /device:TPU:0, one launch (start us, length us, event | category | flops | bytes accessed | tf_op | source)
XLA Modules:
  0.0 275.1 jit_solution(2967544243199225580)
XLA Ops:
  7.2 1.1 constant_dynamic-slice_fusion.1
  8.4 1.6 collective-permute-done
  10.0 1.0 select_bitcast_fusion.1
  11.3 0.8 pad.6
  12.2 1.9 copy-done.2
  14.3 3.2 %collective-permute-start.2 = (bf16[3,256,256]{2,1,0:T(8,128)(2,1)S(1)}, bf16[3,256,256]{2,1,0:T(8,128)(2,1)S(1)}, u32[]{:S(2)}, u32[]{:S(2)}) collective-permute-start(bf16[3,256,256]{2,1,0:T(8,128)(2,1)S(1)} %get-tuple-element.29), channel_id=1, source_target_pairs={{0,8},{4,12},{8,0},{12,4},{16,24},{20,28},{24,16},{28,20},{32,40},... | collective-permute-start | bytes 1179656 | tf_op jit(solution)/shard_map/planes/ppermute | solution.py:434
  17.5 1.1 collective-permute-start.3
  18.6 0.9 collective-permute-start.1
  19.5 1.6 fusion.20
  21.2 1.1 concatenate.7
  22.3 5.3 %all-to-all-start.1 = ((f32[4,256,256]{2,1,0:T(8,128)}), f32[4,256,256]{2,1,0:T(8,128)}, u32[]{:S(2)}, u32[]{:S(2)}) async-start(f32[4,256,256]{2,1,0:T(8,128)} %concatenate.7), calls=%async_computation.1 | async-start | bytes 2097152 | tf_op jit(solution)/shard_map/planes/all_to_all | solution.py:445
  27.6 1.0 collective-permute-done.2
  28.6 14.6 %collective-permute-done.3 = bf16[3,256,256]{2,1,0:T(8,128)(2,1)} collective-permute-done((bf16[3,256,256]{2,1,0:T(8,128)(2,1)S(1)}, bf16[3,256,256]{2,1,0:T(8,128)(2,1)}, u32[]{:S(2)}, u32[]{:S(2)}) %collective-permute-start.3) | collective-permute-done | bytes 393248 | tf_op jit(solution)/shard_map/planes/ppermute | solution.py:434
  43.2 2.5 fusion.6
  45.6 5.3 %all-to-all-start = ((bf16[4,4,256,256]{3,2,1,0:T(8,128)(2,1)}), bf16[4,4,256,256]{3,2,1,0:T(8,128)(2,1)S(1)}, u32[]{:S(2)}, u32[]{:S(2)}) async-start(bf16[4,4,256,256]{3,2,1,0:T(8,128)(2,1)} %fusion.6), calls=%async_computation | async-start | bytes 4194304 | tf_op jit(solution)/shard_map/planes/all_to_all | solution.py:445
  51.6 0.6 fusion.17.place_ref
  52.2 1.6 reduce_sum.67.precoded_ref
  53.8 23.5 %all-to-all-done.square_ref = bf16[4,4,256,256]{3,2,1,0:T(8,128)(2,1)S(1)} async-done(((bf16[4,4,256,256]{3,2,1,0:T(8,128)(2,1)}), bf16[4,4,256,256]{3,2,1,0:T(8,128)(2,1)S(1)}, u32[]{:S(2)}, u32[]{:S(2)}) %all-to-all-start) | async-done | bytes 2097184 | tf_op jit(solution)/shard_map/planes/all_to_all | solution.py:445
  77.3 8.7 %all-gather.5.cloned.1.call-done = bf16[1792,2048]{1,0:T(8,128)(2,1)} async-done(((bf16[112,2048]{1,0:T(8,128)(2,1)}), bf16[1792,2048]{1,0:T(8,128)(2,1)}) %all-gather.5.cloned.1.call-update) | async-done | bytes 7340048 | tf_op jit(solution)/shard_map/newcomers/all_gather | solution.py:462
  86.0 9.7 %columns.1 = bf16[4,304,384]{2,1,0:T(8,128)(2,1)} custom-call(s32[1]{0:T(128)} %bitcast.2.row_ref, bf16[16,112,2048]{2,1,0:T(8,128)(2,1)} %bitcast.72, bf16[3,256,2048]{2,1,0:T(8,128)(2,1)} %channel_ref.3, s32[3,1,384]{2,1,0:T(1,128)} %fusion.17.place_ref), custom_call_target="tpu_custom_call" | custom-call | flops 4000000000 | bytes 12000000 | tf_op jit(solution)/shard_map/columns/columns/pallas_call | solution.py:115
  95.7 4.4 %all-to-all-start.2 = ((bf16[4,304,384]{2,1,0:T(8,128)(2,1)}), bf16[4,304,384]{2,1,0:T(8,128)(2,1)}, u32[]{:S(2)}, u32[]{:S(2)}) async-start(bf16[4,304,384]{2,1,0:T(8,128)(2,1)} %columns.1), calls=%async_computation.2 | async-start | bytes 1867776 | tf_op jit(solution)/shard_map/columns/all_to_all | solution.py:503
  100.2 14.0 %all-to-all-done.2 = bf16[4,304,384]{2,1,0:T(8,128)(2,1)} async-done(((bf16[4,304,384]{2,1,0:T(8,128)(2,1)}), bf16[4,304,384]{2,1,0:T(8,128)(2,1)}, u32[]{:S(2)}, u32[]{:S(2)}) %all-to-all-start.2) | async-done | bytes 933920 | tf_op jit(solution)/shard_map/columns/all_to_all | solution.py:503
  114.2 1.4 convert_reduce_fusion.1.summed_ref
  115.6 1.5 collective-permute-start.4
  117.1 0.7 dynamic-slice_bitcast_fusion.1.place_ref
  117.8 2.7 collective-permute-start.5
  120.5 1.4 collective-permute-start.6
  121.9 1.2 collective-permute-start.7
  123.1 1.1 collective-permute-start.8
  124.3 3.8 %collective-permute-start.9 = (bf16[256,384]{1,0:T(8,128)(2,1)S(1)}, bf16[256,384]{1,0:T(8,128)(2,1)S(1)}, u32[]{:S(2)}, u32[]{:S(2)}) collective-permute-start(bf16[256,384]{1,0:T(8,128)(2,1)S(1)} %slice.58.own_ref), channel_id=1, source_target_pairs={{0,16},{4,20},{8,24},{12,28},{16,32},{20,36},{24,40},{28,44},{32,4... | collective-permute-start | bytes 589832 | tf_op jit(solution)/shard_map/columns/ppermute | solution.py:438
  128.1 1.0 target.1.base_ref
  129.1 2.1 collective-permute-done.8.col2_ref
  131.2 2.1 collective-permute-done.9.col3_ref
  133.3 2.7 middle.1
  136.3 2.0 collective-permute-start.11
  138.3 1.1 collective-permute-start.12
  139.5 3.0 %collective-permute-done.10 = bf16[256,384]{1,0:T(8,128)(2,1)S(1)} collective-permute-done((bf16[256,384]{1,0:T(8,128)(2,1)S(1)}, bf16[256,384]{1,0:T(8,128)(2,1)S(1)}, u32[]{:S(2)}, u32[]{:S(2)}) %collective-permute-start.10) | collective-permute-done | bytes 196640 | tf_op jit(solution)/shard_map/schur/ppermute | solution.py:434
  142.4 1.5 collective-permute-done.11
  143.9 2.6 collective-permute-done.12
  146.5 0.8 fusion.19
  147.3 14.9 %all_to_all.40.shared_ref = bf16[16,24,640]{2,1,0:T(8,128)(2,1)S(1)} all-to-all(bf16[16,24,640]{2,1,0:T(8,128)(2,1)S(1)} %bitcast.62), channel_id=1, replica_groups=mesh['grp'=2,'row'=16,'col'=4] {'row'}, dimensions={0} | all-to-all | bytes 983040 | tf_op jit(solution)/shard_map/schur/all_to_all | solution.py:518
  162.2 1.1 ready.1
  163.2 3.6 %all-to-all-start.4 = ((f32[16,24,640]{2,1,0:T(8,128)}), f32[16,24,640]{2,1,0:T(8,128)S(1)}, u32[]{:S(2)}, u32[]{:S(2)}) async-start(f32[16,24,640]{2,1,0:T(8,128)} %ready.1), calls=%async_computation.4 | async-start | bytes 1966080 | tf_op jit(solution)/shard_map/schur/all_to_all | solution.py:520
  167.5 8.2 %channel.1.channel_ref = bf16[3,256,2048]{2,1,0:T(8,128)(2,1)} custom-call(s32[1]{0:T(128)} %bitcast.1.first_ref, bf16[16,112,2048]{2,1,0:T(8,128)(2,1)} %bitcast.73, bf16[3,256,2048]{2,1,0:T(8,128)(2,1)} %channel_ref.3, s32[3,1,384]{2,1,0:T(1,128)} %fusion.17.place_ref, s32[3,1,384]{2,1,0:T(1,128)} %reshape.280.slots_ref), custom_call_target="tpu_custom_call" | custom-call | flops 4000000000 | bytes 14000000 | tf_op jit(solution)/shard_map/users/channel/pallas_call | solution.py:143
  175.7 5.0 %all-to-all-done.4 = f32[16,24,640]{2,1,0:T(8,128)S(1)} async-done(((f32[16,24,640]{2,1,0:T(8,128)}), f32[16,24,640]{2,1,0:T(8,128)S(1)}, u32[]{:S(2)}, u32[]{:S(2)}) %all-to-all-start.4) | async-done | bytes 983072 | tf_op jit(solution)/shard_map/schur/all_to_all | solution.py:520
  180.7 12.1 %solve.1 = (f32[3,128,128]{2,1,0:T(8,128)S(1)}, bf16[4,256,256]{2,1,0:T(8,128)(2,1)S(1)}) custom-call(s32[1]{0:T(128)} %bitcast.1.first_ref, f32[384,640]{1,0:T(8,128)S(1)} %bitcast.60, f32[256,384]{1,0:T(8,128)S(1)} %get-tuple-element.53.weighted_ref, f32[256,256]{1,0:T(8,128)S(1)} %reduce_sum.67.precoded_ref, s32[1,384]{1,0:T(1,128)S(1)} %bitcast.65), custom_call_target="tpu_custom_call" | custom-call | flops 14000000000 | bytes 4000000 | tf_op jit(solution)/shard_map/users/solve/pallas_call | solution.py:319
  192.9 10.5 %all_to_all.41.users_ref = bf16[4,256,256]{2,1,0:T(8,128)(2,1)S(1)} all-to-all(bf16[4,256,256]{2,1,0:T(8,128)(2,1)S(1)} %get-tuple-element.40), channel_id=1, replica_groups=mesh['grp'=2,'row'=16,'col'=4] {'col'}, dimensions={0} | all-to-all | bytes 1048576 | tf_op jit(solution)/shard_map/users/all_to_all | solution.py:526
  203.4 2.1 signal.1
  205.5 4.5 %all-to-all-start.6 = ((bf16[16,3,16,2048]{3,2,1,0:T(8,128)(2,1)}), bf16[16,3,16,2048]{3,2,1,0:T(8,128)(2,1)}, u32[]{:S(2)}, u32[]{:S(2)}) async-start(bf16[16,3,16,2048]{3,2,1,0:T(8,128)(2,1)} %signal.1), calls=%async_computation.6 | async-start | bytes 6291456 | tf_op jit(solution)/shard_map/signal/all_to_all | solution.py:536
  210.7 1.9 copy-done.7
  212.5 5.6 %update.1 = (bf16[256,1024]{1,0:T(8,128)(2,1)S(1)}, bf16[256,1024]{1,0:T(8,128)(2,1)}, bf16[256,1024]{1,0:T(8,128)(2,1)}, bf16[256,1024]{1,0:T(8,128)(2,1)}) custom-call(s32[2]{0:T(128)S(1)} %pad_add_fusion.1.where_ref, f32[256,384]{1,0:T(8,128)S(1)} %get-tuple-element.53.weighted_ref, f32[384,640]{1,0:T(8,128)S(1)} %bitcast.61, ...), custom_call_target="tpu_custom_call" | custom-call | flops 1500000000 | bytes 8000000 | tf_op jit(solution)/shard_map/update/update/pallas_call | solution.py:406
  218.2 0.6 collective-permute-start.13
  218.8 2.1 collective-permute-start.14
  220.9 0.8 collective-permute-start.15
  221.7 2.1 and_select_fusion
  223.7 24.6 %all-to-all-done.6 = bf16[16,3,16,2048]{3,2,1,0:T(8,128)(2,1)} async-done(((bf16[16,3,16,2048]{3,2,1,0:T(8,128)(2,1)}), bf16[16,3,16,2048]{3,2,1,0:T(8,128)(2,1)}, u32[]{:S(2)}, u32[]{:S(2)}) %all-to-all-start.6) | async-done | bytes 3145760 | tf_op jit(solution)/shard_map/signal/all_to_all | solution.py:536
  248.3 2.5 convert_reduce_fusion
  251.0 0.6 broadcast_in_dim.10
  251.6 5.4 %all-to-all-start.7 = ((f32[64,1,3]{2,1,0:T(1,128)}), f32[64,1,3]{2,1,0:T(1,128)}, u32[]{:S(2)}, u32[]{:S(2)}) async-start(f32[64,1,3]{2,1,0:T(1,128)} %broadcast_in_dim.10), calls=%async_computation.7 | async-start | bytes 65536 | tf_op jit(solution)/shard_map/signal/all_to_all | solution.py:541
  257.0 3.0 %fusion.15 = (f32[1,256,1024]{2,1,0:T(8,128)S(1)}, f32[1,256,1024]{2,1,0:T(8,128)S(1)}, f32[1,256,1024]{2,1,0:T(8,128)S(1)}) fusion(f32[3,256,1024]{2,1,0:T(8,128)} %and_select_fusion, f32[3,256,1024]{2,1,0:T(8,128)S(1)} %copy-done.4, bf16[256,1024]{1,0:T(8,128)(2,1)} %collective-permute-done.15, bf16[256,1024]{1,0:T(8,128)(2,1)} %collective-permute-done.14, ...), kind=kLoop, calls=%fused_computation.24 | loop fusion | flops 4718592 | bytes 11534345 | tf_op jit(solution)/shard_map/final/stack | solution.py:558
  260.0 1.9 pad_maximum_fusion
  261.9 4.6 %all-to-all-done.7 = f32[64,1,3]{2,1,0:T(1,128)} async-done(((f32[64,1,3]{2,1,0:T(1,128)}), f32[64,1,3]{2,1,0:T(1,128)}, u32[]{:S(2)}, u32[]{:S(2)}) %all-to-all-start.7) | async-done | bytes 800 | tf_op jit(solution)/shard_map/signal/all_to_all | solution.py:541
  266.5 0.8 reduce_sum.75
  267.4 0.8 multiply_bitcast_fusion
  (66 shorter events, 3.2 us)
Async XLA Ops:
  7.2 12.4 %copy-start = (bf16[3,1024,256]{2,1,0:T(8,128)(2,1)S(1)}, bf16[3,1024,256]{2,1,0:T(8,128)(2,1)}, u32[]{:S(2)}) copy-start(bf16[3,1024,256]{2,1,0:T(8,128)(2,1)} %param.13) | copy-start | bytes 4718596
  7.2 78.8 %all-gather.5.cloned.1.call-start = ((), (), s32[]{:S(2)}) async-start(), calls=%async_computation.8 | async-start | bytes 7798784 | tf_op jit(solution)/shard_map/newcomers/all_gather | solution.py:462
  8.3 1.7 collective-permute-start
  12.2 1.9 copy-start.2
  14.1 5.4 %copy-start.3 = (f32[3,256,1024]{2,1,0:T(8,128)S(1)}, f32[3,256,1024]{2,1,0:T(8,128)}, u32[]{:S(2)}) copy-start(f32[3,256,1024]{2,1,0:T(8,128)} %inverse_ref.1) | copy-start | bytes 9437188
  14.3 14.3 %collective-permute-start.2 = (bf16[3,256,256]{2,1,0:T(8,128)(2,1)S(1)}, bf16[3,256,256]{2,1,0:T(8,128)(2,1)S(1)}, u32[]{:S(2)}, u32[]{:S(2)}) collective-permute-start(bf16[3,256,256]{2,1,0:T(8,128)(2,1)S(1)} %get-tuple-element.29), channel_id=1, source_target_pairs={{0,8},{4,12},{8,0},{12,4},{16,24},{20,28},{24,16},{28,20},{32,40},... | collective-permute-start | bytes 1179656 | tf_op jit(solution)/shard_map/planes/ppermute | solution.py:434
  17.5 25.7 %collective-permute-start.3 = (bf16[3,256,256]{2,1,0:T(8,128)(2,1)S(1)}, bf16[3,256,256]{2,1,0:T(8,128)(2,1)}, u32[]{:S(2)}, u32[]{:S(2)}) collective-permute-start(bf16[3,256,256]{2,1,0:T(8,128)(2,1)S(1)} %get-tuple-element.30), channel_id=1, source_target_pairs={{0,12},{4,0},{8,4},{12,8},{16,28},{20,16},{24,20},{28,24},{32,44},... | collective-permute-start | bytes 1179656 | tf_op jit(solution)/shard_map/planes/ppermute | solution.py:434
  18.6 24.5 %collective-permute-start.1 = (bf16[3,256,256]{2,1,0:T(8,128)(2,1)S(1)}, bf16[3,256,256]{2,1,0:T(8,128)(2,1)}, u32[]{:S(2)}, u32[]{:S(2)}) collective-permute-start(bf16[3,256,256]{2,1,0:T(8,128)(2,1)S(1)} %get-tuple-element.28), channel_id=1, source_target_pairs={{0,4},{4,8},{8,12},{12,0},{16,20},{20,24},{24,28},{28,16},{32,36},... | collective-permute-start | bytes 1179656 | tf_op jit(solution)/shard_map/planes/ppermute | solution.py:434
  22.3 23.3 %all-to-all-start.1 = ((f32[4,256,256]{2,1,0:T(8,128)}), f32[4,256,256]{2,1,0:T(8,128)}, u32[]{:S(2)}, u32[]{:S(2)}) async-start(f32[4,256,256]{2,1,0:T(8,128)} %concatenate.7), calls=%async_computation.1 | async-start | bytes 2097152 | tf_op jit(solution)/shard_map/planes/all_to_all | solution.py:445
  43.2 7.8 %copy-start.9 = (s32[6,3,128,1]{2,3,1,0:T(1,128)S(1)}, s32[6,3,128,1]{2,3,1,0:T(1,128)}, u32[]{:S(2)}) copy-start(s32[6,3,128,1]{2,3,1,0:T(1,128)} %param.10) | copy-start | bytes 27652
  43.2 8.1 %copy-start.10 = (s32[32]{0:T(128)S(1)}, s32[32]{0:T(128)}, u32[]{:S(2)}) copy-start(s32[32]{0:T(128)} %param.11) | copy-start | bytes 388
  45.6 31.7 %all-to-all-start = ((bf16[4,4,256,256]{3,2,1,0:T(8,128)(2,1)}), bf16[4,4,256,256]{3,2,1,0:T(8,128)(2,1)S(1)}, u32[]{:S(2)}, u32[]{:S(2)}) async-start(bf16[4,4,256,256]{3,2,1,0:T(8,128)(2,1)} %fusion.6), calls=%async_computation | async-start | bytes 4194304 | tf_op jit(solution)/shard_map/planes/all_to_all | solution.py:445
  95.7 21.4 %copy-start.8 = (s32[6,3,128]{2,1,0:T(4,128)S(1)}, s32[6,3,128]{2,1,0:T(4,128)}, u32[]{:S(2)}) copy-start(s32[6,3,128]{2,1,0:T(4,128)} %param.12) | copy-start | bytes 27652
  95.7 18.5 %all-to-all-start.2 = ((bf16[4,304,384]{2,1,0:T(8,128)(2,1)}), bf16[4,304,384]{2,1,0:T(8,128)(2,1)}, u32[]{:S(2)}, u32[]{:S(2)}) async-start(bf16[4,304,384]{2,1,0:T(8,128)(2,1)} %columns.1), calls=%async_computation.2 | async-start | bytes 1867776 | tf_op jit(solution)/shard_map/columns/all_to_all | solution.py:503
  100.2 110.5 %all-gather.7.cloned.1.call-start = ((), (), s32[]{:S(2)}) async-start(), calls=%async_computation.9 | async-start | bytes 3342336 | tf_op jit(solution)/shard_map/schur/all_gather | solution.py:516
  115.6 8.7 %collective-permute-start.4 = (bf16[256,384]{1,0:T(8,128)(2,1)S(1)}, bf16[256,384]{1,0:T(8,128)(2,1)S(1)}, u32[]{:S(2)}, u32[]{:S(2)}) collective-permute-start(bf16[256,384]{1,0:T(8,128)(2,1)S(1)} %slice.58.own_ref), channel_id=1, source_target_pairs={{0,4},{4,8},{8,12},{12,0},{16,20},{20,24},{24,28},{28,16},{32,36},... | collective-permute-start | bytes 589832 | tf_op jit(solution)/shard_map/columns/ppermute | solution.py:434
  117.8 11.3 %collective-permute-start.5 = (bf16[256,384]{1,0:T(8,128)(2,1)S(1)}, bf16[256,384]{1,0:T(8,128)(2,1)S(1)}, u32[]{:S(2)}, u32[]{:S(2)}) collective-permute-start(bf16[256,384]{1,0:T(8,128)(2,1)S(1)} %slice.58.own_ref), channel_id=1, source_target_pairs={{0,8},{4,12},{8,0},{12,4},{16,24},{20,28},{24,16},{28,20},{32,40},... | collective-permute-start | bytes 589832 | tf_op jit(solution)/shard_map/columns/ppermute | solution.py:434
  120.5 8.6 %collective-permute-start.6 = (bf16[256,384]{1,0:T(8,128)(2,1)S(1)}, bf16[256,384]{1,0:T(8,128)(2,1)S(1)}, u32[]{:S(2)}, u32[]{:S(2)}) collective-permute-start(bf16[256,384]{1,0:T(8,128)(2,1)S(1)} %slice.58.own_ref), channel_id=1, source_target_pairs={{0,12},{4,0},{8,4},{12,8},{16,28},{20,16},{24,20},{28,24},{32,44},... | collective-permute-start | bytes 589832 | tf_op jit(solution)/shard_map/columns/ppermute | solution.py:434
  121.9 7.2 %collective-permute-start.7 = (bf16[256,384]{1,0:T(8,128)(2,1)S(1)}, bf16[256,384]{1,0:T(8,128)(2,1)S(1)}, u32[]{:S(2)}, u32[]{:S(2)}) collective-permute-start(bf16[256,384]{1,0:T(8,128)(2,1)S(1)} %slice.58.own_ref), channel_id=1, source_target_pairs={{0,48},{4,52},{8,56},{12,60},{16,0},{20,4},{24,8},{28,12},{32,16},... | collective-permute-start | bytes 589832 | tf_op jit(solution)/shard_map/columns/ppermute | solution.py:438
  123.1 8.1 %collective-permute-start.8 = (bf16[256,384]{1,0:T(8,128)(2,1)S(1)}, bf16[256,384]{1,0:T(8,128)(2,1)S(1)}, u32[]{:S(2)}, u32[]{:S(2)}) collective-permute-start(bf16[256,384]{1,0:T(8,128)(2,1)S(1)} %slice.58.own_ref), channel_id=1, source_target_pairs={{0,32},{4,36},{8,40},{12,44},{16,48},{20,52},{24,56},{28,60},{32,0... | collective-permute-start | bytes 589832 | tf_op jit(solution)/shard_map/columns/ppermute | solution.py:438
  124.3 9.1 %collective-permute-start.9 = (bf16[256,384]{1,0:T(8,128)(2,1)S(1)}, bf16[256,384]{1,0:T(8,128)(2,1)S(1)}, u32[]{:S(2)}, u32[]{:S(2)}) collective-permute-start(bf16[256,384]{1,0:T(8,128)(2,1)S(1)} %slice.58.own_ref), channel_id=1, source_target_pairs={{0,16},{4,20},{8,24},{12,28},{16,32},{20,36},{24,40},{28,44},{32,4... | collective-permute-start | bytes 589832 | tf_op jit(solution)/shard_map/columns/ppermute | solution.py:438
  136.0 6.4 %collective-permute-start.10 = (bf16[256,384]{1,0:T(8,128)(2,1)S(1)}, bf16[256,384]{1,0:T(8,128)(2,1)S(1)}, u32[]{:S(2)}, u32[]{:S(2)}) collective-permute-start(bf16[256,384]{1,0:T(8,128)(2,1)S(1)} %get-tuple-element.37), channel_id=1, source_target_pairs={{0,12},{4,0},{8,4},{12,8},{16,28},{20,16},{24,20},{28,24},{32,44},... | collective-permute-start | bytes 589832 | tf_op jit(solution)/shard_map/schur/ppermute | solution.py:434
  136.3 7.5 %collective-permute-start.11 = (bf16[256,384]{1,0:T(8,128)(2,1)S(1)}, bf16[256,384]{1,0:T(8,128)(2,1)S(1)}, u32[]{:S(2)}, u32[]{:S(2)}) collective-permute-start(bf16[256,384]{1,0:T(8,128)(2,1)S(1)} %get-tuple-element.38), channel_id=1, source_target_pairs={{0,8},{4,12},{8,0},{12,4},{16,24},{20,28},{24,16},{28,20},{32,40},... | collective-permute-start | bytes 589832 | tf_op jit(solution)/shard_map/schur/ppermute | solution.py:434
  138.3 8.1 %collective-permute-start.12 = (bf16[256,384]{1,0:T(8,128)(2,1)S(1)}, bf16[256,384]{1,0:T(8,128)(2,1)S(1)}, u32[]{:S(2)}, u32[]{:S(2)}) collective-permute-start(bf16[256,384]{1,0:T(8,128)(2,1)S(1)} %get-tuple-element.39), channel_id=1, source_target_pairs={{0,4},{4,8},{8,12},{12,0},{16,20},{20,24},{24,28},{28,16},{32,36},... | collective-permute-start | bytes 589832 | tf_op jit(solution)/shard_map/schur/ppermute | solution.py:434
  163.2 17.5 %all-to-all-start.4 = ((f32[16,24,640]{2,1,0:T(8,128)}), f32[16,24,640]{2,1,0:T(8,128)S(1)}, u32[]{:S(2)}, u32[]{:S(2)}) async-start(f32[16,24,640]{2,1,0:T(8,128)} %ready.1), calls=%async_computation.4 | async-start | bytes 1966080 | tf_op jit(solution)/shard_map/schur/all_to_all | solution.py:520
  180.7 22.6 %copy-start.5 = (bf16[3,256,2048]{2,1,0:T(8,128)(2,1)S(1)}, bf16[3,256,2048]{2,1,0:T(8,128)(2,1)}, u32[]{:S(2)}) copy-start(bf16[3,256,2048]{2,1,0:T(8,128)(2,1)} %channel.1.channel_ref) | copy-start | bytes 9437188
  205.5 42.8 %all-to-all-start.6 = ((bf16[16,3,16,2048]{3,2,1,0:T(8,128)(2,1)}), bf16[16,3,16,2048]{3,2,1,0:T(8,128)(2,1)}, u32[]{:S(2)}, u32[]{:S(2)}) async-start(bf16[16,3,16,2048]{3,2,1,0:T(8,128)(2,1)} %signal.1), calls=%async_computation.6 | async-start | bytes 6291456 | tf_op jit(solution)/shard_map/signal/all_to_all | solution.py:536
  210.6 1.9 copy-start.7
  218.1 2.7 copy-start.6
  218.2 32.8 %collective-permute-start.13 = (bf16[256,1024]{1,0:T(8,128)(2,1)}, bf16[256,1024]{1,0:T(8,128)(2,1)}, u32[]{:S(2)}, u32[]{:S(2)}) collective-permute-start(bf16[256,1024]{1,0:T(8,128)(2,1)} %get-tuple-element.44), channel_id=1, source_target_pairs={{0,1},{1,2},{2,3},{3,0},{4,5},{5,6},{6,7},{7,4},{8,9},{9,10},{10,1... | collective-permute-start | bytes 1572872 | tf_op jit(solution)/shard_map/update/ppermute | solution.py:441
  218.8 32.2 %collective-permute-start.14 = (bf16[256,1024]{1,0:T(8,128)(2,1)}, bf16[256,1024]{1,0:T(8,128)(2,1)}, u32[]{:S(2)}, u32[]{:S(2)}) collective-permute-start(bf16[256,1024]{1,0:T(8,128)(2,1)} %get-tuple-element.45), channel_id=1, source_target_pairs={{0,2},{1,3},{2,0},{3,1},{4,6},{5,7},{6,4},{7,5},{8,10},{9,11},{10,... | collective-permute-start | bytes 1572872 | tf_op jit(solution)/shard_map/update/ppermute | solution.py:441
  220.9 36.2 %copy-start.4 = (f32[3,256,1024]{2,1,0:T(8,128)S(1)}, f32[3,256,1024]{2,1,0:T(8,128)}, u32[]{:S(2)}) copy-start(f32[3,256,1024]{2,1,0:T(8,128)} %inverse_ref.1) | copy-start | bytes 9437188
  220.9 30.1 %collective-permute-start.15 = (bf16[256,1024]{1,0:T(8,128)(2,1)}, bf16[256,1024]{1,0:T(8,128)(2,1)}, u32[]{:S(2)}, u32[]{:S(2)}) collective-permute-start(bf16[256,1024]{1,0:T(8,128)(2,1)} %get-tuple-element.46), channel_id=1, source_target_pairs={{0,3},{1,0},{2,1},{3,2},{4,7},{5,4},{6,5},{7,6},{8,11},{9,8},{10,9... | collective-permute-start | bytes 1572872 | tf_op jit(solution)/shard_map/update/ppermute | solution.py:441
  251.6 14.9 %all-to-all-start.7 = ((f32[64,1,3]{2,1,0:T(1,128)}), f32[64,1,3]{2,1,0:T(1,128)}, u32[]{:S(2)}, u32[]{:S(2)}) async-start(f32[64,1,3]{2,1,0:T(1,128)} %broadcast_in_dim.10), calls=%async_computation.7 | async-start | bytes 65536 | tf_op jit(solution)/shard_map/signal/all_to_all | solution.py:541
  260.0 8.2 %copy-start.1 = (bf16[3,1024,256]{2,1,0:T(8,128)(2,1)S(1)}, bf16[3,1024,256]{2,1,0:T(8,128)(2,1)}, u32[]{:S(2)}) copy-start(bf16[3,1024,256]{2,1,0:T(8,128)(2,1)} %param.13) | copy-start | bytes 4718596
Sparse Core Ops, SparseCore 0:
  12.3 73.6 all-gather.4
  147.4 49.3 all-gather.6

commit v5 on v2

--- a/solution.py
+++ b/solution.py
@@ -11,7 +11,7 @@
 STREAMS = 256
 TOTAL = ARRIVE * EPOCHS
 BLOCK = 128
-PANEL = 8
+PANEL = 16
 WINDOW = 48
 SHARE = TOTAL // 16
 

time: 273 us -> 272 us (level)
  no operation moved by 1% of the time
where the time goes in v5:
time: 272 us; the launch traced here: 271 us
  waiting for transfers between devices  113 us (42%)
  starting transfers between devices  58 us (21%)
  Pallas kernels  42.5 us (16%)
  other arithmetic  20.5 us (8%)
  between operations  14.4 us (5%)
  blocking collectives  10.5 us (4%)
  local copies, waits for them, and re-layouts  10.2 us (4%)
    all_to_all x1, waiting for transfers between devices, local(): received = lax.all_to_all(signal_part, 'row', 0, 0, tiled=True)  24.5 us
    all_to_all x2, waiting for transfers between devices, to_planes(): return lax.all_to_all(padded, 'col', 0, 0, tiled=True)  23.5 us
    ppermute x9, waiting for transfers between devices, along_x(): return lax.ppermute(value, 'row', pairs)  19.6 us
    ppermute x9, starting transfers between devices, along_x(): return lax.ppermute(value, 'row', pairs)  14.1 us
    all_to_all x1, waiting for transfers between devices, local(): both = lax.all_to_all(both, 'col', 0, 0, tiled=True)  14 us
    pallas_call x1, Pallas kernels, make_solve(): pl.pallas_call(solve_kernel, out_shape=(jax.ShapeDtypeStruct((EPOCHS, BLO...  12.2 us
    all_to_all x2, starting transfers between devices, to_planes(): return lax.all_to_all(padded, 'col', 0, 0, tiled=True)  10.6 us
    all_to_all x1, blocking collectives, local(): users_side = lax.all_to_all(users, 'col', 0, 0, tiled=True)  10.5 us
  transfers between devices with their start and end apart: 25, of which 13 were waited for; matrix products, arithmetic and copies ran while one was open for 8% of the time, Pallas kernels for 11%

profile of v5, /device:TPU:0, one launch (start us, length us, event | category | flops | bytes accessed | tf_op | source)
XLA Modules:
  0.0 270.7 jit_solution(1474245899764247450)
XLA Ops:
  7.2 1.1 constant_dynamic-slice_fusion.1
  8.4 1.6 collective-permute-done
  10.0 1.0 select_bitcast_fusion.1
  11.3 0.8 pad.6
  12.2 1.9 copy-done.2
  14.3 3.2 %collective-permute-start.2 = (bf16[3,256,256]{2,1,0:T(8,128)(2,1)S(1)}, bf16[3,256,256]{2,1,0:T(8,128)(2,1)S(1)}, u32[]{:S(2)}, u32[]{:S(2)}) collective-permute-start(bf16[3,256,256]{2,1,0:T(8,128)(2,1)S(1)} %get-tuple-element.29), channel_id=1, source_target_pairs={{0,8},{4,12},{8,0},{12,4},{16,24},{20,28},{24,16},{28,20},{32,40},... | collective-permute-start | bytes 1179656 | tf_op jit(solution)/shard_map/planes/ppermute | solution.py:412
  17.5 1.1 collective-permute-start.3
  18.6 0.9 collective-permute-start.1
  19.5 1.6 fusion.20
  21.2 1.1 concatenate.10
  22.3 5.3 %all-to-all-start.1 = ((f32[4,256,256]{2,1,0:T(8,128)}), f32[4,256,256]{2,1,0:T(8,128)}, u32[]{:S(2)}, u32[]{:S(2)}) async-start(f32[4,256,256]{2,1,0:T(8,128)} %concatenate.10), calls=%async_computation.1 | async-start | bytes 2097152 | tf_op jit(solution)/shard_map/planes/all_to_all | solution.py:423
  27.6 1.0 collective-permute-done.2
  28.6 14.6 %collective-permute-done.3 = bf16[3,256,256]{2,1,0:T(8,128)(2,1)} collective-permute-done((bf16[3,256,256]{2,1,0:T(8,128)(2,1)S(1)}, bf16[3,256,256]{2,1,0:T(8,128)(2,1)}, u32[]{:S(2)}, u32[]{:S(2)}) %collective-permute-start.3) | collective-permute-done | bytes 393248 | tf_op jit(solution)/shard_map/planes/ppermute | solution.py:412
  43.2 2.5 fusion.6
  45.6 5.3 %all-to-all-start = ((bf16[4,4,256,256]{3,2,1,0:T(8,128)(2,1)}), bf16[4,4,256,256]{3,2,1,0:T(8,128)(2,1)S(1)}, u32[]{:S(2)}, u32[]{:S(2)}) async-start(bf16[4,4,256,256]{3,2,1,0:T(8,128)(2,1)} %fusion.6), calls=%async_computation | async-start | bytes 4194304 | tf_op jit(solution)/shard_map/planes/all_to_all | solution.py:423
  51.6 0.6 fusion.17.place_ref
  52.2 1.6 reduce_sum.76.precoded_ref
  53.8 23.5 %all-to-all-done.square_ref = bf16[4,4,256,256]{3,2,1,0:T(8,128)(2,1)S(1)} async-done(((bf16[4,4,256,256]{3,2,1,0:T(8,128)(2,1)}), bf16[4,4,256,256]{3,2,1,0:T(8,128)(2,1)S(1)}, u32[]{:S(2)}, u32[]{:S(2)}) %all-to-all-start) | async-done | bytes 2097184 | tf_op jit(solution)/shard_map/planes/all_to_all | solution.py:423
  77.3 8.7 %all-gather.5.cloned.1.call-done = bf16[1792,2048]{1,0:T(8,128)(2,1)} async-done(((bf16[112,2048]{1,0:T(8,128)(2,1)}), bf16[1792,2048]{1,0:T(8,128)(2,1)}) %all-gather.5.cloned.1.call-update) | async-done | bytes 7340048 | tf_op jit(solution)/shard_map/newcomers/all_gather | solution.py:440
  86.0 9.7 %columns.1 = bf16[4,304,384]{2,1,0:T(8,128)(2,1)} custom-call(s32[1]{0:T(128)} %bitcast.3.row_ref, bf16[16,112,2048]{2,1,0:T(8,128)(2,1)} %bitcast.71, bf16[3,256,2048]{2,1,0:T(8,128)(2,1)} %channel_ref.3, s32[3,1,384]{2,1,0:T(1,128)} %fusion.17.place_ref), custom_call_target="tpu_custom_call" | custom-call | flops 4000000000 | bytes 12000000 | tf_op jit(solution)/shard_map/columns/columns/pallas_call | solution.py:115
  95.7 4.4 %all-to-all-start.2 = ((bf16[4,304,384]{2,1,0:T(8,128)(2,1)}), bf16[4,304,384]{2,1,0:T(8,128)(2,1)}, u32[]{:S(2)}, u32[]{:S(2)}) async-start(bf16[4,304,384]{2,1,0:T(8,128)(2,1)} %columns.1), calls=%async_computation.2 | async-start | bytes 1867776 | tf_op jit(solution)/shard_map/columns/all_to_all | solution.py:481
  100.2 14.0 %all-to-all-done.2 = bf16[4,304,384]{2,1,0:T(8,128)(2,1)} async-done(((bf16[4,304,384]{2,1,0:T(8,128)(2,1)}), bf16[4,304,384]{2,1,0:T(8,128)(2,1)}, u32[]{:S(2)}, u32[]{:S(2)}) %all-to-all-start.2) | async-done | bytes 933920 | tf_op jit(solution)/shard_map/columns/all_to_all | solution.py:481
  114.2 1.4 convert_reduce_fusion.1.summed_ref
  115.6 1.6 collective-permute-start.4
  117.2 0.7 dynamic-slice_bitcast_fusion.1.place_ref
  117.8 2.7 collective-permute-start.5
  120.5 1.4 collective-permute-start.6
  121.9 1.2 collective-permute-start.7
  123.2 1.1 collective-permute-start.8
  124.3 3.8 %collective-permute-start.9 = (bf16[256,384]{1,0:T(8,128)(2,1)S(1)}, bf16[256,384]{1,0:T(8,128)(2,1)S(1)}, u32[]{:S(2)}, u32[]{:S(2)}) collective-permute-start(bf16[256,384]{1,0:T(8,128)(2,1)S(1)} %slice.69.own_ref), channel_id=1, source_target_pairs={{0,16},{4,20},{8,24},{12,28},{16,32},{20,36},{24,40},{28,44},{32,4... | collective-permute-start | bytes 589832 | tf_op jit(solution)/shard_map/columns/ppermute | solution.py:416
  128.1 1.0 target.1.base_ref
  129.1 2.3 collective-permute-done.8.col2_ref
  131.5 2.1 collective-permute-done.9.col3_ref
  133.5 3.5 %middle.1 = (f32[256,384]{1,0:T(8,128)S(1)}, bf16[256,384]{1,0:T(8,128)(2,1)}, bf16[256,384]{1,0:T(8,128)(2,1)}, bf16[256,384]{1,0:T(8,128)(2,1)S(1)}, bf16[384,640]{1,0:T(8,128)(2,1)}) custom-call(s32[3]{0:T(128)S(1)} %pad_add_fusion.where_ref, bf16[4,4,256,256]{3,2,1,0:T(8,128)(2,1)S(1)} %all-to-all-done.square_ref, bf16[256,384]{1,0:T(8,128)(2,1)S(1)} %slice.69.own_ref, ...), custom_call_target="tpu_custom_call" | custom-call | flops 2000000000 | bytes 8000000 | tf_op jit(solution)/shard_map/schur/middle/pallas_call | solution.py:220
  137.1 2.0 collective-permute-start.11
  139.1 1.1 collective-permute-start.12
  140.3 5.4 %all-to-all-start.3 = ((bf16[16,24,640]{2,1,0:T(8,128)(2,1)}), bf16[16,24,640]{2,1,0:T(8,128)(2,1)S(1)}, u32[]{:S(2)}, u32[]{:S(2)}) async-start(bf16[16,24,640]{2,1,0:T(8,128)(2,1)} %bitcast.13), calls=%async_computation.3 | async-start | bytes 983040 | tf_op jit(solution)/shard_map/schur/all_to_all | solution.py:496
  145.8 4.0 %collective-permute-done.12 = bf16[256,384]{1,0:T(8,128)(2,1)S(1)} collective-permute-done((bf16[256,384]{1,0:T(8,128)(2,1)S(1)}, bf16[256,384]{1,0:T(8,128)(2,1)S(1)}, u32[]{:S(2)}, u32[]{:S(2)}) %collective-permute-start.12) | collective-permute-done | bytes 196640 | tf_op jit(solution)/shard_map/schur/ppermute | solution.py:412
  149.9 0.8 fusion.19
  150.7 5.0 %all-to-all-done.3 = bf16[16,24,640]{2,1,0:T(8,128)(2,1)S(1)} async-done(((bf16[16,24,640]{2,1,0:T(8,128)(2,1)}), bf16[16,24,640]{2,1,0:T(8,128)(2,1)S(1)}, u32[]{:S(2)}, u32[]{:S(2)}) %all-to-all-start.3) | async-done | bytes 491552 | tf_op jit(solution)/shard_map/schur/all_to_all | solution.py:496
  155.9 1.0 broadcast_in_dim.12
  156.9 3.6 %all-to-all-start.4 = ((f32[16,24,640]{2,1,0:T(8,128)}), f32[16,24,640]{2,1,0:T(8,128)S(1)}, u32[]{:S(2)}, u32[]{:S(2)}) async-start(f32[16,24,640]{2,1,0:T(8,128)} %broadcast_in_dim.12), calls=%async_computation.4 | async-start | bytes 1966080 | tf_op jit(solution)/shard_map/schur/all_to_all | solution.py:505
  160.6 0.6 reshape.281.slots_ref
  161.2 8.2 %channel.1.channel_ref = bf16[3,256,2048]{2,1,0:T(8,128)(2,1)} custom-call(s32[1]{0:T(128)} %bitcast.1.first_ref, bf16[16,112,2048]{2,1,0:T(8,128)(2,1)} %bitcast.72, bf16[3,256,2048]{2,1,0:T(8,128)(2,1)} %channel_ref.3, s32[3,1,384]{2,1,0:T(1,128)} %fusion.17.place_ref, s32[3,1,384]{2,1,0:T(1,128)} %reshape.281.slots_ref), custom_call_target="tpu_custom_call" | custom-call | flops 4000000000 | bytes 14000000 | tf_op jit(solution)/shard_map/users/channel/pallas_call | solution.py:143
  169.4 7.2 %all-to-all-done.4 = f32[16,24,640]{2,1,0:T(8,128)S(1)} async-done(((f32[16,24,640]{2,1,0:T(8,128)}), f32[16,24,640]{2,1,0:T(8,128)S(1)}, u32[]{:S(2)}, u32[]{:S(2)}) %all-to-all-start.4) | async-done | bytes 983072 | tf_op jit(solution)/shard_map/schur/all_to_all | solution.py:505
  176.5 12.2 %solve.1 = (f32[3,128,128]{2,1,0:T(8,128)S(1)}, bf16[4,256,256]{2,1,0:T(8,128)(2,1)S(1)}) custom-call(s32[1]{0:T(128)} %bitcast.1.first_ref, f32[384,640]{1,0:T(8,128)S(1)} %bitcast.60, f32[256,384]{1,0:T(8,128)S(1)} %get-tuple-element.53.weighted_ref, f32[256,256]{1,0:T(8,128)S(1)} %reduce_sum.76.precoded_ref, s32[1,384]{1,0:T(1,128)S(1)} %bitcast.64), custom_call_target="tpu_custom_call" | custom-call | flops 14000000000 | bytes 4000000 | tf_op jit(solution)/shard_map/users/solve/pallas_call | solution.py:297
  188.7 10.5 %all_to_all.40.users_ref = bf16[4,256,256]{2,1,0:T(8,128)(2,1)S(1)} all-to-all(bf16[4,256,256]{2,1,0:T(8,128)(2,1)S(1)} %get-tuple-element.40), channel_id=1, replica_groups=mesh['grp'=2,'row'=16,'col'=4] {'col'}, dimensions={0} | all-to-all | bytes 1048576 | tf_op jit(solution)/shard_map/users/all_to_all | solution.py:511
  199.2 2.1 signal.1
  201.3 4.5 %all-to-all-start.6 = ((bf16[16,3,16,2048]{3,2,1,0:T(8,128)(2,1)}), bf16[16,3,16,2048]{3,2,1,0:T(8,128)(2,1)}, u32[]{:S(2)}, u32[]{:S(2)}) async-start(bf16[16,3,16,2048]{3,2,1,0:T(8,128)(2,1)} %signal.1), calls=%async_computation.6 | async-start | bytes 6291456 | tf_op jit(solution)/shard_map/signal/all_to_all | solution.py:521
  206.5 1.9 copy-done.7
  208.4 5.6 %update.1 = (bf16[256,1024]{1,0:T(8,128)(2,1)S(1)}, bf16[256,1024]{1,0:T(8,128)(2,1)}, bf16[256,1024]{1,0:T(8,128)(2,1)}, bf16[256,1024]{1,0:T(8,128)(2,1)}) custom-call(s32[2]{0:T(128)S(1)} %pad_add_fusion.1.where_ref, f32[256,384]{1,0:T(8,128)S(1)} %get-tuple-element.53.weighted_ref, f32[384,640]{1,0:T(8,128)S(1)} %bitcast.61, ...), custom_call_target="tpu_custom_call" | custom-call | flops 1500000000 | bytes 8000000 | tf_op jit(solution)/shard_map/update/update/pallas_call | solution.py:384
  214.0 0.6 collective-permute-start.13
  214.6 2.1 collective-permute-start.14
  216.7 0.8 collective-permute-start.15
  217.5 2.1 and_select_fusion
  219.6 24.5 %all-to-all-done.6 = bf16[16,3,16,2048]{3,2,1,0:T(8,128)(2,1)} async-done(((bf16[16,3,16,2048]{3,2,1,0:T(8,128)(2,1)}), bf16[16,3,16,2048]{3,2,1,0:T(8,128)(2,1)}, u32[]{:S(2)}, u32[]{:S(2)}) %all-to-all-start.6) | async-done | bytes 3145760 | tf_op jit(solution)/shard_map/signal/all_to_all | solution.py:521
  244.1 2.5 convert_reduce_fusion
  246.7 0.6 broadcast_in_dim.13
  247.4 5.4 %all-to-all-start.7 = ((f32[64,1,3]{2,1,0:T(1,128)}), f32[64,1,3]{2,1,0:T(1,128)}, u32[]{:S(2)}, u32[]{:S(2)}) async-start(f32[64,1,3]{2,1,0:T(1,128)} %broadcast_in_dim.13), calls=%async_computation.7 | async-start | bytes 65536 | tf_op jit(solution)/shard_map/signal/all_to_all | solution.py:526
  252.8 3.0 %fusion.15 = (f32[1,256,1024]{2,1,0:T(8,128)S(1)}, f32[1,256,1024]{2,1,0:T(8,128)S(1)}, f32[1,256,1024]{2,1,0:T(8,128)S(1)}) fusion(f32[3,256,1024]{2,1,0:T(8,128)} %and_select_fusion, f32[3,256,1024]{2,1,0:T(8,128)S(1)} %copy-done.4, bf16[256,1024]{1,0:T(8,128)(2,1)} %collective-permute-done.15, bf16[256,1024]{1,0:T(8,128)(2,1)} %collective-permute-done.14, ...), kind=kLoop, calls=%fused_computation.24 | loop fusion | flops 4718592 | bytes 11534345 | tf_op jit(solution)/shard_map/final/stack | solution.py:543
  255.8 1.9 pad_maximum_fusion
  257.7 4.4 %all-to-all-done.7 = f32[64,1,3]{2,1,0:T(1,128)} async-done(((f32[64,1,3]{2,1,0:T(1,128)}), f32[64,1,3]{2,1,0:T(1,128)}, u32[]{:S(2)}, u32[]{:S(2)}) %all-to-all-start.7) | async-done | bytes 800 | tf_op jit(solution)/shard_map/signal/all_to_all | solution.py:526
  262.2 0.8 reduce_sum.85
  263.0 0.8 multiply_bitcast_fusion
  (72 shorter events, 2.6 us)
Async XLA Ops:
  7.2 12.4 %copy-start = (bf16[3,1024,256]{2,1,0:T(8,128)(2,1)S(1)}, bf16[3,1024,256]{2,1,0:T(8,128)(2,1)}, u32[]{:S(2)}) copy-start(bf16[3,1024,256]{2,1,0:T(8,128)(2,1)} %param.13) | copy-start | bytes 4718596
  7.2 78.8 %all-gather.5.cloned.1.call-start = ((), (), s32[]{:S(2)}) async-start(), calls=%async_computation.8 | async-start | bytes 7798784 | tf_op jit(solution)/shard_map/newcomers/all_gather | solution.py:440
  8.3 1.7 collective-permute-start
  12.2 1.9 copy-start.2
  14.1 5.4 %copy-start.3 = (f32[3,256,1024]{2,1,0:T(8,128)S(1)}, f32[3,256,1024]{2,1,0:T(8,128)}, u32[]{:S(2)}) copy-start(f32[3,256,1024]{2,1,0:T(8,128)} %inverse_ref.1) | copy-start | bytes 9437188
  14.3 14.3 %collective-permute-start.2 = (bf16[3,256,256]{2,1,0:T(8,128)(2,1)S(1)}, bf16[3,256,256]{2,1,0:T(8,128)(2,1)S(1)}, u32[]{:S(2)}, u32[]{:S(2)}) collective-permute-start(bf16[3,256,256]{2,1,0:T(8,128)(2,1)S(1)} %get-tuple-element.29), channel_id=1, source_target_pairs={{0,8},{4,12},{8,0},{12,4},{16,24},{20,28},{24,16},{28,20},{32,40},... | collective-permute-start | bytes 1179656 | tf_op jit(solution)/shard_map/planes/ppermute | solution.py:412
  17.5 25.7 %collective-permute-start.3 = (bf16[3,256,256]{2,1,0:T(8,128)(2,1)S(1)}, bf16[3,256,256]{2,1,0:T(8,128)(2,1)}, u32[]{:S(2)}, u32[]{:S(2)}) collective-permute-start(bf16[3,256,256]{2,1,0:T(8,128)(2,1)S(1)} %get-tuple-element.30), channel_id=1, source_target_pairs={{0,12},{4,0},{8,4},{12,8},{16,28},{20,16},{24,20},{28,24},{32,44},... | collective-permute-start | bytes 1179656 | tf_op jit(solution)/shard_map/planes/ppermute | solution.py:412
  18.6 24.5 %collective-permute-start.1 = (bf16[3,256,256]{2,1,0:T(8,128)(2,1)S(1)}, bf16[3,256,256]{2,1,0:T(8,128)(2,1)}, u32[]{:S(2)}, u32[]{:S(2)}) collective-permute-start(bf16[3,256,256]{2,1,0:T(8,128)(2,1)S(1)} %get-tuple-element.28), channel_id=1, source_target_pairs={{0,4},{4,8},{8,12},{12,0},{16,20},{20,24},{24,28},{28,16},{32,36},... | collective-permute-start | bytes 1179656 | tf_op jit(solution)/shard_map/planes/ppermute | solution.py:412
  22.3 23.3 %all-to-all-start.1 = ((f32[4,256,256]{2,1,0:T(8,128)}), f32[4,256,256]{2,1,0:T(8,128)}, u32[]{:S(2)}, u32[]{:S(2)}) async-start(f32[4,256,256]{2,1,0:T(8,128)} %concatenate.10), calls=%async_computation.1 | async-start | bytes 2097152 | tf_op jit(solution)/shard_map/planes/all_to_all | solution.py:423
  43.2 7.8 %copy-start.9 = (s32[6,3,128,1]{2,3,1,0:T(1,128)S(1)}, s32[6,3,128,1]{2,3,1,0:T(1,128)}, u32[]{:S(2)}) copy-start(s32[6,3,128,1]{2,3,1,0:T(1,128)} %param.10) | copy-start | bytes 27652
  43.2 8.1 %copy-start.10 = (s32[32]{0:T(128)S(1)}, s32[32]{0:T(128)}, u32[]{:S(2)}) copy-start(s32[32]{0:T(128)} %param.11) | copy-start | bytes 388
  45.6 31.7 %all-to-all-start = ((bf16[4,4,256,256]{3,2,1,0:T(8,128)(2,1)}), bf16[4,4,256,256]{3,2,1,0:T(8,128)(2,1)S(1)}, u32[]{:S(2)}, u32[]{:S(2)}) async-start(bf16[4,4,256,256]{3,2,1,0:T(8,128)(2,1)} %fusion.6), calls=%async_computation | async-start | bytes 4194304 | tf_op jit(solution)/shard_map/planes/all_to_all | solution.py:423
  95.7 21.4 %copy-start.8 = (s32[6,3,128]{2,1,0:T(4,128)S(1)}, s32[6,3,128]{2,1,0:T(4,128)}, u32[]{:S(2)}) copy-start(s32[6,3,128]{2,1,0:T(4,128)} %param.12) | copy-start | bytes 27652
  95.7 18.5 %all-to-all-start.2 = ((bf16[4,304,384]{2,1,0:T(8,128)(2,1)}), bf16[4,304,384]{2,1,0:T(8,128)(2,1)}, u32[]{:S(2)}, u32[]{:S(2)}) async-start(bf16[4,304,384]{2,1,0:T(8,128)(2,1)} %columns.1), calls=%async_computation.2 | async-start | bytes 1867776 | tf_op jit(solution)/shard_map/columns/all_to_all | solution.py:481
  115.6 8.7 %collective-permute-start.4 = (bf16[256,384]{1,0:T(8,128)(2,1)S(1)}, bf16[256,384]{1,0:T(8,128)(2,1)S(1)}, u32[]{:S(2)}, u32[]{:S(2)}) collective-permute-start(bf16[256,384]{1,0:T(8,128)(2,1)S(1)} %slice.69.own_ref), channel_id=1, source_target_pairs={{0,4},{4,8},{8,12},{12,0},{16,20},{20,24},{24,28},{28,16},{32,36},... | collective-permute-start | bytes 589832 | tf_op jit(solution)/shard_map/columns/ppermute | solution.py:412
  117.8 11.3 %collective-permute-start.5 = (bf16[256,384]{1,0:T(8,128)(2,1)S(1)}, bf16[256,384]{1,0:T(8,128)(2,1)S(1)}, u32[]{:S(2)}, u32[]{:S(2)}) collective-permute-start(bf16[256,384]{1,0:T(8,128)(2,1)S(1)} %slice.69.own_ref), channel_id=1, source_target_pairs={{0,8},{4,12},{8,0},{12,4},{16,24},{20,28},{24,16},{28,20},{32,40},... | collective-permute-start | bytes 589832 | tf_op jit(solution)/shard_map/columns/ppermute | solution.py:412
  120.5 8.6 %collective-permute-start.6 = (bf16[256,384]{1,0:T(8,128)(2,1)S(1)}, bf16[256,384]{1,0:T(8,128)(2,1)S(1)}, u32[]{:S(2)}, u32[]{:S(2)}) collective-permute-start(bf16[256,384]{1,0:T(8,128)(2,1)S(1)} %slice.69.own_ref), channel_id=1, source_target_pairs={{0,12},{4,0},{8,4},{12,8},{16,28},{20,16},{24,20},{28,24},{32,44},... | collective-permute-start | bytes 589832 | tf_op jit(solution)/shard_map/columns/ppermute | solution.py:412
  121.9 7.2 %collective-permute-start.7 = (bf16[256,384]{1,0:T(8,128)(2,1)S(1)}, bf16[256,384]{1,0:T(8,128)(2,1)S(1)}, u32[]{:S(2)}, u32[]{:S(2)}) collective-permute-start(bf16[256,384]{1,0:T(8,128)(2,1)S(1)} %slice.69.own_ref), channel_id=1, source_target_pairs={{0,48},{4,52},{8,56},{12,60},{16,0},{20,4},{24,8},{28,12},{32,16},... | collective-permute-start | bytes 589832 | tf_op jit(solution)/shard_map/columns/ppermute | solution.py:416
  123.2 8.3 %collective-permute-start.8 = (bf16[256,384]{1,0:T(8,128)(2,1)S(1)}, bf16[256,384]{1,0:T(8,128)(2,1)S(1)}, u32[]{:S(2)}, u32[]{:S(2)}) collective-permute-start(bf16[256,384]{1,0:T(8,128)(2,1)S(1)} %slice.69.own_ref), channel_id=1, source_target_pairs={{0,32},{4,36},{8,40},{12,44},{16,48},{20,52},{24,56},{28,60},{32,0... | collective-permute-start | bytes 589832 | tf_op jit(solution)/shard_map/columns/ppermute | solution.py:416
  124.3 9.2 %collective-permute-start.9 = (bf16[256,384]{1,0:T(8,128)(2,1)S(1)}, bf16[256,384]{1,0:T(8,128)(2,1)S(1)}, u32[]{:S(2)}, u32[]{:S(2)}) collective-permute-start(bf16[256,384]{1,0:T(8,128)(2,1)S(1)} %slice.69.own_ref), channel_id=1, source_target_pairs={{0,16},{4,20},{8,24},{12,28},{16,32},{20,36},{24,40},{28,44},{32,4... | collective-permute-start | bytes 589832 | tf_op jit(solution)/shard_map/columns/ppermute | solution.py:416
  137.0 8.8 %collective-permute-start.10 = (bf16[256,384]{1,0:T(8,128)(2,1)}, bf16[256,384]{1,0:T(8,128)(2,1)S(1)}, u32[]{:S(2)}, u32[]{:S(2)}) collective-permute-start(bf16[256,384]{1,0:T(8,128)(2,1)} %get-tuple-element.37), channel_id=1, source_target_pairs={{0,12},{4,0},{8,4},{12,8},{16,28},{20,16},{24,20},{28,24},{32,44},... | collective-permute-start | bytes 589832 | tf_op jit(solution)/shard_map/schur/ppermute | solution.py:412
  137.1 8.7 %collective-permute-start.11 = (bf16[256,384]{1,0:T(8,128)(2,1)}, bf16[256,384]{1,0:T(8,128)(2,1)S(1)}, u32[]{:S(2)}, u32[]{:S(2)}) collective-permute-start(bf16[256,384]{1,0:T(8,128)(2,1)} %get-tuple-element.38), channel_id=1, source_target_pairs={{0,8},{4,12},{8,0},{12,4},{16,24},{20,28},{24,16},{28,20},{32,40},... | collective-permute-start | bytes 589832 | tf_op jit(solution)/shard_map/schur/ppermute | solution.py:412
  139.1 10.7 %collective-permute-start.12 = (bf16[256,384]{1,0:T(8,128)(2,1)S(1)}, bf16[256,384]{1,0:T(8,128)(2,1)S(1)}, u32[]{:S(2)}, u32[]{:S(2)}) collective-permute-start(bf16[256,384]{1,0:T(8,128)(2,1)S(1)} %get-tuple-element.39), channel_id=1, source_target_pairs={{0,4},{4,8},{8,12},{12,0},{16,20},{20,24},{24,28},{28,16},{32,36},... | collective-permute-start | bytes 589832 | tf_op jit(solution)/shard_map/schur/ppermute | solution.py:412
  140.3 15.4 %all-to-all-start.3 = ((bf16[16,24,640]{2,1,0:T(8,128)(2,1)}), bf16[16,24,640]{2,1,0:T(8,128)(2,1)S(1)}, u32[]{:S(2)}, u32[]{:S(2)}) async-start(bf16[16,24,640]{2,1,0:T(8,128)(2,1)} %bitcast.13), calls=%async_computation.3 | async-start | bytes 983040 | tf_op jit(solution)/shard_map/schur/all_to_all | solution.py:496
  145.7 60.7 %all-gather.7.cloned.1.call-start = ((), (), s32[]{:S(2)}) async-start(), calls=%async_computation.9 | async-start | bytes 3342336 | tf_op jit(solution)/shard_map/schur/all_gather | solution.py:494
  156.9 19.6 %all-to-all-start.4 = ((f32[16,24,640]{2,1,0:T(8,128)}), f32[16,24,640]{2,1,0:T(8,128)S(1)}, u32[]{:S(2)}, u32[]{:S(2)}) async-start(f32[16,24,640]{2,1,0:T(8,128)} %broadcast_in_dim.12), calls=%async_computation.4 | async-start | bytes 1966080 | tf_op jit(solution)/shard_map/schur/all_to_all | solution.py:505
  176.5 22.6 %copy-start.5 = (bf16[3,256,2048]{2,1,0:T(8,128)(2,1)S(1)}, bf16[3,256,2048]{2,1,0:T(8,128)(2,1)}, u32[]{:S(2)}) copy-start(bf16[3,256,2048]{2,1,0:T(8,128)(2,1)} %channel.1.channel_ref) | copy-start | bytes 9437188
  201.3 42.7 %all-to-all-start.6 = ((bf16[16,3,16,2048]{3,2,1,0:T(8,128)(2,1)}), bf16[16,3,16,2048]{3,2,1,0:T(8,128)(2,1)}, u32[]{:S(2)}, u32[]{:S(2)}) async-start(bf16[16,3,16,2048]{3,2,1,0:T(8,128)(2,1)} %signal.1), calls=%async_computation.6 | async-start | bytes 6291456 | tf_op jit(solution)/shard_map/signal/all_to_all | solution.py:521
  206.5 1.9 copy-start.7
  214.0 2.7 %copy-start.6 = (bf16[256,1024]{1,0:T(8,128)(2,1)}, bf16[256,1024]{1,0:T(8,128)(2,1)S(1)}, u32[]{:S(2)}) copy-start(bf16[256,1024]{1,0:T(8,128)(2,1)S(1)} %get-tuple-element.50) | copy-start | bytes 1572868
  214.0 32.7 %collective-permute-start.13 = (bf16[256,1024]{1,0:T(8,128)(2,1)}, bf16[256,1024]{1,0:T(8,128)(2,1)}, u32[]{:S(2)}, u32[]{:S(2)}) collective-permute-start(bf16[256,1024]{1,0:T(8,128)(2,1)} %get-tuple-element.44), channel_id=1, source_target_pairs={{0,1},{1,2},{2,3},{3,0},{4,5},{5,6},{6,7},{7,4},{8,9},{9,10},{10,1... | collective-permute-start | bytes 1572872 | tf_op jit(solution)/shard_map/update/ppermute | solution.py:419
  214.6 32.1 %collective-permute-start.14 = (bf16[256,1024]{1,0:T(8,128)(2,1)}, bf16[256,1024]{1,0:T(8,128)(2,1)}, u32[]{:S(2)}, u32[]{:S(2)}) collective-permute-start(bf16[256,1024]{1,0:T(8,128)(2,1)} %get-tuple-element.45), channel_id=1, source_target_pairs={{0,2},{1,3},{2,0},{3,1},{4,6},{5,7},{6,4},{7,5},{8,10},{9,11},{10,... | collective-permute-start | bytes 1572872 | tf_op jit(solution)/shard_map/update/ppermute | solution.py:419
  216.7 36.1 %copy-start.4 = (f32[3,256,1024]{2,1,0:T(8,128)S(1)}, f32[3,256,1024]{2,1,0:T(8,128)}, u32[]{:S(2)}) copy-start(f32[3,256,1024]{2,1,0:T(8,128)} %inverse_ref.1) | copy-start | bytes 9437188
  216.7 30.0 %collective-permute-start.15 = (bf16[256,1024]{1,0:T(8,128)(2,1)}, bf16[256,1024]{1,0:T(8,128)(2,1)}, u32[]{:S(2)}, u32[]{:S(2)}) collective-permute-start(bf16[256,1024]{1,0:T(8,128)(2,1)} %get-tuple-element.46), channel_id=1, source_target_pairs={{0,3},{1,0},{2,1},{3,2},{4,7},{5,4},{6,5},{7,6},{8,11},{9,8},{10,9... | collective-permute-start | bytes 1572872 | tf_op jit(solution)/shard_map/update/ppermute | solution.py:419
  247.4 14.8 %all-to-all-start.7 = ((f32[64,1,3]{2,1,0:T(1,128)}), f32[64,1,3]{2,1,0:T(1,128)}, u32[]{:S(2)}, u32[]{:S(2)}) async-start(f32[64,1,3]{2,1,0:T(1,128)} %broadcast_in_dim.13), calls=%async_computation.7 | async-start | bytes 65536 | tf_op jit(solution)/shard_map/signal/all_to_all | solution.py:526
  255.8 8.0 %copy-start.1 = (bf16[3,1024,256]{2,1,0:T(8,128)(2,1)S(1)}, bf16[3,1024,256]{2,1,0:T(8,128)(2,1)}, u32[]{:S(2)}) copy-start(bf16[3,1024,256]{2,1,0:T(8,128)(2,1)} %param.13) | copy-start | bytes 4718596
Sparse Core Ops, SparseCore 0:
  12.3 73.6 all-gather.4
  150.8 50.4 all-gather.6
